TPU v7x, 512 devices: a whole 4x8x8 slice. The times are simulated.
512 devices in a mesh: seq: 32 (over z, x), section: 8 (over y_lo, core), dp: 2 (over y_hi).
Axes of the slice: x: 4, y: 8 (y_hi: 2, y_lo: 4; y = y_hi * 4 + y_lo), z: 8, core: 2. Of those that a mesh axis runs over, the one named last changes fastest.
Arguments:
- queries: bfloat16 [8, 4096, 3584], P('section', 'seq', 'dp'), may hold values from -5 to 5
- key_vectors: bfloat16 [8, 4096, 3584], P('section', 'seq', 'dp'), may hold values from -5 to 5
- value_vectors: bfloat16 [8, 4096, 3584], P('section', 'seq', 'dp'), may hold values from -6 to 6
- out_grad: bfloat16 [8, 4096, 3584], P('section', 'seq', 'dp'), may hold values from -6 to 6
- doc_lengths: int32 [8], replicated, may hold values from 1 to 1536, 4096 in all
Outputs:
- query_grad: bfloat16 [8, 4096, 3584], P('section', 'seq', 'dp')
- key_grad: bfloat16 [8, 4096, 3584], P('section', 'seq', 'dp')
- value_grad: bfloat16 [8, 4096, 3584], P('section', 'seq', 'dp')
Inputs may be any that keep to these rules, and one draw needn't show every extreme that they name: `doc_lengths`: the 8 lengths sum to 4096; the longest is exactly 1536.
All inputs are finite; a program needn't handle non-finite values.
Results may differ from a plain program's by a relative error of at most 0.024.
Values may be sent and summed in bfloat16 or wider, within the bound.
A program may use at most 192 MiB of HBM per device.

v0:
```python
import jax
import jax.numpy as jnp
from jax import lax
from jax.sharding import PartitionSpec as P

HEAD = 224


def pick_slot(stacked, slot):
    return lax.dynamic_index_in_dim(stacked, slot, 0, keepdims=False)


def put_slot(stacked, update, slot):
    return lax.dynamic_update_index_in_dim(stacked, update, slot, 0)


def shards(queries, key_vectors, value_vectors, out_grad, doc_lengths):
    local_rows = queries.shape[1]
    local_width = queries.shape[2]
    head_count = local_width // HEAD
    seq_size = lax.axis_size("seq")
    group = seq_size // head_count
    scaling = HEAD ** (-0.5)

    def spread(matrix):
        shaped = matrix.reshape(local_rows, head_count, 1, HEAD)
        copies = jnp.broadcast_to(shaped, (local_rows, head_count, group, HEAD))
        return copies.reshape(local_rows, seq_size * HEAD)

    query_head, key_head, value_head, cot_head = (
        lax.all_to_all(spread(queries), "seq", split_axis=1, concat_axis=0, tiled=True),
        lax.all_to_all(spread(key_vectors), "seq", split_axis=1, concat_axis=0, tiled=True),
        lax.all_to_all(spread(value_vectors), "seq", split_axis=1, concat_axis=0, tiled=True),
        lax.all_to_all(spread(out_grad), "seq", split_axis=1, concat_axis=0, tiled=True),
    )
    length = key_head.shape[0]
    member = lax.axis_index("seq") % group
    blocks = 2 * group
    block = length // blocks
    bounds = jnp.cumsum(doc_lengths)
    positions = jnp.arange(length, dtype=jnp.int32)
    doc_index = jnp.sum((positions[:, None] >= bounds[None, :]).astype(jnp.int32), axis=1)
    row_list = [member, blocks - 1 - member]
    query_list = []
    cot_list = []
    pos_list = []
    for which in range(2):
        offset = row_list[which] * block
        query_list.append(lax.dynamic_slice_in_dim(query_head, offset, block, 0))
        cot_list.append(lax.dynamic_slice_in_dim(cot_head, offset, block, 0))
        pos_list.append(offset + jnp.arange(block, dtype=jnp.int32))
    query_stack = jnp.stack(query_list)
    cot_stack = jnp.stack(cot_list)
    pos_stack = jnp.stack(pos_list)
    doc_stack = jnp.take(doc_index, pos_stack)
    plan = []
    for number in range(blocks + 1):
        first = number <= member
        slot = jnp.where(first, 0, 1).astype(jnp.int32)
        col_block = jnp.where(first, number, number - member - 1)
        flag = None
        plan.append((slot, col_block, flag))
    row_max = jnp.full((2, block), -jnp.inf, jnp.float32)
    row_sum = jnp.zeros((2, block), jnp.float32)
    stored = []
    for slot, col_block, flag in plan:

        def score_tile(carry, slot=slot, col_block=col_block):
            maxima, totals = carry
            query_rows = pick_slot(query_stack, slot)
            key_rows = lax.dynamic_slice_in_dim(key_head, col_block * block, block, 0)
            col_docs = lax.dynamic_slice_in_dim(doc_index, col_block * block, block, 0)
            col_positions = col_block * block + jnp.arange(block, dtype=jnp.int32)
            raw = jnp.dot(query_rows, key_rows.T, preferred_element_type=jnp.float32) * scaling
            allowed = (pick_slot(doc_stack, slot)[:, None] == col_docs[None, :]) & (
                pick_slot(pos_stack, slot)[:, None] >= col_positions[None, :]
            )
            scores = jnp.where(allowed, raw, -jnp.inf)
            before = pick_slot(maxima, slot)
            after = jnp.maximum(before, jnp.max(scores, axis=1))
            safe = jnp.where(jnp.isfinite(after), after, 0.0)
            total = pick_slot(totals, slot) * jnp.exp(before - safe) + jnp.sum(
                jnp.exp(scores - safe[:, None]), axis=1
            )
            return (scores, put_slot(maxima, after, slot), put_slot(totals, total, slot))

        scores, row_max, row_sum = score_tile((row_max, row_sum))
        stored.append(scores)

    def tile_weights(scores, slot):
        return (
            jnp.exp(scores - pick_slot(row_max, slot)[:, None]) / pick_slot(row_sum, slot)[:, None]
        )

    summed = jnp.zeros((2, block, HEAD), jnp.float32)
    for (slot, col_block, flag), scores in zip(plan, stored):

        def add_values(carry, slot=slot, col_block=col_block, scores=scores):
            rounded = tile_weights(scores, slot).astype(jnp.bfloat16)
            value_rows = lax.dynamic_slice_in_dim(value_head, col_block * block, block, 0)
            term = jnp.dot(rounded, value_rows, preferred_element_type=jnp.float32)
            return put_slot(carry, pick_slot(carry, slot) + term, slot)

        summed = add_values(summed)
    attended = summed.astype(jnp.bfloat16)
    row_dot = jnp.sum(cot_stack.astype(jnp.float32) * attended.astype(jnp.float32), axis=2)
    query_acc = jnp.zeros((2, block, HEAD), jnp.float32)
    key_acc = jnp.zeros((length, HEAD), jnp.float32)
    value_acc = jnp.zeros((length, HEAD), jnp.float32)
    for (slot, col_block, flag), scores in zip(plan, stored):

        def backward_tile(carry, slot=slot, col_block=col_block, scores=scores):
            query_sum, key_sum, value_sum = carry
            weights = tile_weights(scores, slot)
            rounded = weights.astype(jnp.bfloat16)
            query_rows = pick_slot(query_stack, slot)
            cot_rows = pick_slot(cot_stack, slot)
            start = col_block * block
            key_rows = lax.dynamic_slice_in_dim(key_head, start, block, 0)
            value_rows = lax.dynamic_slice_in_dim(value_head, start, block, 0)
            value_term = jnp.dot(rounded.T, cot_rows, preferred_element_type=jnp.float32)
            prob_grad = jnp.dot(cot_rows, value_rows.T, preferred_element_type=jnp.float32)
            score_grad = (
                weights * (prob_grad - pick_slot(row_dot, slot)[:, None]) * scaling
            ).astype(jnp.bfloat16)
            query_term = jnp.dot(score_grad, key_rows, preferred_element_type=jnp.float32)
            key_term = jnp.dot(score_grad.T, query_rows, preferred_element_type=jnp.float32)
            query_sum = put_slot(query_sum, pick_slot(query_sum, slot) + query_term, slot)
            key_sum = lax.dynamic_update_slice_in_dim(
                key_sum, lax.dynamic_slice_in_dim(key_sum, start, block, 0) + key_term, start, 0
            )
            value_sum = lax.dynamic_update_slice_in_dim(
                value_sum,
                lax.dynamic_slice_in_dim(value_sum, start, block, 0) + value_term,
                start,
                0,
            )
            return (query_sum, key_sum, value_sum)

        query_acc, key_acc, value_acc = backward_tile((query_acc, key_acc, value_acc))
    query_rounded = query_acc.astype(jnp.bfloat16)
    key_back, value_back = (
        lax.all_to_all(key_acc, "seq", split_axis=0, concat_axis=1, tiled=True),
        lax.all_to_all(value_acc, "seq", split_axis=0, concat_axis=1, tiled=True),
    )

    def settle(received):
        shaped = received.astype(jnp.float32).reshape(local_rows, head_count, group, HEAD)
        return jnp.sum(shaped, axis=2).reshape(1, local_rows, local_width).astype(jnp.bfloat16)

    query_full = jnp.zeros((length, HEAD), jnp.bfloat16)
    for which in range(2):
        query_full = lax.dynamic_update_slice_in_dim(
            query_full, query_rounded[which], row_list[which] * block, 0
        )
    query_back = lax.all_to_all(query_full, "seq", split_axis=0, concat_axis=1, tiled=True)
    query_out = settle(query_back)
    return (query_out, settle(key_back), settle(value_back))


def solution(mesh):
    return jax.shard_map(
        shards,
        mesh=mesh,
        in_specs=(
            P("section", "seq", "dp"),
            P("section", "seq", "dp"),
            P("section", "seq", "dp"),
            P("section", "seq", "dp"),
            P(),
        ),
        out_specs=(P("section", "seq", "dp"), P("section", "seq", "dp"), P("section", "seq", "dp")),
        check_vma=False,
    )
```

profile of v0, /device:TPU:56, one launch (start us, length us, event | category | flops | bytes accessed | tf_op | source)
XLA Modules:
  0.0 459.5 jit_solution(12948339711171515117)
XLA Ops:
  0.6 1.3 copy.94
  1.9 1.6 broadcast_in_dim.238
  3.5 13.3 %all-to-all-start = ((bf16[128,32,224]{0,2,1:T(8,128)(2,1)}), bf16[128,32,224]{0,2,1:T(8,128)(2,1)S(1)}, u32[]{:S(2)}, u32[]{:S(2)}) async-start(bf16[128,32,224]{0,2,1:T(8,128)(2,1)} %bitcast.368), calls=%async_computation | async-start | bytes 3670016 | tf_op jit(solution)/shard_map/all_to_all | solution.py:31
  17.4 44.0 %all-to-all-done = bf16[128,32,224]{0,2,1:T(8,128)(2,1)S(1)} async-done(((bf16[128,32,224]{0,2,1:T(8,128)(2,1)}), bf16[128,32,224]{0,2,1:T(8,128)(2,1)S(1)}, u32[]{:S(2)}, u32[]{:S(2)}) %all-to-all-start) | async-done | bytes 1835040 | tf_op jit(solution)/shard_map/all_to_all | solution.py:31
  61.4 1.5 broadcast_in_dim.240
  62.9 6.0 %all-to-all-start.1 = ((bf16[128,32,224]{0,2,1:T(8,128)(2,1)}), bf16[128,32,224]{0,2,1:T(8,128)(2,1)}, u32[]{:S(2)}, u32[]{:S(2)}) async-start(bf16[128,32,224]{0,2,1:T(8,128)(2,1)} %bitcast.369), calls=%async_computation.1 | async-start | bytes 3670016 | tf_op jit(solution)/shard_map/all_to_all | solution.py:32
  69.0 6.2 %gather_fusion = s32[1024]{0:T(1024)S(1)} fusion(s32[4096]{0:T(1024)S(1)} %convert_reduce_fusion, s32[1024]{0:T(1024)S(1)} %broadcast_clamp_fusion), kind=kCustom, calls=%fused_computation | custom fusion | bytes 12288 | tf_op jit(solution)/shard_map/jit(_take)/gather | solution.py:55
  75.5 1.3 copy.100
  77.5 34.7 %all-to-all-done.1 = bf16[128,32,224]{0,2,1:T(8,128)(2,1)} async-done(((bf16[128,32,224]{0,2,1:T(8,128)(2,1)}), bf16[128,32,224]{0,2,1:T(8,128)(2,1)}, u32[]{:S(2)}, u32[]{:S(2)}) %all-to-all-start.1) | async-done | bytes 1835040 | tf_op jit(solution)/shard_map/all_to_all | solution.py:32
  112.2 1.6 broadcast_in_dim.247
  113.8 6.0 %all-to-all-start.2 = ((bf16[128,32,224]{0,2,1:T(8,128)(2,1)}), bf16[128,32,224]{0,2,1:T(8,128)(2,1)}, u32[]{:S(2)}, u32[]{:S(2)}) async-start(bf16[128,32,224]{0,2,1:T(8,128)(2,1)} %bitcast.69), calls=%async_computation.2 | async-start | bytes 3670016 | tf_op jit(solution)/shard_map/all_to_all | solution.py:34
  119.8 1.7 copy_bitcast_fusion.5
  121.5 1.4 fusion.299
  123.0 1.4 exponential_reduce_fusion.8
  124.9 1.0 copy-done.16
  126.2 0.5 fusion.301
  126.7 1.0 copy-done.19
  128.1 0.5 fusion.302
  128.5 1.0 copy-done.22
  130.3 1.0 copy-done.25
  132.1 1.0 copy-done.28
  133.4 1.5 fusion.305
  134.8 27.4 %all-to-all-done.2 = bf16[128,32,224]{0,2,1:T(8,128)(2,1)} async-done(((bf16[128,32,224]{0,2,1:T(8,128)(2,1)}), bf16[128,32,224]{0,2,1:T(8,128)(2,1)}, u32[]{:S(2)}, u32[]{:S(2)}) %all-to-all-start.2) | async-done | bytes 1835040 | tf_op jit(solution)/shard_map/all_to_all | solution.py:34
  162.2 1.5 broadcast_in_dim.249
  163.7 6.1 %all-to-all-start.3 = ((bf16[128,32,224]{0,2,1:T(8,128)(2,1)}), bf16[128,32,224]{0,2,1:T(8,128)(2,1)}, u32[]{:S(2)}, u32[]{:S(2)}) async-start(bf16[128,32,224]{0,2,1:T(8,128)(2,1)} %bitcast.370), calls=%async_computation.3 | async-start | bytes 3670016 | tf_op jit(solution)/shard_map/all_to_all | solution.py:33
  170.7 1.0 copy-done.34
  172.5 1.0 copy-done.37
  174.1 1.7 copy_bitcast_fusion.3
  175.8 0.8 dynamic-slice_bitcast_fusion.1
  176.6 35.2 %all-to-all-done.3 = bf16[128,32,224]{0,2,1:T(8,128)(2,1)} async-done(((bf16[128,32,224]{0,2,1:T(8,128)(2,1)}), bf16[128,32,224]{0,2,1:T(8,128)(2,1)}, u32[]{:S(2)}, u32[]{:S(2)}) %all-to-all-start.3) | async-done | bytes 1835040 | tf_op jit(solution)/shard_map/all_to_all | solution.py:33
  211.8 1.7 copy_bitcast_fusion.2
  214.1 0.8 copy-done.17
  215.3 0.8 copy-done.20
  216.5 0.8 copy-done.23
  217.7 0.8 copy-done.26
  219.0 0.8 copy-done.29
  220.2 0.8 copy-done.32
  221.4 0.8 copy-done.35
  222.6 0.8 copy-done.38
  223.8 0.6 copy-done.40
  232.4 1.5 copy_bitcast_fusion.6
  233.9 6.1 %all-to-all-start.4 = ((bf16[32,128,224]{1,2,0:T(8,128)(2,1)}), bf16[32,128,224]{1,2,0:T(8,128)(2,1)S(1)}, u32[]{:S(2)}, u32[]{:S(2)}) async-start(bf16[32,128,224]{1,2,0:T(8,128)(2,1)} %copy_bitcast_fusion.6), calls=%async_computation.4 | async-start | bytes 3670016 | tf_op jit(solution)/shard_map/all_to_all | solution.py:156
  240.4 0.8 copy-done.15
  241.7 0.8 copy-done.18
  242.9 0.8 copy-done.21
  244.2 0.8 copy-done.24
  245.4 0.8 copy-done.27
  246.6 0.8 copy-done.30
  247.8 0.8 copy-done.33
  249.1 0.8 copy-done.36
  250.3 0.8 copy-done.39
  251.5 2.3 copy_bitcast_fusion
  253.8 27.5 %all-to-all-done.4 = bf16[32,128,224]{1,2,0:T(8,128)(2,1)S(1)} async-done(((bf16[32,128,224]{1,2,0:T(8,128)(2,1)}), bf16[32,128,224]{1,2,0:T(8,128)(2,1)S(1)}, u32[]{:S(2)}, u32[]{:S(2)}) %all-to-all-start.4) | async-done | bytes 1835040 | tf_op jit(solution)/shard_map/all_to_all | solution.py:156
  281.4 5.4 %all-to-all-start.6 = ((f32[32,128,224]{1,2,0:T(8,128)}), f32[32,128,224]{1,2,0:T(8,128)}, u32[]{:S(2)}, u32[]{:S(2)}) async-start(f32[32,128,224]{1,2,0:T(8,128)} %copy_bitcast_fusion), calls=%async_computation.6 | async-start | bytes 7340032 | tf_op jit(solution)/shard_map/all_to_all | solution.py:144
  287.2 0.6 copy-done.13
  292.1 2.4 copy_bitcast_fusion.1
  294.5 73.2 %all-to-all-done.6 = f32[32,128,224]{1,2,0:T(8,128)} async-done(((f32[32,128,224]{1,2,0:T(8,128)}), f32[32,128,224]{1,2,0:T(8,128)}, u32[]{:S(2)}, u32[]{:S(2)}) %all-to-all-start.6) | async-done | bytes 3670048 | tf_op jit(solution)/shard_map/all_to_all | solution.py:144
  367.7 6.7 %all-to-all-start.5 = ((f32[32,128,224]{1,2,0:T(8,128)}), f32[32,128,224]{1,2,0:T(8,128)}, u32[]{:S(2)}, u32[]{:S(2)}) async-start(f32[32,128,224]{1,2,0:T(8,128)} %copy_bitcast_fusion.1), calls=%async_computation.5 | async-start | bytes 7340032 | tf_op jit(solution)/shard_map/all_to_all | solution.py:143
  374.7 1.0 copy.120
  375.6 2.4 bitcast_reduce_fusion
  378.3 1.0 copy.122
  379.3 76.5 %all-to-all-done.5 = f32[32,128,224]{1,2,0:T(8,128)} async-done(((f32[32,128,224]{1,2,0:T(8,128)}), f32[32,128,224]{1,2,0:T(8,128)}, u32[]{:S(2)}, u32[]{:S(2)}) %all-to-all-start.5) | async-done | bytes 3670048 | tf_op jit(solution)/shard_map/all_to_all | solution.py:143
  455.8 2.4 bitcast_reduce_fusion.1
  458.5 1.0 copy.121
  (232 shorter events, 27.4 us)
Async XLA Ops:
  3.5 13.4 %copy-start.46 = (s32[8]{0:T(128)S(1)}, s32[8]{0:T(128)}, u32[]{:S(2)}) copy-start(s32[8]{0:T(128)} %param.9) | copy-start | bytes 100
  3.5 13.6 %copy-start.44 = (bf16[1,128,1792]{2,1,0:T(8,128)(2,1)S(1)}, bf16[1,128,1792]{2,1,0:T(8,128)(2,1)}, u32[]{:S(2)}) copy-start(bf16[1,128,1792]{2,1,0:T(8,128)(2,1)} %param.6) | copy-start | bytes 1376260
  3.5 57.9 %all-to-all-start = ((bf16[128,32,224]{0,2,1:T(8,128)(2,1)}), bf16[128,32,224]{0,2,1:T(8,128)(2,1)S(1)}, u32[]{:S(2)}, u32[]{:S(2)}) async-start(bf16[128,32,224]{0,2,1:T(8,128)(2,1)} %bitcast.368), calls=%async_computation | async-start | bytes 3670016 | tf_op jit(solution)/shard_map/all_to_all | solution.py:31
  62.9 49.3 %all-to-all-start.1 = ((bf16[128,32,224]{0,2,1:T(8,128)(2,1)}), bf16[128,32,224]{0,2,1:T(8,128)(2,1)}, u32[]{:S(2)}, u32[]{:S(2)}) async-start(bf16[128,32,224]{0,2,1:T(8,128)(2,1)} %bitcast.369), calls=%async_computation.1 | async-start | bytes 3670016 | tf_op jit(solution)/shard_map/all_to_all | solution.py:32
  69.0 6.2 %copy-start.45 = (bf16[1,128,1792]{2,1,0:T(8,128)(2,1)S(1)}, bf16[1,128,1792]{2,1,0:T(8,128)(2,1)}, u32[]{:S(2)}) copy-start(bf16[1,128,1792]{2,1,0:T(8,128)(2,1)} %param.8) | copy-start | bytes 1376260
  113.8 48.4 %all-to-all-start.2 = ((bf16[128,32,224]{0,2,1:T(8,128)(2,1)}), bf16[128,32,224]{0,2,1:T(8,128)(2,1)}, u32[]{:S(2)}, u32[]{:S(2)}) async-start(bf16[128,32,224]{0,2,1:T(8,128)(2,1)} %bitcast.69), calls=%async_computation.2 | async-start | bytes 3670016 | tf_op jit(solution)/shard_map/all_to_all | solution.py:34
  124.9 1.0 copy-start.16
  126.7 1.0 copy-start.19
  128.5 1.0 copy-start.22
  130.3 1.0 copy-start.25
  132.1 1.0 copy-start.28
  163.7 6.2 %copy-start.31 = (f32[512,512]{0,1:T(8,128)S(1)}, f32[512,512]{0,1:T(8,128)}, u32[]{:S(2)}) copy-start(f32[512,512]{0,1:T(8,128)} %get-tuple-element.102) | copy-start | bytes 3145732
  163.7 48.1 %all-to-all-start.3 = ((bf16[128,32,224]{0,2,1:T(8,128)(2,1)}), bf16[128,32,224]{0,2,1:T(8,128)(2,1)}, u32[]{:S(2)}, u32[]{:S(2)}) async-start(bf16[128,32,224]{0,2,1:T(8,128)(2,1)} %bitcast.370), calls=%async_computation.3 | async-start | bytes 3670016 | tf_op jit(solution)/shard_map/all_to_all | solution.py:33
  170.7 1.0 copy-start.34
  172.5 1.1 copy-start.37
  176.6 37.0 %copy-start.14 = (f32[512,512]{0,1:T(8,128)S(1)}, f32[512,512]{0,1:T(8,128)}, u32[]{:S(2)}) copy-start(f32[512,512]{0,1:T(8,128)} %get-tuple-element.90) | copy-start | bytes 3145732
  213.6 1.2 copy-start.17
  214.8 1.2 copy-start.20
  216.1 1.2 copy-start.23
  217.3 1.2 copy-start.26
  218.5 1.2 copy-start.29
  219.7 1.2 copy-start.32
  221.0 1.2 copy-start.35
  222.2 1.2 copy-start.38
  223.4 0.9 copy-start.40
  223.4 1.0 copy-start.42
  225.1 3.8 copy-start.12
  225.6 3.7 copy-start.10
  226.0 3.6 copy-start.8
  226.5 3.5 copy-start.6
  227.0 3.4 copy-start.4
  227.4 3.3 copy-start.2
  227.9 3.1 copy-start
  233.9 47.5 %all-to-all-start.4 = ((bf16[32,128,224]{1,2,0:T(8,128)(2,1)}), bf16[32,128,224]{1,2,0:T(8,128)(2,1)S(1)}, u32[]{:S(2)}, u32[]{:S(2)}) async-start(bf16[32,128,224]{1,2,0:T(8,128)(2,1)} %copy_bitcast_fusion.6), calls=%async_computation.4 | async-start | bytes 3670016 | tf_op jit(solution)/shard_map/all_to_all | solution.py:156
  240.0 1.2 copy-start.15
  240.0 1.2 copy-start.41
  240.0 1.3 copy-start.43
  241.3 1.2 copy-start.18
  242.5 1.2 copy-start.21
  243.8 1.2 copy-start.24
  245.0 1.2 copy-start.27
  246.2 1.2 copy-start.30
  247.4 1.2 copy-start.33
  248.7 1.2 copy-start.36
  249.9 1.2 copy-start.39
  281.4 86.3 %all-to-all-start.6 = ((f32[32,128,224]{1,2,0:T(8,128)}), f32[32,128,224]{1,2,0:T(8,128)}, u32[]{:S(2)}, u32[]{:S(2)}) async-start(f32[32,128,224]{1,2,0:T(8,128)} %copy_bitcast_fusion), calls=%async_computation.6 | async-start | bytes 7340032 | tf_op jit(solution)/shard_map/all_to_all | solution.py:144
  286.8 1.0 copy-start.13
  286.8 1.4 copy-start.11
  287.8 1.1 copy-start.9
  288.2 1.1 copy-start.7
  288.9 1.1 copy-start.5
  289.3 1.1 copy-start.3
  290.0 1.1 copy-start.1
  367.7 88.1 %all-to-all-start.5 = ((f32[32,128,224]{1,2,0:T(8,128)}), f32[32,128,224]{1,2,0:T(8,128)}, u32[]{:S(2)}, u32[]{:S(2)}) async-start(f32[32,128,224]{1,2,0:T(8,128)} %copy_bitcast_fusion.1), calls=%async_computation.5 | async-start | bytes 7340032 | tf_op jit(solution)/shard_map/all_to_all | solution.py:143
where the time goes:
time: 461 us; the launch traced here: 459 us
  waiting for transfers between devices  319 us (69%)
  local copies, waits for them, and re-layouts  57.5 us (12%)
  starting transfers between devices  49.5 us (11%)
  matrix products  22.8 us (5%)
  other arithmetic  9.02 us (2%)
    all_to_all x1, waiting for transfers between devices, shards(): lax.all_to_all(key_acc, 'seq', split_axis=0, concat_axis=1, tiled=True)  76.5 us
    all_to_all x1, waiting for transfers between devices, shards(): lax.all_to_all(value_acc, 'seq', split_axis=0, concat_axis=1, tiled=True)  73.2 us
    all_to_all x1, waiting for transfers between devices, shards(): lax.all_to_all(spread(queries), 'seq', split_axis=1, concat_axis=0, tiled...  44 us
    all_to_all x1, waiting for transfers between devices, shards(): lax.all_to_all(spread(value_vectors), 'seq', split_axis=1, concat_axis=0,...  35.2 us
    all_to_all x1, waiting for transfers between devices, shards(): lax.all_to_all(spread(key_vectors), 'seq', split_axis=1, concat_axis=0, t...  34.7 us
    unnamed x103, local copies, waits for them, and re-layouts  29.6 us
    all_to_all x1, waiting for transfers between devices, shards(): lax.all_to_all(query_full, 'seq', split_axis=0, concat_axis=1, tiled=True)  27.5 us
    all_to_all x1, waiting for transfers between devices, shards(): lax.all_to_all(spread(out_grad), 'seq', split_axis=1, concat_axis=0, tile...  27.4 us
  transfers between devices with their start and end apart: 7, of which 7 were waited for; matrix products, arithmetic and copies ran while one was open for 9% of the time, Pallas kernels for 0%

commit v1 on v0

v1 whole, which is shorter than its diff:
```python
import functools

import jax
import jax.numpy as jnp
from jax import lax
from jax.experimental import pallas as pl
from jax.experimental.pallas import tpu as pltpu
from jax.sharding import PartitionSpec as P

HEAD = 224
ZN, XN = 8, 4
SCALE = HEAD ** (-0.5)
NEG = -1e30
LOW = -1e20
TQ = 256
TK = 256
ITEMS = ((0, 3), (1, 3), (2, 3), (0, 2), (1, 2), (2, 2), (3, 0), (3, 1), (3, 2), (2, 0), (2, 1))


class Docs:
    def __init__(self, lengths):
        self.bounds = []
        total = jnp.int32(0)
        for d in range(8):
            total = total + lengths[d]
            self.bounds.append(total)

    def start(self, t):
        r = jnp.int32(0)
        for b in self.bounds[:7]:
            r = jnp.where(b <= t, b, r)
        return r

    def end(self, t):
        r = jnp.int32(4096)
        for b in reversed(self.bounds):
            r = jnp.where(b > t, b, r)
        return r

    def row_start(self, pos):
        r = jnp.zeros_like(pos)
        for b in self.bounds[:7]:
            r = jnp.where(pos >= b, b, r)
        return r

    def case(self, t):
        before = t - self.start(t - 1)
        after = self.end(t - 1) - t
        keys = after > 1024
        return keys, (before > 1024) & jnp.logical_not(keys)


def slots(docs, z):
    lk, lq = docs.case(z * 512)
    rk, rq = docs.case(z * 512 + 512)
    lm = jnp.logical_not(lk | lq)
    rm = jnp.logical_not(rk | rq)
    q_ids = (z, z + 1, jnp.where(rq, z + 1, z + 2), z)
    k_ids = (z, z - 1, jnp.where(lk, z - 1, z - 2), z)
    valid = {
        (0, 3): True,
        (1, 3): jnp.logical_not(rk),
        (2, 3): rm,
        (0, 2): lk,
        (1, 2): lk & jnp.logical_not(rk),
        (2, 2): (lk & rm) | (rq & lm),
        (3, 0): True,
        (3, 1): jnp.logical_not(lq),
        (3, 2): lm,
        (2, 0): rq,
        (2, 1): rq & jnp.logical_not(lq),
    }
    return q_ids, k_ids, valid


NT = (((1,), (1,)), ((), ()))


def for_tiles(docs, z, body):
    q_ids, k_ids, valid = slots(docs, z)
    for qs, ks in ITEMS:
        qid, kid, ok = q_ids[qs], k_ids[ks], valid[(qs, ks)]
        use = (qid < ZN) & (kid >= 0) & ok
        for qt in range(512 // TQ):
            q0 = qid * 512 + qt * TQ
            first = docs.start(q0)
            for kt in range(512 // TK):
                k0 = kid * 512 + kt * TK
                k1 = k0 + TK - 1
                hit = use & (k0 <= q0 + TQ - 1) & ((k1 >= q0) | (k1 >= first))

                @pl.when(hit)
                def _():
                    body(qs, ks, qt, kt, q0, k0)


def masked_scores(docs, k, q, q0, k0):
    s = lax.dot_general(k, q, NT, preferred_element_type=jnp.float32) * SCALE
    kpos = k0 + lax.broadcasted_iota(jnp.int32, (TK, 1), 0)
    qpos = q0 + lax.broadcasted_iota(jnp.int32, (1, TQ), 1)
    qstart = docs.row_start(qpos)
    return jnp.where((kpos <= qpos) & (kpos >= qstart), s, NEG)


def stats_kernel(len_ref, q_ref, do_ref, k_ref, v_ref, st_ref):
    z = lax.axis_index("seq") // XN
    docs = Docs(len_ref)
    st_ref[0:4, :] = jnp.full((4, 512), LOW, jnp.float32)
    st_ref[4:16, :] = jnp.zeros((12, 512), jnp.float32)

    def body(qs, ks, qt, kt, q0, k0):
        rows, cols = pl.ds(qt * TQ, TQ), pl.ds(kt * TK, TK)
        q, do = q_ref[qs, rows, :], do_ref[qs, rows, :]
        k, v = k_ref[ks, cols, :], v_ref[ks, cols, :]
        s = masked_scores(docs, k, q, q0, k0)
        dp = lax.dot_general(v, do, NT, preferred_element_type=jnp.float32)
        old = st_ref[qs : qs + 1, rows]
        new = jnp.maximum(old, jnp.max(s, axis=0, keepdims=True))
        p = jnp.exp(s - new)
        alpha = jnp.exp(old - new)
        st_ref[qs : qs + 1, rows] = new
        st_ref[4 + qs : 5 + qs, rows] = st_ref[4 + qs : 5 + qs, rows] * alpha + jnp.sum(p, axis=0, keepdims=True)
        st_ref[8 + qs : 9 + qs, rows] = st_ref[8 + qs : 9 + qs, rows] * alpha + jnp.sum(p * dp, axis=0, keepdims=True)

    for_tiles(docs, z, body)


def combine_stats(docs, z, mine, up1, up2, down1, down2):
    lk, lq = docs.case(z * 512)
    rk, rq = docs.case(z * 512 + 512)
    lm = jnp.logical_not(lk | lq)
    rm = jnp.logical_not(rk | rq)
    bk, bq = docs.case(z * 512 - 512)
    bm = jnp.logical_not(bk | bq) & (z >= 2)

    def part(ref, slot, use=None):
        m, l, d = ref[slot : slot + 1, :], ref[4 + slot : 5 + slot, :], ref[8 + slot : 9 + slot, :]
        if use is not None:
            m = jnp.where(use, m, LOW)
            l = jnp.where(use, l, 0.0)
            d = jnp.where(use, d, 0.0)
        return m, l, d

    groups = (
        (part(mine, 0), part(down1, 1, z >= 1), part(down2, 2, bm)),
        (part(mine, 1), part(up1, 0, z + 1 < ZN), part(down1, 2, lm & (z >= 1))),
        (part(mine, 2), part(up2, 0, rm & (z + 2 < ZN)), part(up1, 1, rm & (z + 1 < ZN)), part(up1, 3, rq & (z + 1 < ZN))),
        (part(mine, 3), part(down1, 2, lq & (z >= 1))),
    )
    out = []
    for parts in groups:
        m = functools.reduce(jnp.maximum, [p[0] for p in parts])
        l = sum(p[1] * jnp.exp(p[0] - m) for p in parts)
        d = sum(p[2] * jnp.exp(p[0] - m) for p in parts)
        inv = jnp.where(l > 0.0, 1.0 / jnp.where(l > 0.0, l, 1.0), 0.0)
        out.append((m, inv, d * inv))
    return out


def grads_kernel(len_ref, q_ref, do_ref, k_ref, v_ref, mine, up1, up2, down1, down2,
                 dq_ref, dk_ref, dv_ref, stat, kt_ref, dqt, dk_acc, dv_acc):
    z = lax.axis_index("seq") // XN
    docs = Docs(len_ref)
    for qs, (m, inv, d) in enumerate(combine_stats(docs, z, mine, up1, up2, down1, down2)):
        stat[qs : qs + 1, :] = m
        stat[4 + qs : 5 + qs, :] = inv
        stat[8 + qs : 9 + qs, :] = d
    for i in range(4):
        kt_ref[i] = k_ref[i].T
    dqt[...] = jnp.zeros_like(dqt)
    dk_acc[...] = jnp.zeros_like(dk_acc)
    dv_acc[...] = jnp.zeros_like(dv_acc)

    def body(qs, ks, qt, kt, q0, k0):
        rows, cols = pl.ds(qt * TQ, TQ), pl.ds(kt * TK, TK)
        q, do = q_ref[qs, rows, :], do_ref[qs, rows, :]
        k, v = k_ref[ks, cols, :], v_ref[ks, cols, :]
        s = masked_scores(docs, k, q, q0, k0)
        dp = lax.dot_general(v, do, NT, preferred_element_type=jnp.float32)
        p = jnp.exp(s - stat[qs : qs + 1, rows]) * stat[4 + qs : 5 + qs, rows]
        ds = (p * (dp - stat[8 + qs : 9 + qs, rows])).astype(jnp.bfloat16)
        dv_acc[ks, cols, :] += jnp.dot(p.astype(jnp.bfloat16), do, preferred_element_type=jnp.float32)
        dk_acc[ks, cols, :] += jnp.dot(ds, q, preferred_element_type=jnp.float32)
        dqt[qs, :, rows] += jnp.dot(kt_ref[ks, :, cols], ds, preferred_element_type=jnp.float32)

    for_tiles(docs, z, body)
    for i in range(4):
        dq_ref[i] = (dqt[i] * SCALE).T.astype(jnp.bfloat16)
        dk_ref[i] = (dk_acc[i] * SCALE).astype(jnp.bfloat16)
        dv_ref[i] = dv_acc[i].astype(jnp.bfloat16)


VM = pl.BlockSpec(memory_space=pltpu.VMEM)
SM = pl.BlockSpec(memory_space=pltpu.SMEM)
BIG = pltpu.CompilerParams(vmem_limit_bytes=48 * 1024 * 1024)


def shards(queries, key_vectors, value_vectors, out_grad, doc_lengths):
    rows, width = queries.shape[1], queries.shape[2]
    idx = lax.axis_index("seq")
    z = idx // XN
    docs = Docs(doc_lengths)
    x_groups = [[XN * a + b for b in range(XN)] for a in range(ZN)]
    n = ZN * XN

    def move(value, dz):
        return lax.ppermute(value, "seq", [(i, (i + XN * dz) % n) for i in range(n)])

    stacked = jnp.concatenate([queries, out_grad, key_vectors, value_vectors], axis=0)
    shaped = stacked.reshape(4, rows, XN, 2, HEAD).transpose(2, 3, 0, 1, 4)
    got = lax.all_to_all(shaped, "seq", split_axis=0, concat_axis=0, axis_index_groups=x_groups, tiled=True)
    got = got.transpose(1, 2, 0, 3, 4).reshape(2, 4, XN * rows, HEAD)
    a_q, a_k = got[0, 0:2], got[0, 2:4]
    b_q, b_k = got[1, 0:2], got[1, 2:4]
    lk, lq = docs.case(z * 512)
    rk, rq = docs.case(z * 512 + 512)
    back1 = move(a_q, -1)
    fore1 = move(b_k, 1)
    back2 = move(jnp.where(lq, b_q, back1), -1)
    fore2 = move(jnp.where(rk, a_k, fore1), 1)
    qs = jnp.stack([a_q[0], back1[0], back2[0], b_q[0]])
    dos = jnp.stack([a_q[1], back1[1], back2[1], b_q[1]])
    ks = jnp.stack([b_k[0], fore1[0], fore2[0], a_k[0]])
    vs = jnp.stack([b_k[1], fore1[1], fore2[1], a_k[1]])
    mine = pl.pallas_call(
        stats_kernel,
        out_shape=jax.ShapeDtypeStruct((16, 512), jnp.float32),
        in_specs=[SM] + [VM] * 4,
        out_specs=VM,
        compiler_params=BIG,
    )(doc_lengths, qs, dos, ks, vs)
    up1, up2 = move(mine, -1), move(mine, -2)
    down1, down2 = move(mine, 1), move(mine, 2)
    block = jax.ShapeDtypeStruct((4, 512, HEAD), jnp.bfloat16)
    dq, dk, dv = pl.pallas_call(
        grads_kernel,
        out_shape=(block, block, block),
        in_specs=[SM] + [VM] * 9,
        out_specs=(VM, VM, VM),
        scratch_shapes=[
            pltpu.VMEM((16, 512), jnp.float32),
            pltpu.VMEM((4, HEAD, 512), jnp.bfloat16),
            pltpu.VMEM((4, HEAD, 512), jnp.float32),
            pltpu.VMEM((4, 512, HEAD), jnp.float32),
            pltpu.VMEM((4, 512, HEAD), jnp.float32),
        ],
        compiler_params=BIG,
    )(doc_lengths, qs, dos, ks, vs, mine, up1, up2, down1, down2)
    kv = jnp.stack([dk, dv])
    f32 = jnp.float32

    def plus(base, term, use):
        return (base.astype(f32) + jnp.where(use, term.astype(f32), 0.0)).astype(jnp.bfloat16)

    lm = jnp.logical_not(lk | lq)
    rm = jnp.logical_not(rk | rq)
    q2 = move(dq[2], 1)
    k2 = move(kv[:, 2], -1)
    q_first = plus(dq[1], q2, lm & (z >= 1))
    q_b = plus(dq[3], q2, lq & (z >= 1))
    k_first = plus(kv[:, 1], k2, rm & (z < ZN - 1))
    k_a = plus(kv[:, 3], k2, rk & (z < ZN - 1))
    q_a = plus(dq[0], move(q_first, 1), z >= 1)
    k_b = plus(kv[:, 0], move(k_first, -1), z < ZN - 1)
    out = jnp.stack([jnp.stack([q_a, k_a[0], k_a[1]]), jnp.stack([q_b, k_b[0], k_b[1]])])
    out = out.reshape(2, 3, XN, rows, HEAD).transpose(2, 0, 1, 3, 4)
    home = lax.all_to_all(out, "seq", split_axis=0, concat_axis=0, axis_index_groups=x_groups, tiled=True)
    home = home.transpose(2, 3, 0, 1, 4).reshape(3, 1, rows, width)
    return home[0], home[1], home[2]


def solution(mesh):
    spec = P("section", "seq", "dp")
    return jax.shard_map(
        shards,
        mesh=mesh,
        in_specs=(spec, spec, spec, spec, P()),
        out_specs=(spec, spec, spec),
        check_vma=False,
    )
```

time: 461 us -> 168 us (0.36)
  waiting for transfers between devices: 319 us -> 19.1 us
  local copies, waits for them, and re-layouts: 57.5 us -> 14.6 us
  blocking collectives: 0 us -> 42.8 us
  matrix products: 22.8 us -> 0 us
  starting transfers between devices: 49.5 us -> 61 us
  Pallas kernels: 0 us -> 9.57 us
  between operations: 2.13 us -> 11.3 us
    all_to_all x7 -> x0, waiting for transfers between devices: 319 us -> none  [the longest x1 76.5 us: shards(): lax.all_to_all(key_acc, 'seq', split_axis=0, concat_axis=1, tiled=True)]
    ppermute x0 -> x12, starting transfers between devices: none -> 61 us  [move(): lax.ppermute(value, 'seq', [(i, (i + XN * dz) % n) for i in range(n)])]
    all_to_all x7 -> x0, starting transfers between devices: 49.5 us -> none  [the longest x1 13.3 us: shards(): lax.all_to_all(spread(queries), 'seq', split_axis=1, concat_axis=0, tiled...]
    all_to_all x0 -> x2, blocking collectives: none -> 42.8 us  [the longest x1 27.7 us: shards(): lax.all_to_all(shaped, 'seq', split_axis=0, concat_axis=0, axis_index_gro...]
    unnamed x103 -> x21, local copies, waits for them, and re-layouts: 29.6 us -> 6.29 us
    dot_general x54 -> x0, matrix products: 22.8 us -> none  [the longest x9 6.18 us: score_tile(): jnp.dot(query_rows, key_rows.T, preferred_element_type=jnp.float32)]
    ppermute x0 -> x12, waiting for transfers between devices: none -> 19.1 us  [move(): lax.ppermute(value, 'seq', [(i, (i + XN * dz) % n) for i in range(n)])]
    all_to_all x7 -> x1, local copies, waits for them, and re-layouts: 11.5 us -> 0.09 us  [shards(): lax.all_to_all(out, 'seq', split_axis=0, concat_axis=0, axis_index_groups...]
  transfers between devices with their start and end apart: 7 -> 12, of which waited for: 7 -> 6; matrix products, arithmetic and copies ran while one was open for 9% -> 6% of each run, Pallas kernels for 0% -> 0%
where the time goes in v1:
time: 168 us; the launch traced here: 167 us
  starting transfers between devices  61 us (36%)
  blocking collectives  42.8 us (25%)
  waiting for transfers between devices  19.1 us (11%)
  local copies, waits for them, and re-layouts  14.6 us (9%)
  between operations  11.3 us (7%)
  Pallas kernels  9.57 us (6%)
  other arithmetic  8.84 us (5%)
    ppermute x12, starting transfers between devices, move(): lax.ppermute(value, 'seq', [(i, (i + XN * dz) % n) for i in range(n)])  61 us
    all_to_all x1, blocking collectives, shards(): lax.all_to_all(shaped, 'seq', split_axis=0, concat_axis=0, axis_index_gro...  27.7 us
    ppermute x12, waiting for transfers between devices, move(): lax.ppermute(value, 'seq', [(i, (i + XN * dz) % n) for i in range(n)])  19.1 us
    all_to_all x1, blocking collectives, shards(): lax.all_to_all(out, 'seq', split_axis=0, concat_axis=0, axis_index_groups...  15.1 us
    convert_element_type x4, other arithmetic, plus(): (base.astype(f32) + jnp.where(use, term.astype(f32), 0.0)).astype(jnp.bfl...  6.44 us
    unnamed x21, local copies, waits for them, and re-layouts  6.29 us
    pallas_call x1, Pallas kernels, shards(): pl.pallas_call(grads_kernel, out_shape=(block, block, block), in_specs=[S...  6.27 us
  transfers between devices with their start and end apart: 12, of which 6 were waited for; matrix products, arithmetic and copies ran while one was open for 6% of the time, Pallas kernels for 0%

profile of v1, /device:TPU:56, one launch (start us, length us, event | category | flops | bytes accessed | tf_op | source)
XLA Modules:
  0.0 167.2 jit_solution(18321521778829117800)
XLA Ops:
  0.6 0.0 copy-start.5
  0.6 0.0 copy-start.6
  0.7 1.4 copy.30
  2.0 1.3 copy.32
  3.3 0.0 copy-done.5
  3.3 0.3 copy.33
  3.6 0.3 copy.31
  3.8 0.2 pad_maximum_fusion
  4.1 0.1 copy.34
  4.2 27.7 %all_to_all.10 = bf16[4,2,4,128,224]{3,4,1,2,0:T(8,128)(2,1)} all-to-all(bf16[4,2,4,128,224]{3,4,1,2,0:T(8,128)(2,1)S(1)} %copy.34), channel_id=1, replica_groups={{0,16,32,48},{64,80,96,112},{128,144,160,176},{192,208,224,240},{256,27..., dimensions={0} | all-to-all | bytes 3670016 | tf_op jit(solution)/shard_map/all_to_all | solution.py:211
  31.9 2.7 %copy.35 = bf16[2,4,4,128,224]{4,3,2,1,0:T(8,128)(2,1)S(1)} copy(bf16[2,4,4,128,224]{3,4,0,1,2:T(8,128)(2,1)} %bitcast.99) | data formatting | bytes 3670016 | tf_op jit(solution)/shard_map/transpose | solution.py:212
  34.7 0.0 copy-start.2
  34.7 1.0 slice_bitcast_fusion.1
  35.7 4.3 %collective-permute-start.2 = (bf16[2,512,224]{2,1,0:T(8,128)(2,1)}, bf16[2,512,224]{2,1,0:T(8,128)(2,1)S(1)}, u32[]{:S(2)}, u32[]{:S(2)}) collective-permute-start(bf16[2,512,224]{2,1,0:T(8,128)(2,1)} %get-tuple-element.27), channel_id=1, source_target_pairs={{0,64},{16,80},{32,96},{48,112},{64,128},{80,144},{96,160},{112,17... | collective-permute-start | bytes 1376264 | tf_op jit(solution)/shard_map/ppermute | solution.py:207
  40.0 8.6 %collective-permute-start = (bf16[2,512,224]{2,1,0:T(8,128)(2,1)}, bf16[2,512,224]{2,1,0:T(8,128)(2,1)S(1)}, u32[]{:S(2)}, u32[]{:S(2)}) collective-permute-start(bf16[2,512,224]{2,1,0:T(8,128)(2,1)} %get-tuple-element.28), channel_id=1, source_target_pairs={{0,448},{16,464},{32,480},{48,496},{64,0},{80,16},{96,32},{112,48}... | collective-permute-start | bytes 1376264 | tf_op jit(solution)/shard_map/ppermute | solution.py:207
  48.6 0.7 fusion.24
  58.2 0.1 slice_bitcast_fusion.5
  58.4 0.0 collective-permute-done.2
  58.4 0.5 collective-permute-done
  58.9 0.1 fusion.16
  59.0 1.9 %collective-permute-start.3 = (bf16[2,512,224]{2,1,0:T(8,128)(2,1)S(1)}, bf16[2,512,224]{2,1,0:T(8,128)(2,1)S(1)}, u32[]{:S(2)}, u32[]{:S(2)}) collective-permute-start(bf16[2,512,224]{2,1,0:T(8,128)(2,1)S(1)} %get-tuple-element.25), channel_id=1, source_target_pairs={{0,64},{16,80},{32,96},{48,112},{64,128},{80,144},{96,160},{112,17... | collective-permute-start | bytes 1376264 | tf_op jit(solution)/shard_map/ppermute | solution.py:207
  60.9 5.5 %collective-permute-start.1 = (bf16[2,512,224]{2,1,0:T(8,128)(2,1)S(1)}, bf16[2,512,224]{2,1,0:T(8,128)(2,1)S(1)}, u32[]{:S(2)}, u32[]{:S(2)}) collective-permute-start(bf16[2,512,224]{2,1,0:T(8,128)(2,1)S(1)} %get-tuple-element.26), channel_id=1, source_target_pairs={{0,448},{16,464},{32,480},{48,496},{64,0},{80,16},{96,32},{112,48}... | collective-permute-start | bytes 1376264 | tf_op jit(solution)/shard_map/ppermute | solution.py:207
  66.5 7.8 %collective-permute-done.3 = bf16[2,512,224]{2,1,0:T(8,128)(2,1)S(1)} collective-permute-done((bf16[2,512,224]{2,1,0:T(8,128)(2,1)S(1)}, bf16[2,512,224]{2,1,0:T(8,128)(2,1)S(1)}, u32[]{:S(2)}, u32[]{:S(2)}) %collective-permute-start.3) | collective-permute-done | bytes 458784 | tf_op jit(solution)/shard_map/ppermute | solution.py:207
  74.3 0.5 pad_maximum_fusion.3
  74.8 0.0 copy-start
  74.9 0.6 collective-permute-done.1
  75.5 0.5 pad_maximum_fusion.1
  76.0 0.2 copy-done.1
  76.2 3.3 %shard_map.76.mine = f32[16,512]{1,0:T(8,128)S(1)} custom-call(s32[8]{0:T(128)S(1)} %copy-done.2, bf16[4,512,224]{2,1,0:T(8,128)(2,1)S(1)} %get-tuple-element.50.q_ref, bf16[4,512,224]{2,1,0:T(8,128)(2,1)S(1)} %get-tuple-element.51.do_ref, bf16[4,512,224]{2,1,0:T(8,128)(2,1)S(1)} %get-tuple-element.52.k_ref, bf16[4,512,224]{2,1,0:T(8,128)(2,1)S(1)} %get-tuple-element.53.v_ref), custom_call_target="tpu_custom_call" | custom-call | tf_op jit(solution)/shard_map/pallas_call | solution.py:225
  79.5 10.0 %collective-permute-start.7 = (f32[16,512]{1,0:T(8,128)S(1)}, f32[16,512]{1,0:T(8,128)S(1)}, u32[]{:S(2)}, u32[]{:S(2)}) collective-permute-start(f32[16,512]{1,0:T(8,128)S(1)} %shard_map.76.mine), channel_id=1, source_target_pairs={{0,128},{16,144},{32,160},{48,176},{64,192},{80,208},{96,224},{112... | collective-permute-start | bytes 98312 | tf_op jit(solution)/shard_map/ppermute | solution.py:207
  89.5 2.1 %collective-permute-start.6 = (f32[16,512]{1,0:T(8,128)S(1)}, f32[16,512]{1,0:T(8,128)S(1)}, u32[]{:S(2)}, u32[]{:S(2)}) collective-permute-start(f32[16,512]{1,0:T(8,128)S(1)} %shard_map.76.mine), channel_id=1, source_target_pairs={{0,64},{16,80},{32,96},{48,112},{64,128},{80,144},{96,160},{112,17... | collective-permute-start | bytes 98312 | tf_op jit(solution)/shard_map/ppermute | solution.py:207
  91.6 6.0 %collective-permute-start.5 = (f32[16,512]{1,0:T(8,128)S(1)}, f32[16,512]{1,0:T(8,128)S(1)}, u32[]{:S(2)}, u32[]{:S(2)}) collective-permute-start(f32[16,512]{1,0:T(8,128)S(1)} %shard_map.76.mine), channel_id=1, source_target_pairs={{0,384},{16,400},{32,416},{48,432},{64,448},{80,464},{96,480},{112... | collective-permute-start | bytes 98312 | tf_op jit(solution)/shard_map/ppermute | solution.py:207
  97.6 1.9 %collective-permute-start.4 = (f32[16,512]{1,0:T(8,128)S(1)}, f32[16,512]{1,0:T(8,128)S(1)}, u32[]{:S(2)}, u32[]{:S(2)}) collective-permute-start(f32[16,512]{1,0:T(8,128)S(1)} %shard_map.76.mine), channel_id=1, source_target_pairs={{0,448},{16,464},{32,480},{48,496},{64,0},{80,16},{96,32},{112,48}... | collective-permute-start | bytes 98312 | tf_op jit(solution)/shard_map/ppermute | solution.py:207
  99.6 0.0 collective-permute-done.7.down2
  99.6 0.0 collective-permute-done.6.down1
  99.6 0.0 collective-permute-done.5.up2
  99.6 3.8 %collective-permute-done.4.up1 = f32[16,512]{1,0:T(8,128)S(1)} collective-permute-done((f32[16,512]{1,0:T(8,128)S(1)}, f32[16,512]{1,0:T(8,128)S(1)}, u32[]{:S(2)}, u32[]{:S(2)}) %collective-permute-start.4) | collective-permute-done | bytes 32800 | tf_op jit(solution)/shard_map/ppermute | solution.py:207
  103.4 6.3 %shard_map.77 = (bf16[4,512,224]{2,1,0:T(8,128)(2,1)S(1)}, bf16[4,512,224]{2,1,0:T(8,128)(2,1)S(1)}, bf16[4,512,224]{2,1,0:T(8,128)(2,1)S(1)}) custom-call(s32[8]{0:T(128)S(1)} %copy-done.2, bf16[4,512,224]{2,1,0:T(8,128)(2,1)S(1)} %get-tuple-element.50.q_ref, bf16[4,512,224]{2,1,0:T(8,128)(2,1)S(1)} %get-tuple-element.51.do_ref, ...), custom_call_target="tpu_custom_call" | custom-call | tf_op jit(solution)/shard_map/pallas_call | solution.py:235
  109.8 11.5 %collective-permute-start.8 = (bf16[512,224]{1,0:T(8,128)(2,1)S(1)}, bf16[512,224]{1,0:T(8,128)(2,1)}, u32[]{:S(2)}, u32[]{:S(2)}) collective-permute-start(bf16[512,224]{1,0:T(8,128)(2,1)S(1)} %slice_bitcast_fusion.12), channel_id=1, source_target_pairs={{0,64},{16,80},{32,96},{48,112},{64,128},{80,144},{96,160},{112,17... | collective-permute-start | bytes 688136 | tf_op jit(solution)/shard_map/ppermute | solution.py:207
  121.3 0.9 fusion.14
  122.2 1.9 %collective-permute-start.10 = (bf16[2,512,224]{2,1,0:T(8,128)(2,1)}, bf16[2,512,224]{2,1,0:T(8,128)(2,1)}, u32[]{:S(2)}, u32[]{:S(2)}) collective-permute-start(bf16[2,512,224]{2,1,0:T(8,128)(2,1)} %fusion.14), channel_id=1, source_target_pairs={{0,448},{16,464},{32,480},{48,496},{64,0},{80,16},{96,32},{112,48}... | collective-permute-start | bytes 1376264 | tf_op jit(solution)/shard_map/ppermute | solution.py:207
  125.5 0.0 collective-permute-done.8
  125.5 1.8 %fusion.6 = (bf16[512,224]{1,0:T(8,128)(2,1)}, bf16[512,224]{1,0:T(8,128)(2,1)S(1)}) fusion(bf16[512,224]{1,0:T(8,128)(2,1)} %collective-permute-done.8, bf16[4,512,224]{2,1,0:T(8,128)(2,1)S(1)} %get-tuple-element.6, pred[]{:T(512)S(6)} %and.26, pred[]{:T(512)S(6)} %and.28), kind=kLoop, calls=%fused_computation.24 | loop fusion | flops 1032192 | bytes 1146882 | tf_op jit(solution)/shard_map/convert_element_type | solution.py:253
  127.3 4.2 %collective-permute-start.9 = (bf16[512,224]{1,0:T(8,128)(2,1)}, bf16[512,224]{1,0:T(8,128)(2,1)}, u32[]{:S(2)}, u32[]{:S(2)}) collective-permute-start(bf16[512,224]{1,0:T(8,128)(2,1)} %get-tuple-element.32), channel_id=1, source_target_pairs={{0,64},{16,80},{32,96},{48,112},{64,128},{80,144},{96,160},{112,17... | collective-permute-start | bytes 688136 | tf_op jit(solution)/shard_map/ppermute | solution.py:207
  131.5 2.1 %collective-permute-done.10 = bf16[2,512,224]{2,1,0:T(8,128)(2,1)} collective-permute-done((bf16[2,512,224]{2,1,0:T(8,128)(2,1)}, bf16[2,512,224]{2,1,0:T(8,128)(2,1)}, u32[]{:S(2)}, u32[]{:S(2)}) %collective-permute-start.10) | collective-permute-done | bytes 458784 | tf_op jit(solution)/shard_map/ppermute | solution.py:207
  133.6 2.4 %fusion.1 = (bf16[2,512,224]{2,1,0:T(8,128)(2,1)}, bf16[2,512,224]{2,1,0:T(8,128)(2,1)}) fusion(bf16[2,512,224]{2,1,0:T(8,128)(2,1)} %collective-permute-done.10, bf16[1,4,512,224]{3,2,1,0:T(8,128)(2,1)S(1)} %bitcast.90, bf16[1,4,512,224]{3,2,1,0:T(8,128)(2,1)S(1)} %bitcast.93, pred[]{:T(512)S(6)} %and.27, pred[]{:T(512)S(6)} %and.30), kind=kLoop, calls=%fused_computation.12 | loop fusion | flops 2523136 | bytes 3211266 | tf_op jit(solution)/shard_map/convert_element_type | solution.py:253
  136.0 3.1 %collective-permute-start.11 = (bf16[2,512,224]{2,1,0:T(8,128)(2,1)}, bf16[2,512,224]{2,1,0:T(8,128)(2,1)}, u32[]{:S(2)}, u32[]{:S(2)}) collective-permute-start(bf16[2,512,224]{2,1,0:T(8,128)(2,1)} %get-tuple-element.16), channel_id=1, source_target_pairs={{0,448},{16,464},{32,480},{48,496},{64,0},{80,16},{96,32},{112,48}... | collective-permute-start | bytes 1376264 | tf_op jit(solution)/shard_map/ppermute | solution.py:207
  139.1 0.8 copy.41
  139.9 0.0 collective-permute-done.9
  139.9 1.0 fusion.18
  141.0 0.8 copy.38
  141.8 1.3 copy.39
  143.1 0.0 copy-start.3
  143.1 0.0 copy-start.4
  143.1 4.2 %collective-permute-done.11 = bf16[2,512,224]{2,1,0:T(8,128)(2,1)} collective-permute-done((bf16[2,512,224]{2,1,0:T(8,128)(2,1)}, bf16[2,512,224]{2,1,0:T(8,128)(2,1)}, u32[]{:S(2)}, u32[]{:S(2)}) %collective-permute-start.11) | collective-permute-done | bytes 458784 | tf_op jit(solution)/shard_map/ppermute | solution.py:207
  147.4 1.2 fusion.4
  148.6 0.3 copy.42
  148.9 0.1 maximum_bitcast_fusion
  149.0 15.1 %all_to_all.11 = bf16[4,2,3,128,224]{3,4,1,2,0:T(8,128)(2,1)S(1)} all-to-all(bf16[4,2,3,128,224]{3,4,1,2,0:T(8,128)(2,1)S(1)} %maximum_bitcast_fusion), channel_id=1, replica_groups={{0,16,32,48},{64,80,96,112},{128,144,160,176},{192,208,224,240},{256,27..., dimensions={0} | all-to-all | bytes 2752512 | tf_op jit(solution)/shard_map/all_to_all | solution.py:267
  164.1 0.1 copy.51
  164.2 0.1 fusion.19
  164.3 1.0 copy.46
  165.3 1.0 copy.45
  166.2 1.0 copy.44
  (11 shorter events, 0.2 us)
Async XLA Ops:
  0.6 2.7 %copy-start.5 = (bf16[1,128,1792]{2,1,0:T(8,128)(2,1)S(1)}, bf16[1,128,1792]{2,1,0:T(8,128)(2,1)}, u32[]{:S(2)}) copy-start(bf16[1,128,1792]{2,1,0:T(8,128)(2,1)} %param.7) | copy-start | bytes 1376260
  0.6 2.9 %copy-start.6 = (bf16[1,128,1792]{2,1,0:T(8,128)(2,1)S(1)}, bf16[1,128,1792]{2,1,0:T(8,128)(2,1)}, u32[]{:S(2)}) copy-start(bf16[1,128,1792]{2,1,0:T(8,128)(2,1)} %param.8) | copy-start | bytes 1376260
  34.7 14.0 %copy-start.2 = (s32[8]{0:T(128)S(1)}, s32[8]{0:T(128)}, u32[]{:S(2)}) copy-start(s32[8]{0:T(128)} %len_ref.3) | copy-start | bytes 100
  35.7 22.7 %collective-permute-start.2 = (bf16[2,512,224]{2,1,0:T(8,128)(2,1)}, bf16[2,512,224]{2,1,0:T(8,128)(2,1)S(1)}, u32[]{:S(2)}, u32[]{:S(2)}) collective-permute-start(bf16[2,512,224]{2,1,0:T(8,128)(2,1)} %get-tuple-element.27), channel_id=1, source_target_pairs={{0,64},{16,80},{32,96},{48,112},{64,128},{80,144},{96,160},{112,17... | collective-permute-start | bytes 1376264 | tf_op jit(solution)/shard_map/ppermute | solution.py:207
  40.0 18.9 %collective-permute-start = (bf16[2,512,224]{2,1,0:T(8,128)(2,1)}, bf16[2,512,224]{2,1,0:T(8,128)(2,1)S(1)}, u32[]{:S(2)}, u32[]{:S(2)}) collective-permute-start(bf16[2,512,224]{2,1,0:T(8,128)(2,1)} %get-tuple-element.28), channel_id=1, source_target_pairs={{0,448},{16,464},{32,480},{48,496},{64,0},{80,16},{96,32},{112,48}... | collective-permute-start | bytes 1376264 | tf_op jit(solution)/shard_map/ppermute | solution.py:207
  59.0 15.3 %collective-permute-start.3 = (bf16[2,512,224]{2,1,0:T(8,128)(2,1)S(1)}, bf16[2,512,224]{2,1,0:T(8,128)(2,1)S(1)}, u32[]{:S(2)}, u32[]{:S(2)}) collective-permute-start(bf16[2,512,224]{2,1,0:T(8,128)(2,1)S(1)} %get-tuple-element.25), channel_id=1, source_target_pairs={{0,64},{16,80},{32,96},{48,112},{64,128},{80,144},{96,160},{112,17... | collective-permute-start | bytes 1376264 | tf_op jit(solution)/shard_map/ppermute | solution.py:207
  60.9 14.6 %collective-permute-start.1 = (bf16[2,512,224]{2,1,0:T(8,128)(2,1)S(1)}, bf16[2,512,224]{2,1,0:T(8,128)(2,1)S(1)}, u32[]{:S(2)}, u32[]{:S(2)}) collective-permute-start(bf16[2,512,224]{2,1,0:T(8,128)(2,1)S(1)} %get-tuple-element.26), channel_id=1, source_target_pairs={{0,448},{16,464},{32,480},{48,496},{64,0},{80,16},{96,32},{112,48}... | collective-permute-start | bytes 1376264 | tf_op jit(solution)/shard_map/ppermute | solution.py:207
  74.8 1.2 copy-start
  74.8 1.4 copy-start.1
  79.5 20.1 %collective-permute-start.7 = (f32[16,512]{1,0:T(8,128)S(1)}, f32[16,512]{1,0:T(8,128)S(1)}, u32[]{:S(2)}, u32[]{:S(2)}) collective-permute-start(f32[16,512]{1,0:T(8,128)S(1)} %shard_map.76.mine), channel_id=1, source_target_pairs={{0,128},{16,144},{32,160},{48,176},{64,192},{80,208},{96,224},{112... | collective-permute-start | bytes 98312 | tf_op jit(solution)/shard_map/ppermute | solution.py:207
  89.5 10.1 %collective-permute-start.6 = (f32[16,512]{1,0:T(8,128)S(1)}, f32[16,512]{1,0:T(8,128)S(1)}, u32[]{:S(2)}, u32[]{:S(2)}) collective-permute-start(f32[16,512]{1,0:T(8,128)S(1)} %shard_map.76.mine), channel_id=1, source_target_pairs={{0,64},{16,80},{32,96},{48,112},{64,128},{80,144},{96,160},{112,17... | collective-permute-start | bytes 98312 | tf_op jit(solution)/shard_map/ppermute | solution.py:207
  91.6 8.0 %collective-permute-start.5 = (f32[16,512]{1,0:T(8,128)S(1)}, f32[16,512]{1,0:T(8,128)S(1)}, u32[]{:S(2)}, u32[]{:S(2)}) collective-permute-start(f32[16,512]{1,0:T(8,128)S(1)} %shard_map.76.mine), channel_id=1, source_target_pairs={{0,384},{16,400},{32,416},{48,432},{64,448},{80,464},{96,480},{112... | collective-permute-start | bytes 98312 | tf_op jit(solution)/shard_map/ppermute | solution.py:207
  97.6 5.8 %collective-permute-start.4 = (f32[16,512]{1,0:T(8,128)S(1)}, f32[16,512]{1,0:T(8,128)S(1)}, u32[]{:S(2)}, u32[]{:S(2)}) collective-permute-start(f32[16,512]{1,0:T(8,128)S(1)} %shard_map.76.mine), channel_id=1, source_target_pairs={{0,448},{16,464},{32,480},{48,496},{64,0},{80,16},{96,32},{112,48}... | collective-permute-start | bytes 98312 | tf_op jit(solution)/shard_map/ppermute | solution.py:207
  109.8 15.7 %collective-permute-start.8 = (bf16[512,224]{1,0:T(8,128)(2,1)S(1)}, bf16[512,224]{1,0:T(8,128)(2,1)}, u32[]{:S(2)}, u32[]{:S(2)}) collective-permute-start(bf16[512,224]{1,0:T(8,128)(2,1)S(1)} %slice_bitcast_fusion.12), channel_id=1, source_target_pairs={{0,64},{16,80},{32,96},{48,112},{64,128},{80,144},{96,160},{112,17... | collective-permute-start | bytes 688136 | tf_op jit(solution)/shard_map/ppermute | solution.py:207
  122.2 11.4 %collective-permute-start.10 = (bf16[2,512,224]{2,1,0:T(8,128)(2,1)}, bf16[2,512,224]{2,1,0:T(8,128)(2,1)}, u32[]{:S(2)}, u32[]{:S(2)}) collective-permute-start(bf16[2,512,224]{2,1,0:T(8,128)(2,1)} %fusion.14), channel_id=1, source_target_pairs={{0,448},{16,464},{32,480},{48,496},{64,0},{80,16},{96,32},{112,48}... | collective-permute-start | bytes 1376264 | tf_op jit(solution)/shard_map/ppermute | solution.py:207
  127.3 12.6 %collective-permute-start.9 = (bf16[512,224]{1,0:T(8,128)(2,1)}, bf16[512,224]{1,0:T(8,128)(2,1)}, u32[]{:S(2)}, u32[]{:S(2)}) collective-permute-start(bf16[512,224]{1,0:T(8,128)(2,1)} %get-tuple-element.32), channel_id=1, source_target_pairs={{0,64},{16,80},{32,96},{48,112},{64,128},{80,144},{96,160},{112,17... | collective-permute-start | bytes 688136 | tf_op jit(solution)/shard_map/ppermute | solution.py:207
  136.0 11.4 %collective-permute-start.11 = (bf16[2,512,224]{2,1,0:T(8,128)(2,1)}, bf16[2,512,224]{2,1,0:T(8,128)(2,1)}, u32[]{:S(2)}, u32[]{:S(2)}) collective-permute-start(bf16[2,512,224]{2,1,0:T(8,128)(2,1)} %get-tuple-element.16), channel_id=1, source_target_pairs={{0,448},{16,464},{32,480},{48,496},{64,0},{80,16},{96,32},{112,48}... | collective-permute-start | bytes 1376264 | tf_op jit(solution)/shard_map/ppermute | solution.py:207
  143.1 5.8 %copy-start.3 = (bf16[1,1,4,128,224]{3,4,0,1,2:T(8,128)(2,1)S(1)}, bf16[1,1,4,128,224]{3,4,0,1,2:T(8,128)(2,1)}, u32[]{:S(2)}) copy-start(bf16[1,1,4,128,224]{3,4,0,1,2:T(8,128)(2,1)} %copy.41) | copy-start | bytes 688132
  143.1 5.7 %copy-start.4 = (bf16[1,1,4,128,224]{3,4,0,1,2:T(8,128)(2,1)S(1)}, bf16[1,1,4,128,224]{3,4,0,1,2:T(8,128)(2,1)}, u32[]{:S(2)}) copy-start(bf16[1,1,4,128,224]{3,4,0,1,2:T(8,128)(2,1)} %copy.38) | copy-start | bytes 688132

commit v2 on v1

--- a/solution.py
+++ b/solution.py
@@ -158,7 +158,7 @@
 
 
 def grads_kernel(len_ref, q_ref, do_ref, k_ref, v_ref, mine, up1, up2, down1, down2,
-                 dq_ref, dk_ref, dv_ref, stat, kt_ref, dqt, dk_acc, dv_acc):
+                 qp_ref, kp_ref, stat, kt_ref, dqt, dk_acc, dv_acc):
     z = lax.axis_index("seq") // XN
     docs = Docs(len_ref)
     for qs, (m, inv, d) in enumerate(combine_stats(docs, z, mine, up1, up2, down1, down2)):
@@ -185,88 +185,311 @@
 
     for_tiles(docs, z, body)
     for i in range(4):
-        dq_ref[i] = (dqt[i] * SCALE).T.astype(jnp.bfloat16)
-        dk_ref[i] = (dk_acc[i] * SCALE).astype(jnp.bfloat16)
-        dv_ref[i] = dv_acc[i].astype(jnp.bfloat16)
+        dq = (dqt[i] * SCALE).T.astype(jnp.bfloat16)
+        dk = (dk_acc[i] * SCALE).astype(jnp.bfloat16)
+        dv = dv_acc[i].astype(jnp.bfloat16)
+        for c in range(XN):
+            r = c * 128
+            qp_ref[i, c] = jnp.concatenate([dq[r + 32 * j : r + 32 * j + 32] for j in range(4)], axis=1)
+            kp_ref[i, c] = pack_pair(dk[r : r + 128], dv[r : r + 128])
+
+
+def copy_to(src, dst, send, recv, device):
+    return pltpu.make_async_remote_copy(
+        src_ref=src,
+        dst_ref=dst,
+        send_sem=send,
+        recv_sem=recv,
+        device_id={"seq": device},
+        device_id_type=pl.DeviceIdType.MESH,
+    )
+
+
+def greet(devices):
+    barrier = pltpu.get_barrier_semaphore()
+    for device in devices:
+        pl.semaphore_signal(barrier, inc=1, device_id={"seq": device}, device_id_type=pl.DeviceIdType.MESH)
+    pl.semaphore_wait(barrier, len(devices))
+
+
+def window(ref, off):
+    low = off // 128 * 128
+    high = -(-(off + HEAD) // 128) * 128
+    return ref[:, low:high][:, off - low : off - low + HEAD]
+
+
+def pack_pair(first, second):
+    return jnp.concatenate([first[:64], second[:64], first[64:], second[64:]], axis=1)
+
+
+def place():
+    me = lax.axis_index("seq")
+    z, x = me // XN, me % XN
+    up = lax.rem(z + 1, ZN) * XN + x
+    down = lax.rem(z + ZN - 1, ZN) * XN + x
+    peer = [z * XN + lax.rem(x + d, XN) for d in range(XN)]
+    return z, x, up, down, peer
+
+
+TYPES = (("q", 0), ("k", 1), ("q", 1), ("k", 0))
+
+
+def gather_kernel(len_ref, q_in, k_in, v_in, do_in, q_out, do_out, k_out, v_out,
+                  packed, own, q1, k1, qsel, ksel, q2, k2,
+                  x_send, x_recv, z_send, z_recv):
+    z, x, up, down, peer = place()
+    docs = Docs(len_ref)
+    lk, lq = docs.case(z * 512)
+    rk, rq = docs.case(z * 512 + 512)
+    arrays = {"q": (q_in, do_in), "k": (k_in, v_in)}
+
+    def pack(t):
+        kind, head = TYPES[t]
+        a, b = arrays[kind]
+        for xp in range(XN):
+            off = (2 * xp + head) * HEAD
+            packed[t, xp] = pack_pair(window(a, off), window(b, off))
+
+    def x_copy(t, d):
+        to = lax.rem(x + d, XN)
+        return copy_to(packed.at[t, to], own.at[t, x], x_send.at[t, d - 1], x_recv.at[t, d - 1], peer[d])
+
+    def z_copy(i, c):
+        src, dst, to = ((own.at[0, c], q1.at[c], down), (own.at[1, c], k1.at[c], up),
+                        (qsel.at[c], q2.at[c], down), (ksel.at[c], k2.at[c], up))[i]
+        return copy_to(src, dst, z_send.at[i, c], z_recv.at[i, c], to)
+
+    def unpack(value, slot, c, first, second):
+        top, low = pl.ds(c * 128, 64), pl.ds(c * 128 + 64, 64)
+        first[slot, top, :] = value[:, 0:HEAD]
+        second[slot, top, :] = value[:, HEAD : 2 * HEAD]
+        first[slot, low, :] = value[:, 2 * HEAD : 3 * HEAD]
+        second[slot, low, :] = value[:, 3 * HEAD : 4 * HEAD]
+
+    pack(0)
+    pack(1)
+    greet(peer[1:] + [up, down])
+    for t in (0, 1):
+        own[t, x] = packed[t, x]
+        for d in (2, 1, 3):
+            x_copy(t, d).start()
+    z_copy(0, x).start()
+    z_copy(1, x).start()
+    for t in (2, 3):
+        pack(t)
+        own[t, x] = packed[t, x]
+        for d in (2, 1, 3):
+            x_copy(t, d).start()
+
+    def source(d):
+        return lax.rem(x + d, XN)
+
+    def got_x(t, d):
+        back = XN - d
+        copy_to(packed.at[t, x], own.at[t, source(d)], x_send.at[t, back - 1], x_recv.at[t, back - 1], peer[d]).wait_recv()
+
+    for d in (1, 3, 2):
+        c = source(d)
+        for t in (0, 1):
+            got_x(t, d)
+            z_copy(t, c).start()
+    for d in (0, 1, 3, 2):
+        c = source(d)
+        if d:
+            got_x(2, d)
+            got_x(3, d)
+        z_copy(0, c).wait_recv()
+        qsel[c] = jnp.where(lq, own[2, c], q1[c])
+        z_copy(2, c).start()
+        z_copy(1, c).wait_recv()
+        ksel[c] = jnp.where(rk, own[3, c], k1[c])
+        z_copy(3, c).start()
+        unpack(own[0, c], 0, c, q_out, do_out)
+        unpack(own[1, c], 0, c, k_out, v_out)
+        unpack(own[2, c], 3, c, q_out, do_out)
+        unpack(own[3, c], 3, c, k_out, v_out)
+        unpack(q1[c], 1, c, q_out, do_out)
+        unpack(k1[c], 1, c, k_out, v_out)
+    for d in (0, 1, 3, 2):
+        c = source(d)
+        z_copy(2, c).wait_recv()
+        unpack(q2[c], 2, c, q_out, do_out)
+        z_copy(3, c).wait_recv()
+        unpack(k2[c], 2, c, k_out, v_out)
+    for t in range(4):
+        for d in (1, 2, 3):
+            x_copy(t, d).wait_send()
+        for c in range(XN):
+            z_copy(t, c).wait_send()
+
+
+def share_kernel(mine, up1, up2, down1, down2, send, recv):
+    z, x, up, down, _ = place()
+    upper = lax.rem(z + 2, ZN) * XN + x
+    lower = lax.rem(z + ZN - 2, ZN) * XN + x
+    greet([up, upper, down, lower])
+    copies = [copy_to(mine, ref, send.at[i], recv.at[i], to)
+              for i, (ref, to) in enumerate(((up1, down), (up2, lower), (down1, up), (down2, upper)))]
+    for copy in copies:
+        copy.start()
+    for copy in copies:
+        copy.wait()
+
+
+def scatter_kernel(len_ref, qp, kp, dq_out, dk_out, dv_out,
+                   rq2, rk2, rq1, rk1, qs, ks, qfin, kfin, qhome, khome,
+                   z_send, z_recv, x_send, x_recv):
+    z, x, up, down, peer = place()
+    docs = Docs(len_ref)
+    lk, lq = docs.case(z * 512)
+    rk, rq = docs.case(z * 512 + 512)
+    low, top = z >= 1, z < ZN - 1
+    lm = jnp.logical_not(lk | lq) & low
+    rm = jnp.logical_not(rk | rq) & top
+    lq, rk = lq & low, rk & top
+
+    def z_copy(i, c):
+        src, dst, to = ((qp.at[2, c], rq2.at[c], up), (kp.at[2, c], rk2.at[c], down),
+                        (qs.at[c], rq1.at[c], up), (ks.at[c], rk1.at[c], down))[i]
+        return copy_to(src, dst, z_send.at[i, c], z_recv.at[i, c], to)
+
+    def plus(a, b, use):
+        return (a.astype(jnp.float32) + jnp.where(use, b.astype(jnp.float32), 0.0)).astype(jnp.bfloat16)
+
+    def dest(d):
+        return lax.rem(x + d, XN)
+
+    def x_copy(kind, head, d):
+        src, dst = ((qfin, qhome), (kfin, khome))[kind]
+        i = 2 * kind + head
+        return copy_to(src.at[head, dest(d)], dst.at[head, x], x_send.at[i, d - 1], x_recv.at[i, d - 1], peer[d])
+
+    def send_home(kind, head, d, value):
+        src, dst = ((qfin, qhome), (kfin, khome))[kind]
+        if d:
+            src[head, dest(d)] = value
+            x_copy(kind, head, d).start()
+        else:
+            dst[head, x] = value
+
+    order = (2, 1, 3, 0)
+    greet(peer[1:] + [up, down])
+    for d in order:
+        z_copy(1, dest(d)).start()
+        z_copy(0, dest(d)).start()
+    for d in order:
+        c = dest(d)
+        z_copy(1, c).wait_recv()
+        back = rk2[c]
+        ks[c] = plus(kp[1, c], back, rm)
+        z_copy(3, c).start()
+        z_copy(0, c).wait_recv()
+        fore = rq2[c]
+        qs[c] = plus(qp[1, c], fore, lm)
+        z_copy(2, c).start()
+        send_home(1, 0, d, plus(kp[3, c], back, rk))
+        send_home(0, 1, d, plus(qp[3, c], fore, lq))
+    for d in order:
+        c = dest(d)
+        z_copy(3, c).wait_recv()
+        send_home(1, 1, d, plus(kp[0, c], rk1[c], top))
+        z_copy(2, c).wait_recv()
+        send_home(0, 0, d, plus(qp[0, c], rq1[c], low))
+    for i in range(4):
+        for d in (1, 2, 3):
+            x_copy(i // 2, i % 2, d).wait_recv()
+    for a, out, n in ((0, dq_out, 4), (0, dk_out, 2), (1, dv_out, 2)):
+        home = qhome if n == 4 else khome
+        step = 128 // n
+        for part in range(n):
+            lanes = (part if n == 4 else 2 * part + a) * HEAD
+            pieces = []
+            for xs in range(XN):
+                for head in range(2):
+                    pieces.append(home[head, xs][:, lanes : lanes + HEAD])
+            out[part * step : (part + 1) * step, :] = jnp.concatenate(pieces, axis=1)
+    for i in range(4):
+        for c in range(XN):
+            z_copy(i, c).wait_send()
+        for d in (1, 2, 3):
+            x_copy(i // 2, i % 2, d).wait_send()
 
 
 VM = pl.BlockSpec(memory_space=pltpu.VMEM)
 SM = pl.BlockSpec(memory_space=pltpu.SMEM)
-BIG = pltpu.CompilerParams(vmem_limit_bytes=48 * 1024 * 1024)
+LIMIT = 48 * 1024 * 1024
+BIG = pltpu.CompilerParams(vmem_limit_bytes=LIMIT)
+DMA = pltpu.SemaphoreType.DMA
+
+
+def remote(number):
+    return pltpu.CompilerParams(vmem_limit_bytes=LIMIT, collective_id=number, has_side_effects=True)
+
+
+def buf(*shape, dtype=jnp.bfloat16):
+    return pltpu.VMEM(shape, dtype)
+
+
+def out(*shape, dtype=jnp.bfloat16):
+    return jax.ShapeDtypeStruct(shape, dtype)
 
 
 def shards(queries, key_vectors, value_vectors, out_grad, doc_lengths):
     rows, width = queries.shape[1], queries.shape[2]
-    idx = lax.axis_index("seq")
-    z = idx // XN
-    docs = Docs(doc_lengths)
-    x_groups = [[XN * a + b for b in range(XN)] for a in range(ZN)]
-    n = ZN * XN
-
-    def move(value, dz):
-        return lax.ppermute(value, "seq", [(i, (i + XN * dz) % n) for i in range(n)])
-
-    stacked = jnp.concatenate([queries, out_grad, key_vectors, value_vectors], axis=0)
-    shaped = stacked.reshape(4, rows, XN, 2, HEAD).transpose(2, 3, 0, 1, 4)
-    got = lax.all_to_all(shaped, "seq", split_axis=0, concat_axis=0, axis_index_groups=x_groups, tiled=True)
-    got = got.transpose(1, 2, 0, 3, 4).reshape(2, 4, XN * rows, HEAD)
-    a_q, a_k = got[0, 0:2], got[0, 2:4]
-    b_q, b_k = got[1, 0:2], got[1, 2:4]
-    lk, lq = docs.case(z * 512)
-    rk, rq = docs.case(z * 512 + 512)
-    back1 = move(a_q, -1)
-    fore1 = move(b_k, 1)
-    back2 = move(jnp.where(lq, b_q, back1), -1)
-    fore2 = move(jnp.where(rk, a_k, fore1), 1)
-    qs = jnp.stack([a_q[0], back1[0], back2[0], b_q[0]])
-    dos = jnp.stack([a_q[1], back1[1], back2[1], b_q[1]])
-    ks = jnp.stack([b_k[0], fore1[0], fore2[0], a_k[0]])
-    vs = jnp.stack([b_k[1], fore1[1], fore2[1], a_k[1]])
+    chunk = (XN, 64, 4 * HEAD)
+    small = (XN, 32, 4 * HEAD)
+    block = out(4, 512, HEAD)
+    qs, dos, ks, vs = pl.pallas_call(
+        gather_kernel,
+        out_shape=(block,) * 4,
+        in_specs=[SM] + [VM] * 4,
+        out_specs=(VM,) * 4,
+        scratch_shapes=[buf(4, *chunk), buf(4, *chunk)] + [buf(*chunk)] * 6
+        + [DMA((4, 3)), DMA((4, 3)), DMA((4, 4)), DMA((4, 4))],
+        compiler_params=remote(0),
+    )(doc_lengths, queries[0], key_vectors[0], value_vectors[0], out_grad[0])
+    stat = out(16, 512, dtype=jnp.float32)
     mine = pl.pallas_call(
         stats_kernel,
-        out_shape=jax.ShapeDtypeStruct((16, 512), jnp.float32),
+        out_shape=stat,
         in_specs=[SM] + [VM] * 4,
         out_specs=VM,
         compiler_params=BIG,
     )(doc_lengths, qs, dos, ks, vs)
-    up1, up2 = move(mine, -1), move(mine, -2)
-    down1, down2 = move(mine, 1), move(mine, 2)
-    block = jax.ShapeDtypeStruct((4, 512, HEAD), jnp.bfloat16)
-    dq, dk, dv = pl.pallas_call(
+    others = pl.pallas_call(
+        share_kernel,
+        out_shape=(stat,) * 4,
+        in_specs=[VM],
+        out_specs=(VM,) * 4,
+        scratch_shapes=[DMA((4,)), DMA((4,))],
+        compiler_params=remote(1),
+    )(mine)
+    qp, kp = pl.pallas_call(
         grads_kernel,
-        out_shape=(block, block, block),
+        out_shape=(out(4, *small), out(4, *chunk)),
         in_specs=[SM] + [VM] * 9,
-        out_specs=(VM, VM, VM),
+        out_specs=(VM, VM),
         scratch_shapes=[
-            pltpu.VMEM((16, 512), jnp.float32),
-            pltpu.VMEM((4, HEAD, 512), jnp.bfloat16),
-            pltpu.VMEM((4, HEAD, 512), jnp.float32),
-            pltpu.VMEM((4, 512, HEAD), jnp.float32),
-            pltpu.VMEM((4, 512, HEAD), jnp.float32),
+            buf(16, 512, dtype=jnp.float32),
+            buf(4, HEAD, 512),
+            buf(4, HEAD, 512, dtype=jnp.float32),
+            buf(4, 512, HEAD, dtype=jnp.float32),
+            buf(4, 512, HEAD, dtype=jnp.float32),
         ],
         compiler_params=BIG,
-    )(doc_lengths, qs, dos, ks, vs, mine, up1, up2, down1, down2)
-    kv = jnp.stack([dk, dv])
-    f32 = jnp.float32
-
-    def plus(base, term, use):
-        return (base.astype(f32) + jnp.where(use, term.astype(f32), 0.0)).astype(jnp.bfloat16)
-
-    lm = jnp.logical_not(lk | lq)
-    rm = jnp.logical_not(rk | rq)
-    q2 = move(dq[2], 1)
-    k2 = move(kv[:, 2], -1)
-    q_first = plus(dq[1], q2, lm & (z >= 1))
-    q_b = plus(dq[3], q2, lq & (z >= 1))
-    k_first = plus(kv[:, 1], k2, rm & (z < ZN - 1))
-    k_a = plus(kv[:, 3], k2, rk & (z < ZN - 1))
-    q_a = plus(dq[0], move(q_first, 1), z >= 1)
-    k_b = plus(kv[:, 0], move(k_first, -1), z < ZN - 1)
-    out = jnp.stack([jnp.stack([q_a, k_a[0], k_a[1]]), jnp.stack([q_b, k_b[0], k_b[1]])])
-    out = out.reshape(2, 3, XN, rows, HEAD).transpose(2, 0, 1, 3, 4)
-    home = lax.all_to_all(out, "seq", split_axis=0, concat_axis=0, axis_index_groups=x_groups, tiled=True)
-    home = home.transpose(2, 3, 0, 1, 4).reshape(3, 1, rows, width)
-    return home[0], home[1], home[2]
+    )(doc_lengths, qs, dos, ks, vs, mine, *others)
+    full = out(rows, width)
+    grads = pl.pallas_call(
+        scatter_kernel,
+        out_shape=(full,) * 3,
+        in_specs=[SM, VM, VM],
+        out_specs=(VM,) * 3,
+        scratch_shapes=[buf(*small), buf(*chunk), buf(*small), buf(*chunk), buf(*small), buf(*chunk),
+                        buf(2, *small), buf(2, *chunk), buf(2, *small), buf(2, *chunk),
+                        DMA((4, 4)), DMA((4, 4)), DMA((4, 3)), DMA((4, 3))],
+        compiler_params=remote(2),
+    )(doc_lengths, qp, kp)
+    return tuple(g[None] for g in grads)
 
 
 def solution(mesh):

time: 168 us -> 102 us (0.61)
  Pallas kernels: 9.57 us -> 92.2 us
  starting transfers between devices: 61 us -> 0 us
  blocking collectives: 42.8 us -> 0 us
  waiting for transfers between devices: 19.1 us -> 0 us
  between operations: 11.3 us -> 0.68 us
  other arithmetic: 8.84 us -> 0 us
  local copies, waits for them, and re-layouts: 14.6 us -> 8.52 us
    pallas_call x2 -> x5, Pallas kernels: 9.57 us -> 92.2 us  [the longest x1 43.3 us: shards(): pl.pallas_call(gather_kernel, out_shape=(block,) * 4, in_specs=[SM] + [VM...]
    ppermute x12 -> x0, starting transfers between devices: 61 us -> none  [move(): lax.ppermute(value, 'seq', [(i, (i + XN * dz) % n) for i in range(n)])]
    all_to_all x2 -> x0, blocking collectives: 42.8 us -> none  [the longest x1 27.7 us: shards(): lax.all_to_all(shaped, 'seq', split_axis=0, concat_axis=0, axis_index_gro...]
    ppermute x12 -> x0, waiting for transfers between devices: 19.1 us -> none  [move(): lax.ppermute(value, 'seq', [(i, (i + XN * dz) % n) for i in range(n)])]
    convert_element_type x4 -> x0, other arithmetic: 6.44 us -> none  [plus(): (base.astype(f32) + jnp.where(use, term.astype(f32), 0.0)).astype(jnp.bfl...]
    another operation x4 -> x0, local copies, waits for them, and re-layouts: 3.2 us -> none  [the longest x2 2.12 us: shards(): jnp.stack([q_a, k_a[0], k_a[1]])]
    transpose x2 -> x0, local copies, waits for them, and re-layouts: 2.87 us -> none  [the longest x1 2.75 us: shards(): got = got.transpose(1, 2, 0, 3, 4).reshape(2, 4, XN * rows, HEAD)]
    unnamed x21 -> x15, local copies, waits for them, and re-layouts: 6.29 us -> 8.52 us
  transfers between devices with their start and end apart: 12 -> 0, of which waited for: 6 -> 0; matrix products, arithmetic and copies ran while one was open for 6% -> 0% of each run, Pallas kernels for 0% -> 0%
where the time goes in v2:
time: 102 us; the launch traced here: 101 us
  Pallas kernels  92.2 us (90%)
  local copies, waits for them, and re-layouts  8.52 us (8%)
    pallas_call x1, Pallas kernels, shards(): pl.pallas_call(gather_kernel, out_shape=(block,) * 4, in_specs=[SM] + [VM...  43.3 us
    pallas_call x1, Pallas kernels, shards(): pl.pallas_call(scatter_kernel, out_shape=(full,) * 3, in_specs=[SM, VM, V...  29.7 us
    unnamed x15, local copies, waits for them, and re-layouts  8.52 us
    pallas_call x1, Pallas kernels, shards(): pl.pallas_call(grads_kernel, out_shape=(out(4, *small), out(4, *chunk)),...  7.81 us
    pallas_call x1, Pallas kernels, shards(): pl.pallas_call(share_kernel, out_shape=(stat,) * 4, in_specs=[VM], out_sp...  7.44 us
    pallas_call x1, Pallas kernels, shards(): pl.pallas_call(stats_kernel, out_shape=stat, in_specs=[SM] + [VM] * 4, ou...  3.98 us

profile of v2, /device:TPU:56, one launch (start us, length us, event | category | flops | bytes accessed | tf_op | source)
XLA Modules:
  0.0 101.4 jit_solution(17379284733829714631)
XLA Ops:
  0.6 0.0 copy-start.1
  0.6 1.0 copy-done.1
  1.7 0.0 copy-start.2
  1.7 1.0 %copy-done.2 = bf16[1,128,1792]{2,1,0:T(8,128)(2,1)S(1)} copy-done((bf16[1,128,1792]{2,1,0:T(8,128)(2,1)S(1)}, bf16[1,128,1792]{2,1,0:T(8,128)(2,1)}, u32[]{:S(2)}) %copy-start.2) | copy-done | bytes 458776
  2.7 0.0 copy-start.3
  2.7 1.0 %copy-done.3 = bf16[1,128,1792]{2,1,0:T(8,128)(2,1)S(1)} copy-done((bf16[1,128,1792]{2,1,0:T(8,128)(2,1)S(1)}, bf16[1,128,1792]{2,1,0:T(8,128)(2,1)}, u32[]{:S(2)}) %copy-start.3) | copy-done | bytes 458776
  3.7 0.0 copy-start.4
  3.7 1.0 %copy-done.4 = bf16[1,128,1792]{2,1,0:T(8,128)(2,1)S(1)} copy-done((bf16[1,128,1792]{2,1,0:T(8,128)(2,1)S(1)}, bf16[1,128,1792]{2,1,0:T(8,128)(2,1)}, u32[]{:S(2)}) %copy-start.4) | copy-done | bytes 458776
  4.7 0.0 copy-start.5
  4.7 0.7 copy-done.5
  5.4 43.3 %shard_map.76 = (bf16[4,512,224]{2,1,0:T(8,128)(2,1)S(1)}, bf16[4,512,224]{2,1,0:T(8,128)(2,1)S(1)}, bf16[4,512,224]{2,1,0:T(8,128)(2,1)S(1)}, bf16[4,512,224]{2,1,0:T(8,128)(2,1)S(1)}) custom-call(s32[8]{0:T(128)S(1)} %copy-done.5, bf16[128,1792]{1,0:T(8,128)(2,1)S(1)} %bitcast.10, bf16[128,1792]{1,0:T(8,128)(2,1)S(1)} %bitcast.11, ...), custom_call_target="tpu_custom_call" | custom-call | tf_op jit(solution)/shard_map/pallas_call | solution.py:442
  48.6 4.0 %shard_map.77.mine = f32[16,512]{1,0:T(8,128)S(1)} custom-call(s32[8]{0:T(128)S(1)} %copy-done.5, bf16[4,512,224]{2,1,0:T(8,128)(2,1)S(1)} %get-tuple-element.16.q_ref, bf16[4,512,224]{2,1,0:T(8,128)(2,1)S(1)} %get-tuple-element.17.do_ref, bf16[4,512,224]{2,1,0:T(8,128)(2,1)S(1)} %get-tuple-element.18.k_ref, bf16[4,512,224]{2,1,0:T(8,128)(2,1)S(1)} %get-tuple-element.19.v_ref), custom_call_target="tpu_custom_call" | custom-call | tf_op jit(solution)/shard_map/pallas_call | solution.py:452
  52.6 7.4 %shard_map.78 = (f32[16,512]{1,0:T(8,128)S(1)}, f32[16,512]{1,0:T(8,128)S(1)}, f32[16,512]{1,0:T(8,128)S(1)}, f32[16,512]{1,0:T(8,128)S(1)}) custom-call(f32[16,512]{1,0:T(8,128)S(1)} %shard_map.77.mine), custom_call_target="tpu_custom_call" | custom-call | tf_op jit(solution)/shard_map/pallas_call | solution.py:459
  60.1 7.8 %shard_map.79 = (bf16[4,4,32,896]{3,2,1,0:T(8,128)(2,1)S(1)}, bf16[4,4,64,896]{3,2,1,0:T(8,128)(2,1)}) custom-call(s32[8]{0:T(128)S(1)} %copy-done.5, bf16[4,512,224]{2,1,0:T(8,128)(2,1)S(1)} %get-tuple-element.16.q_ref, bf16[4,512,224]{2,1,0:T(8,128)(2,1)S(1)} %get-tuple-element.17.do_ref, bf16[4,512,224]{2,1,0:T(8,128)(2,1)S(1)} %get-tuple-element.18.k_ref, ...), custom_call_target="tpu_custom_call" | custom-call | tf_op jit(solution)/shard_map/pallas_call | solution.py:467
  67.9 0.0 copy-start
  67.9 1.5 %copy-done = bf16[4,4,64,896]{3,2,1,0:T(8,128)(2,1)S(1)} copy-done((bf16[4,4,64,896]{3,2,1,0:T(8,128)(2,1)S(1)}, bf16[4,4,64,896]{3,2,1,0:T(8,128)(2,1)}, u32[]{:S(2)}) %copy-start) | copy-done | bytes 1835032
  69.4 29.7 %shard_map.80 = (bf16[128,1792]{1,0:T(8,128)(2,1)S(1)}, bf16[128,1792]{1,0:T(8,128)(2,1)S(1)}, bf16[128,1792]{1,0:T(8,128)(2,1)S(1)}) custom-call(s32[8]{0:T(128)S(1)} %copy-done.5, bf16[4,4,32,896]{3,2,1,0:T(8,128)(2,1)S(1)} %get-tuple-element.24.qp, bf16[4,4,64,896]{3,2,1,0:T(8,128)(2,1)S(1)} %copy-done), custom_call_target="tpu_custom_call" | custom-call | tf_op jit(solution)/shard_map/pallas_call | solution.py:482
  99.1 0.8 copy.11
  99.9 0.8 copy.12
  100.6 0.8 copy.13
Async XLA Ops:
  0.6 1.0 %copy-start.1 = (bf16[1,128,1792]{2,1,0:T(8,128)(2,1)S(1)}, bf16[1,128,1792]{2,1,0:T(8,128)(2,1)}, u32[]{:S(2)}) copy-start(bf16[1,128,1792]{2,1,0:T(8,128)(2,1)} %param.5) | copy-start | bytes 1376260
  1.7 1.0 %copy-start.2 = (bf16[1,128,1792]{2,1,0:T(8,128)(2,1)S(1)}, bf16[1,128,1792]{2,1,0:T(8,128)(2,1)}, u32[]{:S(2)}) copy-start(bf16[1,128,1792]{2,1,0:T(8,128)(2,1)} %param.6) | copy-start | bytes 1376260
  2.7 1.0 %copy-start.3 = (bf16[1,128,1792]{2,1,0:T(8,128)(2,1)S(1)}, bf16[1,128,1792]{2,1,0:T(8,128)(2,1)}, u32[]{:S(2)}) copy-start(bf16[1,128,1792]{2,1,0:T(8,128)(2,1)} %param.7) | copy-start | bytes 1376260
  3.7 1.0 %copy-start.4 = (bf16[1,128,1792]{2,1,0:T(8,128)(2,1)S(1)}, bf16[1,128,1792]{2,1,0:T(8,128)(2,1)}, u32[]{:S(2)}) copy-start(bf16[1,128,1792]{2,1,0:T(8,128)(2,1)} %param.8) | copy-start | bytes 1376260
  4.7 0.7 copy-start.5
  67.9 1.5 %copy-start = (bf16[4,4,64,896]{3,2,1,0:T(8,128)(2,1)S(1)}, bf16[4,4,64,896]{3,2,1,0:T(8,128)(2,1)}, u32[]{:S(2)}) copy-start(bf16[4,4,64,896]{3,2,1,0:T(8,128)(2,1)} %get-tuple-element.25.kp) | copy-start | bytes 5505028

commit v3 on v2

v3 whole, which is shorter than its diff:
```python
import functools

import jax
import jax.numpy as jnp
from jax import lax
from jax.experimental import pallas as pl
from jax.experimental.pallas import tpu as pltpu
from jax.sharding import PartitionSpec as P

HEAD = 224
ZN, XN = 8, 4
SCALE = HEAD ** (-0.5)
NEG = -1e30
LOW = -1e20
TILE = 256
GROUP = 4
ITEMS = ((0, 3), (1, 3), (2, 3), (0, 2), (1, 2), (2, 2), (3, 0), (3, 1), (3, 2), (2, 0), (2, 1))


class Docs:
    def __init__(self, lengths):
        self.bounds = []
        total = jnp.int32(0)
        for d in range(8):
            total = total + lengths[d]
            self.bounds.append(total)

    def start(self, t):
        r = jnp.int32(0)
        for b in self.bounds[:7]:
            r = jnp.where(b <= t, b, r)
        return r

    def end(self, t):
        r = jnp.int32(4096)
        for b in reversed(self.bounds):
            r = jnp.where(b > t, b, r)
        return r

    def row_start(self, pos):
        r = jnp.zeros_like(pos)
        for b in self.bounds[:7]:
            r = jnp.where(pos >= b, b, r)
        return r

    def case(self, t):
        before = t - self.start(t - 1)
        after = self.end(t - 1) - t
        keys = after > 1024
        return keys, (before > 1024) & jnp.logical_not(keys)


def slots(docs, z):
    lk, lq = docs.case(z * 512)
    rk, rq = docs.case(z * 512 + 512)
    lm = jnp.logical_not(lk | lq)
    rm = jnp.logical_not(rk | rq)
    q_ids = (z, z + 1, jnp.where(rq, z + 1, z + 2), z)
    k_ids = (z, z - 1, jnp.where(lk, z - 1, z - 2), z)
    valid = {
        (0, 3): True,
        (1, 3): jnp.logical_not(rk),
        (2, 3): rm,
        (0, 2): lk,
        (1, 2): lk & jnp.logical_not(rk),
        (2, 2): (lk & rm) | (rq & lm),
        (3, 0): True,
        (3, 1): jnp.logical_not(lq),
        (3, 2): lm,
        (2, 0): rq,
        (2, 1): rq & jnp.logical_not(lq),
    }
    return q_ids, k_ids, valid


NT = (((1,), (1,)), ((), ()))


def list_tiles(docs, z, todo):
    q_ids, k_ids, valid = slots(docs, z)
    firsts = [[docs.start(q_ids[qs] * 512 + qt * TILE) for qt in range(2)] for qs in range(4)]
    count = jnp.int32(0)
    for qs, ks in ITEMS:
        qid, kid, ok = q_ids[qs], k_ids[ks], valid[(qs, ks)]
        use = (qid < ZN) & (kid >= 0) & ok
        for qt in range(2):
            q0 = qid * 512 + qt * TILE
            for kt in range(2):
                k0 = kid * 512 + kt * TILE
                k1 = k0 + TILE - 1
                hit = use & (k0 <= q0 + TILE - 1) & ((k1 >= q0) | (k1 >= firsts[qs][qt]))
                todo[0, count] = 2 * qs + qt
                todo[1, count] = 2 * ks + kt
                todo[2, count] = q0
                todo[3, count] = k0
                count = count + jnp.where(hit, 1, 0)
    for i in range(GROUP - 1):
        todo[0, count + i] = 0
        todo[1, count + i] = 0
        todo[2, count + i] = 0
        todo[3, count + i] = 1 << 20
    return count


def for_groups(count, todo, body):
    @pl.loop(0, (count + GROUP - 1) // GROUP)
    def _(g):
        body([tuple(todo[j, g * GROUP + i] for j in range(4)) for i in range(GROUP)])


def tile_rows(ref, i):
    return ref[pl.ds(pl.multiple_of(i * TILE, TILE), TILE), :]


def raw_scores(k, q):
    return lax.dot_general(k, q, NT, preferred_element_type=jnp.float32)


def masked(docs, s, q0, k0):
    kpos = k0 + lax.broadcasted_iota(jnp.int32, (TILE, 1), 0)
    qpos = q0 + lax.broadcasted_iota(jnp.int32, (1, TILE), 1)
    qstart = docs.row_start(qpos)
    return jnp.where((kpos <= qpos) & (kpos >= qstart), s * SCALE, NEG)


def stats_kernel(len_ref, q_ref, do_ref, k_ref, v_ref, st_ref, todo):
    z = lax.axis_index("seq") // XN
    docs = Docs(len_ref)
    st_ref[:, 0:1, :] = jnp.full((8, 1, TILE), LOW, jnp.float32)
    st_ref[:, 1:4, :] = jnp.zeros((8, 3, TILE), jnp.float32)

    def body(tiles):
        raw = []
        for qi, ki, q0, k0 in tiles:
            s = raw_scores(tile_rows(k_ref, ki), tile_rows(q_ref, qi))
            raw.append((s, raw_scores(tile_rows(v_ref, ki), tile_rows(do_ref, qi))))
        for (qi, ki, q0, k0), (s, dp) in zip(tiles, raw):
            s = masked(docs, s, q0, k0)
            old = st_ref[qi, 0:1, :]
            new = jnp.maximum(old, jnp.max(s, axis=0, keepdims=True))
            p = jnp.exp(s - new)
            alpha = jnp.exp(old - new)
            st_ref[qi, 0:1, :] = new
            st_ref[qi, 1:2, :] = st_ref[qi, 1:2, :] * alpha + jnp.sum(p, axis=0, keepdims=True)
            st_ref[qi, 2:3, :] = st_ref[qi, 2:3, :] * alpha + jnp.sum(p * dp, axis=0, keepdims=True)

    for_groups(list_tiles(docs, z, todo), todo, body)


def combine_stats(docs, z, mine, up1, up2, down1, down2):
    lk, lq = docs.case(z * 512)
    rk, rq = docs.case(z * 512 + 512)
    lm = jnp.logical_not(lk | lq)
    rm = jnp.logical_not(rk | rq)
    bk, bq = docs.case(z * 512 - 512)
    bm = jnp.logical_not(bk | bq) & (z >= 2)

    def part(ref, slot, use=None):
        m, l, d = (ref[2 * slot : 2 * slot + 2, r : r + 1, :] for r in range(3))
        if use is not None:
            m = jnp.where(use, m, LOW)
            l = jnp.where(use, l, 0.0)
            d = jnp.where(use, d, 0.0)
        return m, l, d

    groups = (
        (part(mine, 0), part(down1, 1, z >= 1), part(down2, 2, bm)),
        (part(mine, 1), part(up1, 0, z + 1 < ZN), part(down1, 2, lm & (z >= 1))),
        (part(mine, 2), part(up2, 0, rm & (z + 2 < ZN)), part(up1, 1, rm & (z + 1 < ZN)), part(up1, 3, rq & (z + 1 < ZN))),
        (part(mine, 3), part(down1, 2, lq & (z >= 1))),
    )
    out = []
    for parts in groups:
        m = functools.reduce(jnp.maximum, [p[0] for p in parts])
        l = sum(p[1] * jnp.exp(p[0] - m) for p in parts)
        d = sum(p[2] * jnp.exp(p[0] - m) for p in parts)
        inv = jnp.where(l > 0.0, 1.0 / jnp.where(l > 0.0, l, 1.0), 0.0)
        out.append((m, inv, d * inv))
    return out


def grads_kernel(len_ref, q_ref, do_ref, k_ref, v_ref, mine, up1, up2, down1, down2,
                 qp_ref, kp_ref, stat, todo, kt_ref, dqt, dk_acc, dv_acc):
    z = lax.axis_index("seq") // XN
    docs = Docs(len_ref)
    for qs, values in enumerate(combine_stats(docs, z, mine, up1, up2, down1, down2)):
        for r, value in enumerate(values):
            stat[2 * qs : 2 * qs + 2, r : r + 1, :] = value
    for i in range(8):
        kt_ref[i] = k_ref[i * TILE : (i + 1) * TILE, :].T
    dqt[...] = jnp.zeros_like(dqt)
    dk_acc[...] = jnp.zeros_like(dk_acc)
    dv_acc[...] = jnp.zeros_like(dv_acc)

    def body(tiles):
        raw = []
        for qi, ki, q0, k0 in tiles:
            s = raw_scores(tile_rows(k_ref, ki), tile_rows(q_ref, qi))
            raw.append((s, raw_scores(tile_rows(v_ref, ki), tile_rows(do_ref, qi))))
        weights = []
        for (qi, ki, q0, k0), (s, dp) in zip(tiles, raw):
            p = jnp.exp(masked(docs, s, q0, k0) - stat[qi, 0:1, :]) * stat[qi, 1:2, :]
            weights.append((p.astype(jnp.bfloat16), (p * (dp - stat[qi, 2:3, :])).astype(jnp.bfloat16)))
        terms = []
        for (qi, ki, q0, k0), (p, ds) in zip(tiles, weights):
            terms.append((
                jnp.dot(p, tile_rows(do_ref, qi), preferred_element_type=jnp.float32),
                jnp.dot(ds, tile_rows(q_ref, qi), preferred_element_type=jnp.float32),
                jnp.dot(kt_ref[ki], ds, preferred_element_type=jnp.float32),
            ))
        for (qi, ki, q0, k0), (dv, dk, dq) in zip(tiles, terms):
            dv_acc[ki] += dv
            dk_acc[ki] += dk
            dqt[qi] += dq

    for_groups(list_tiles(docs, z, todo), todo, body)
    for i in range(8):
        dq = (dqt[i] * SCALE).T.astype(jnp.bfloat16)
        dk = (dk_acc[i] * SCALE).astype(jnp.bfloat16)
        dv = dv_acc[i].astype(jnp.bfloat16)
        for half in range(2):
            r, c = half * 128, 2 * (i % 2) + half
            qp_ref[i // 2, c] = jnp.concatenate([dq[r + 32 * j : r + 32 * j + 32] for j in range(4)], axis=1)
            kp_ref[i // 2, c] = pack_pair(dk[r : r + 128], dv[r : r + 128])


def copy_to(src, dst, send, recv, device):
    return pltpu.make_async_remote_copy(
        src_ref=src,
        dst_ref=dst,
        send_sem=send,
        recv_sem=recv,
        device_id={"seq": device},
        device_id_type=pl.DeviceIdType.MESH,
    )


def meet(devices):
    for device in devices:
        pl.semaphore_signal(
            pltpu.get_barrier_semaphore(), inc=1, device_id={"seq": device}, device_id_type=pl.DeviceIdType.MESH
        )


def greet(devices):
    meet(devices)
    pl.semaphore_wait(pltpu.get_barrier_semaphore(), len(devices))


def window(ref, off):
    low = off // 128 * 128
    high = -(-(off + HEAD) // 128) * 128
    return ref[:, low:high][:, off - low : off - low + HEAD]


def pack_pair(first, second):
    return jnp.concatenate([first[:64], second[:64], first[64:], second[64:]], axis=1)


def place():
    me = lax.axis_index("seq")
    z, x = me // XN, me % XN
    up = lax.rem(z + 1, ZN) * XN + x
    down = lax.rem(z + ZN - 1, ZN) * XN + x
    peer = [z * XN + lax.rem(x + d, XN) for d in range(XN)]
    return z, x, up, down, peer


TYPES = (("q", 0), ("k", 1), ("q", 1), ("k", 0))


def gather_kernel(len_ref, raw, q_out, do_out, k_out, v_out,
                  packed, own, q1, k1, qsel, ksel, q2, k2,
                  x_send, x_recv, z_send, z_recv):
    z, x, up, down, peer = place()
    low, top = z > 0, z < ZN - 1
    meet(peer[1:])
    pl.when(low)(lambda: meet([down]))
    pl.when(top)(lambda: meet([up]))
    docs = Docs(len_ref)
    lk, lq = docs.case(z * 512)
    rk, rq = docs.case(z * 512 + 512)

    def pack(t, xp):
        kind, head = TYPES[t]
        i = 0 if kind == "q" else 2
        off = (2 * xp + head) * HEAD
        packed[t, xp] = pack_pair(window(raw.at[i], off), window(raw.at[i + 1], off))

    def x_copy(t, d):
        to = lax.rem(x + d, XN)
        return copy_to(packed.at[t, to], own.at[t, x], x_send.at[t, d - 1], x_recv.at[t, d - 1], peer[d])

    def z_copy(i, c):
        src, dst, to = ((own.at[0, c], q1.at[c], down), (own.at[1, c], k1.at[c], up),
                        (qsel.at[c], q2.at[c], down), (ksel.at[c], k2.at[c], up))[i]
        return copy_to(src, dst, z_send.at[i, c], z_recv.at[i, c], to)

    def z_start(i, c):
        pl.when((low, top)[i % 2])(lambda: z_copy(i, c).start())

    def z_got(i, c):
        pl.when((top, low)[i % 2])(lambda: z_copy(i, c).wait_recv())

    def unpack(value, slot, c, first, second):
        row = slot * 512 + c * 128
        upper = pl.ds(pl.multiple_of(row, 64), 64)
        lower = pl.ds(pl.multiple_of(row + 64, 64), 64)
        first[upper, :] = value[:, 0:HEAD]
        second[upper, :] = value[:, HEAD : 2 * HEAD]
        first[lower, :] = value[:, 2 * HEAD : 3 * HEAD]
        second[lower, :] = value[:, 3 * HEAD : 4 * HEAD]

    def source(d):
        return lax.rem(x + d, XN)

    def got_x(t, d):
        back = XN - d
        copy_to(packed.at[t, x], own.at[t, source(d)], x_send.at[t, back - 1], x_recv.at[t, back - 1], peer[d]).wait_recv()

    def second(i, c):
        z_got(i - 2, c)
        if i == 2:
            qsel[c] = jnp.where(lq, own[2, c], q1[c])
        else:
            ksel[c] = jnp.where(rk, own[3, c], k1[c])
        z_start(i, c)

    def first(t, d):
        got_x(t, d)
        z_start(t, source(d))

    def unpack_own(t, c):
        unpack(own[t, c], *((0, c, q_out, do_out), (0, c, k_out, v_out), (3, c, q_out, do_out), (3, c, k_out, v_out))[t])

    for xp in range(XN):
        pack(0, xp)
    own[0, x] = packed[0, x]
    pl.semaphore_wait(pltpu.get_barrier_semaphore(), 3 + jnp.where(low, 1, 0) + jnp.where(top, 1, 0))
    for d in (1, 3):
        x_copy(0, d).start()
    z_start(0, x)
    for xp in range(XN):
        pack(1, xp)
    own[1, x] = packed[1, x]
    for d in (1, 3):
        x_copy(1, d).start()
    z_start(1, x)
    for t in (0, 1):
        x_copy(t, 2).start()
    for t in (2, 3):
        for xp in range(XN):
            pack(t, xp)
        own[t, x] = packed[t, x]
    second(2, x)
    second(3, x)
    unpack_own(0, x)
    unpack_own(1, x)
    first(0, 1)
    first(0, 3)
    first(1, 1)
    first(1, 3)
    for d in (1, 3):
        x_copy(2, d).start()
        x_copy(3, d).start()
    unpack_own(2, x)
    unpack_own(3, x)
    for t in (0, 1):
        unpack_own(t, source(1))
        unpack_own(t, source(3))
    first(0, 2)
    first(1, 2)
    x_copy(2, 2).start()
    x_copy(3, 2).start()
    unpack(q1[x], 1, x, q_out, do_out)
    unpack(k1[x], 1, x, k_out, v_out)
    for t in (0, 1):
        unpack_own(t, source(2))
    for d in (1, 3, 2):
        c = source(d)
        for t in (2, 3):
            got_x(t, d)
            second(t, c)
        unpack(q1[c], 1, c, q_out, do_out)
        unpack(k1[c], 1, c, k_out, v_out)
        unpack_own(2, c)
        unpack_own(3, c)
    for d in (0, 1, 3, 2):
        c = source(d)
        z_got(2, c)
        unpack(q2[c], 2, c, q_out, do_out)
        z_got(3, c)
        unpack(k2[c], 2, c, k_out, v_out)
    for t in range(4):
        for d in (1, 2, 3):
            x_copy(t, d).wait_send()
    for t in range(4):
        for c in range(XN):
            pl.when((low, top)[t % 2])(z_copy(t, c).wait_send)


def share_kernel(mine, up1, up2, down1, down2, send, recv):
    z, x, up, down, _ = place()
    upper = lax.rem(z + 2, ZN) * XN + x
    lower = lax.rem(z + ZN - 2, ZN) * XN + x
    greet([up, upper, down, lower])
    copies = []
    for i, (ref, tiles, to) in enumerate(((up1, (0, 8), down), (down1, (2, 4), up), (up2, (0, 2), lower), (down2, (4, 2), upper))):
        part = pl.ds(*tiles)
        copies.append(copy_to(mine.at[part], ref.at[part], send.at[i], recv.at[i], to))
    for copy in copies:
        copy.start()
    for copy in copies:
        copy.wait()


def scatter_kernel(len_ref, qp, kp, qhome, khome,
                   rq2, rk2, rq1, rk1, qs, ks, qfin, kfin,
                   z_send, z_recv, x_send, x_recv):
    z, x, up, down, peer = place()
    docs = Docs(len_ref)
    lk, lq = docs.case(z * 512)
    rk, rq = docs.case(z * 512 + 512)
    low, top = z >= 1, z < ZN - 1
    lm = jnp.logical_not(lk | lq) & low
    rm = jnp.logical_not(rk | rq) & top
    lq, rk = lq & low, rk & top

    def z_start(i, c):
        pl.when((top, low)[i % 2])(lambda: z_copy(i, c).start())

    def z_got(i, c):
        pl.when((low, top)[i % 2])(lambda: z_copy(i, c).wait_recv())

    def z_copy(i, c):
        src, dst, to = ((qp.at[2, c], rq2.at[c], up), (kp.at[2, c], rk2.at[c], down),
                        (qs.at[c], rq1.at[c], up), (ks.at[c], rk1.at[c], down))[i]
        return copy_to(src, dst, z_send.at[i, c], z_recv.at[i, c], to)

    def plus(a, b, use):
        return (a.astype(jnp.float32) + jnp.where(use, b.astype(jnp.float32), 0.0)).astype(jnp.bfloat16)

    def dest(d):
        return lax.rem(x + d, XN)

    def x_copy(kind, head, d):
        src, dst = ((qfin, qhome), (kfin, khome))[kind]
        i = 2 * kind + head
        return copy_to(src.at[head, dest(d)], dst.at[head, x], x_send.at[i, d - 1], x_recv.at[i, d - 1], peer[d])

    def send_home(kind, head, d, value):
        src, dst = ((qfin, qhome), (kfin, khome))[kind]
        if d:
            src[head, dest(d)] = value
            x_copy(kind, head, d).start()
        else:
            dst[head, x] = value

    order = (2, 1, 3, 0)
    meet(peer[1:])
    pl.when(low)(lambda: meet([down]))
    pl.when(top)(lambda: meet([up]))
    pl.semaphore_wait(pltpu.get_barrier_semaphore(), 3 + jnp.where(low, 1, 0) + jnp.where(top, 1, 0))
    def second(d):
        z_start(1, dest(d))
        z_start(0, dest(d))

    second(order[0])
    second(order[1])
    for n, d in enumerate(order):
        c = dest(d)
        z_got(1, c)
        if n + 2 < XN:
            second(order[n + 2])
        back = rk2[c]
        ks[c] = plus(kp[1, c], back, rm)
        z_start(3, c)
        z_got(0, c)
        fore = rq2[c]
        qs[c] = plus(qp[1, c], fore, lm)
        z_start(2, c)
        send_home(1, 0, d, plus(kp[3, c], back, rk))
        send_home(0, 1, d, plus(qp[3, c], fore, lq))
    for d in order:
        c = dest(d)
        z_got(3, c)
        send_home(1, 1, d, plus(kp[0, c], rk1[c], top))
        z_got(2, c)
        send_home(0, 0, d, plus(qp[0, c], rq1[c], low))
    for i in range(4):
        for d in (1, 2, 3):
            x_copy(i // 2, i % 2, d).wait_recv()
    for i in range(4):
        for c in range(XN):
            pl.when((top, low)[i % 2])(z_copy(i, c).wait_send)
        for d in (1, 2, 3):
            x_copy(i // 2, i % 2, d).wait_send()


def unpack_kernel(qhome, khome, dq_out, dk_out, dv_out):
    for a, out, n in ((0, dq_out, 4), (0, dk_out, 2), (1, dv_out, 2)):
        home = qhome if n == 4 else khome
        step = 128 // n
        for part in range(n):
            lanes = (part if n == 4 else 2 * part + a) * HEAD
            pieces = []
            for xs in range(XN):
                for head in range(2):
                    pieces.append(home[head, xs][:, lanes : lanes + HEAD])
            out[part * step : (part + 1) * step, :] = jnp.concatenate(pieces, axis=1)


VM = pl.BlockSpec(memory_space=pltpu.VMEM)
SM = pl.BlockSpec(memory_space=pltpu.SMEM)
LIMIT = 26 * 1024 * 1024
BIG = pltpu.CompilerParams(vmem_limit_bytes=LIMIT)
HB = pl.BlockSpec(memory_space=pltpu.HBM)
DMA = pltpu.SemaphoreType.DMA


def remote(number, limit=26):
    return pltpu.CompilerParams(vmem_limit_bytes=limit * 1024 * 1024, collective_id=number, has_side_effects=True)


def buf(*shape, dtype=jnp.bfloat16):
    return pltpu.VMEM(shape, dtype)


def out(*shape, dtype=jnp.bfloat16):
    return jax.ShapeDtypeStruct(shape, dtype)


def shards(queries, key_vectors, value_vectors, out_grad, doc_lengths):
    rows, width = queries.shape[1], queries.shape[2]
    chunk = (XN, 64, 4 * HEAD)
    small = (XN, 32, 4 * HEAD)
    block = out(2048, HEAD)
    qs, dos, ks, vs = pl.pallas_call(
        gather_kernel,
        out_shape=(block,) * 4,
        name="gather",
        in_specs=[SM, VM],
        out_specs=(VM,) * 4,
        scratch_shapes=[buf(4, *chunk), buf(4, *chunk)] + [buf(*chunk)] * 6
        + [DMA((4, 3)), DMA((4, 3)), DMA((4, 4)), DMA((4, 4))],
        compiler_params=remote(0),
    )(doc_lengths, jnp.concatenate([queries, out_grad, key_vectors, value_vectors]))
    stat = out(8, 4, TILE, dtype=jnp.float32)
    todo = pltpu.SMEM((4, 64), jnp.int32)
    mine = pl.pallas_call(
        stats_kernel,
        name="stats",
        out_shape=stat,
        in_specs=[SM] + [VM] * 4,
        out_specs=VM,
        scratch_shapes=[todo],
        compiler_params=BIG,
    )(doc_lengths, qs, dos, ks, vs)
    others = pl.pallas_call(
        share_kernel,
        name="share",
        out_shape=(stat,) * 4,
        in_specs=[VM],
        out_specs=(VM,) * 4,
        scratch_shapes=[DMA((4,)), DMA((4,))],
        compiler_params=remote(1),
    )(mine)
    qp, kp = pl.pallas_call(
        grads_kernel,
        name="grads",
        out_shape=(out(4, *small), out(4, *chunk)),
        in_specs=[SM] + [VM] * 9,
        out_specs=(VM, VM),
        scratch_shapes=[
            buf(8, 4, TILE, dtype=jnp.float32),
            todo,
            buf(8, HEAD, TILE),
            buf(8, HEAD, TILE, dtype=jnp.float32),
            buf(8, TILE, HEAD, dtype=jnp.float32),
            buf(8, TILE, HEAD, dtype=jnp.float32),
        ],
        compiler_params=BIG,
    )(doc_lengths, qs, dos, ks, vs, mine, *others)
    full = out(rows, width)
    home = pl.pallas_call(
        scatter_kernel,
        name="scatter",
        out_shape=(out(2, *small), out(2, *chunk)),
        in_specs=[SM, VM, VM],
        out_specs=(VM,) * 2,
        scratch_shapes=[buf(*small), buf(*chunk), buf(*small), buf(*chunk), buf(*small), buf(*chunk),
                        buf(2, *small), buf(2, *chunk),
                        DMA((4, 4)), DMA((4, 4)), DMA((4, 3)), DMA((4, 3))],
        compiler_params=remote(2),
    )(doc_lengths, qp, kp)
    full = out(rows, width)
    grads = pl.pallas_call(
        unpack_kernel,
        name="unpack",
        out_shape=(full,) * 3,
        in_specs=[VM, VM],
        out_specs=(VM,) * 3,
        compiler_params=BIG,
    )(*home)
    return tuple(g[None] for g in grads)


def solution(mesh):
    spec = P("section", "seq", "dp")
    return jax.shard_map(
        shards,
        mesh=mesh,
        in_specs=(spec, spec, spec, spec, P()),
        out_specs=(spec, spec, spec),
        check_vma=False,
    )
```

time: 102 us -> 88 us (0.86)
  the two profiles are of different devices: /device:TPU:56 before, /device:TPU:136 now
where the time goes in v3:
time: 88 us; the launch traced here: 87.8 us
  Pallas kernels  85.4 us (97%)
  other arithmetic  1.67 us (2%)
    pallas_call x1, Pallas kernels, shards(): pl.pallas_call(gather_kernel, out_shape=(block,) * 4, name='gather', in_s...  32.6 us
    pallas_call x1, Pallas kernels, shards(): pl.pallas_call(scatter_kernel, name='scatter', out_shape=(out(2, *small),...  32.2 us
    pallas_call x1, Pallas kernels, shards(): pl.pallas_call(share_kernel, name='share', out_shape=(stat,) * 4, in_spec...  10.1 us
    pallas_call x1, Pallas kernels, shards(): pl.pallas_call(grads_kernel, name='grads', out_shape=(out(4, *small), out...  6.06 us
    pallas_call x1, Pallas kernels, shards(): pl.pallas_call(stats_kernel, name='stats', out_shape=stat, in_specs=[SM]...  3.17 us

profile of v3, /device:TPU:136, one launch (start us, length us, event | category | flops | bytes accessed | tf_op | source)
XLA Modules:
  0.0 87.8 jit_solution(14373498132056981511)
XLA Ops:
  0.6 0.0 copy-start
  0.6 1.7 %pad_maximum_fusion.raw = bf16[4,128,1792]{2,1,0:T(8,128)(2,1)S(1)} fusion(bf16[1,128,1792]{2,1,0:T(8,128)(2,1)} %param.7, bf16[1,128,1792]{2,1,0:T(8,128)(2,1)} %param.6, bf16[1,128,1792]{2,1,0:T(8,128)(2,1)} %param.8, bf16[1,128,1792]{2,1,0:T(8,128)(2,1)} %param.5), kind=kLoop, calls=%fused_computation | loop fusion | flops 2752512 | bytes 3670016 | tf_op jit(solution)/shard_map/concatenate | solution.py:547
  2.3 0.0 copy-done
  2.3 32.6 %gather.1 = (bf16[2048,224]{1,0:T(8,128)(2,1)S(1)}, bf16[2048,224]{1,0:T(8,128)(2,1)S(1)}, bf16[2048,224]{1,0:T(8,128)(2,1)S(1)}, bf16[2048,224]{1,0:T(8,128)(2,1)S(1)}) custom-call(s32[8]{0:T(128)S(1)} %copy-done, bf16[4,128,1792]{2,1,0:T(8,128)(2,1)S(1)} %pad_maximum_fusion.raw), custom_call_target="tpu_custom_call" | custom-call | tf_op jit(solution)/shard_map/gather/pallas_call | solution.py:538
  35.0 3.2 %stats.1.mine = f32[8,4,256]{2,1,0:T(4,128)S(1)} custom-call(s32[8]{0:T(128)S(1)} %copy-done, bf16[2048,224]{1,0:T(8,128)(2,1)S(1)} %get-tuple-element.18.q_ref, bf16[2048,224]{1,0:T(8,128)(2,1)S(1)} %get-tuple-element.19.do_ref, bf16[2048,224]{1,0:T(8,128)(2,1)S(1)} %get-tuple-element.20.k_ref, bf16[2048,224]{1,0:T(8,128)(2,1)S(1)} %get-tuple-element.21.v_ref), custom_call_target="tpu_custom_call" | custom-call | tf_op jit(solution)/shard_map/stats/pallas_call | solution.py:550
  38.1 10.1 %share.1 = (f32[8,4,256]{2,1,0:T(4,128)S(1)}, f32[8,4,256]{2,1,0:T(4,128)S(1)}, f32[8,4,256]{2,1,0:T(4,128)S(1)}, f32[8,4,256]{2,1,0:T(4,128)S(1)}) custom-call(f32[8,4,256]{2,1,0:T(4,128)S(1)} %stats.1.mine), custom_call_target="tpu_custom_call" | custom-call | tf_op jit(solution)/shard_map/share/pallas_call | solution.py:559
  48.2 6.1 %grads.1 = (bf16[4,4,32,896]{3,2,1,0:T(8,128)(2,1)S(1)}, bf16[4,4,64,896]{3,2,1,0:T(8,128)(2,1)S(1)}) custom-call(s32[8]{0:T(128)S(1)} %copy-done, bf16[2048,224]{1,0:T(8,128)(2,1)S(1)} %get-tuple-element.18.q_ref, bf16[2048,224]{1,0:T(8,128)(2,1)S(1)} %get-tuple-element.19.do_ref, bf16[2048,224]{1,0:T(8,128)(2,1)S(1)} %get-tuple-element.20.k_ref, ...), custom_call_target="tpu_custom_call" | custom-call | tf_op jit(solution)/shard_map/grads/pallas_call | solution.py:568
  54.3 32.2 %scatter.1 = (bf16[2,4,32,896]{3,2,1,0:T(8,128)(2,1)S(1)}, bf16[2,4,64,896]{3,2,1,0:T(8,128)(2,1)S(1)}) custom-call(s32[8]{0:T(128)S(1)} %copy-done, bf16[4,4,32,896]{3,2,1,0:T(8,128)(2,1)S(1)} %get-tuple-element.26.qp, bf16[4,4,64,896]{3,2,1,0:T(8,128)(2,1)S(1)} %get-tuple-element.27.kp), custom_call_target="tpu_custom_call" | custom-call | tf_op jit(solution)/shard_map/scatter/pallas_call | solution.py:585
  86.5 1.3 %unpack.1 = (bf16[128,1792]{1,0:T(8,128)(2,1)}, bf16[128,1792]{1,0:T(8,128)(2,1)}, bf16[128,1792]{1,0:T(8,128)(2,1)}) custom-call(bf16[2,4,32,896]{3,2,1,0:T(8,128)(2,1)S(1)} %get-tuple-element.28.qhome, bf16[2,4,64,896]{3,2,1,0:T(8,128)(2,1)S(1)} %get-tuple-element.29.khome), custom_call_target="tpu_custom_call" | custom-call | tf_op jit(solution)/shard_map/unpack/pallas_call | solution.py:597
Async XLA Ops:
  0.6 1.7 %copy-start = (s32[8]{0:T(128)S(1)}, s32[8]{0:T(128)}, u32[]{:S(2)}) copy-start(s32[8]{0:T(128)} %len_ref.7) | copy-start | bytes 100

commit v4 on v3

--- a/solution.py
+++ b/solution.py
@@ -15,6 +15,9 @@
 TILE = 256
 GROUP = 4
 ITEMS = ((0, 3), (1, 3), (2, 3), (0, 2), (1, 2), (2, 2), (3, 0), (3, 1), (3, 2), (2, 0), (2, 1))
+
+LATE = tuple(item for item in ITEMS if 2 in item)
+OFF = tuple(item for item in ITEMS if item not in ((0, 3), (3, 0)))
 
 
 class Docs:
@@ -76,11 +79,11 @@
 NT = (((1,), (1,)), ((), ()))
 
 
-def list_tiles(docs, z, todo):
+def list_tiles(docs, z, todo, items):
     q_ids, k_ids, valid = slots(docs, z)
     firsts = [[docs.start(q_ids[qs] * 512 + qt * TILE) for qt in range(2)] for qs in range(4)]
     count = jnp.int32(0)
-    for qs, ks in ITEMS:
+    for qs, ks in items:
         qid, kid, ok = q_ids[qs], k_ids[ks], valid[(qs, ks)]
         use = (qid < ZN) & (kid >= 0) & ok
         for qt in range(2):
@@ -123,11 +126,60 @@
     return jnp.where((kpos <= qpos) & (kpos >= qstart), s * SCALE, NEG)
 
 
-def stats_kernel(len_ref, q_ref, do_ref, k_ref, v_ref, st_ref, todo):
+FAR = 1 << 20
+
+
+def diagonal_tiles(z):
+    a, b = z * 512, z * 512 + TILE
+    return [
+        (0, a, [(6, a)]),
+        (1, b, [(6, a), (7, b)]),
+        (6, a, [(0, a)]),
+        (7, b, [(0, a), (1, b)]),
+    ]
+
+
+def near_tiles(docs, z):
+    _, lq = docs.case(z * 512)
+    rk, _ = docs.case(z * 512 + 512)
+    a, b = z * 512, z * 512 + TILE
+    fore = jnp.where(jnp.logical_not(rk) & (z < ZN - 1), a, FAR)
+    back = jnp.where(jnp.logical_not(lq) & (z > 0), a - 512, FAR)
+    tiles = diagonal_tiles(z)
+    for i in (2, 3):
+        tiles[i][2].extend([(2, back), (3, back + TILE)])
+    for i in range(2):
+        tiles.append((2 + i, a + 512 + i * TILE, [(6, fore), (7, fore + TILE)]))
+    return tiles
+
+
+def near_stats(docs, z, q_ref, do_ref, k_ref, v_ref, st_ref):
+    for qi, q0, keys in near_tiles(docs, z):
+        raw = []
+        for ki, k0 in keys:
+            s = raw_scores(tile_rows(k_ref, ki), tile_rows(q_ref, qi))
+            raw.append((masked(docs, s, q0, k0), raw_scores(tile_rows(v_ref, ki), tile_rows(do_ref, qi))))
+        m = jnp.full((1, TILE), LOW, jnp.float32)
+        for s, dp in raw:
+            m = jnp.maximum(m, jnp.max(s, axis=0, keepdims=True))
+        l = jnp.zeros((1, TILE), jnp.float32)
+        d = jnp.zeros((1, TILE), jnp.float32)
+        for s, dp in raw:
+            p = jnp.exp(s - m)
+            l = l + jnp.sum(p, axis=0, keepdims=True)
+            d = d + jnp.sum(p * dp, axis=0, keepdims=True)
+        st_ref[qi, 0:1, :] = m
+        st_ref[qi, 1:2, :] = l
+        st_ref[qi, 2:3, :] = d
+    for qi in (4, 5):
+        st_ref[qi, 0:1, :] = jnp.full((1, TILE), LOW, jnp.float32)
+        st_ref[qi, 1:3, :] = jnp.zeros((2, TILE), jnp.float32)
+
+
+def stats_kernel(len_ref, q_ref, do_ref, k_ref, v_ref, near, st_ref, todo):
     z = lax.axis_index("seq") // XN
     docs = Docs(len_ref)
-    st_ref[:, 0:1, :] = jnp.full((8, 1, TILE), LOW, jnp.float32)
-    st_ref[:, 1:4, :] = jnp.zeros((8, 3, TILE), jnp.float32)
+    st_ref[...] = near[...]
 
     def body(tiles):
         raw = []
@@ -144,7 +196,7 @@
             st_ref[qi, 1:2, :] = st_ref[qi, 1:2, :] * alpha + jnp.sum(p, axis=0, keepdims=True)
             st_ref[qi, 2:3, :] = st_ref[qi, 2:3, :] * alpha + jnp.sum(p * dp, axis=0, keepdims=True)
 
-    for_groups(list_tiles(docs, z, todo), todo, body)
+    for_groups(list_tiles(docs, z, todo, LATE), todo, body)
 
 
 def combine_stats(docs, z, mine, up1, up2, down1, down2):
@@ -179,8 +231,51 @@
     return out
 
 
+def tile_grads(docs, tiles, q_ref, do_ref, k_ref, v_ref, stat, kt_ref):
+    raw = []
+    for qi, ki, q0, k0 in tiles:
+        s = raw_scores(tile_rows(k_ref, ki), tile_rows(q_ref, qi))
+        raw.append((s, raw_scores(tile_rows(v_ref, ki), tile_rows(do_ref, qi))))
+    weights = []
+    for (qi, ki, q0, k0), (s, dp) in zip(tiles, raw):
+        p = jnp.exp(masked(docs, s, q0, k0) - stat[qi, 0:1, :]) * stat[qi, 1:2, :]
+        weights.append((p.astype(jnp.bfloat16), (p * (dp - stat[qi, 2:3, :])).astype(jnp.bfloat16)))
+    terms = []
+    for (qi, ki, q0, k0), (p, ds) in zip(tiles, weights):
+        terms.append((
+            jnp.dot(p, tile_rows(do_ref, qi), preferred_element_type=jnp.float32),
+            jnp.dot(ds, tile_rows(q_ref, qi), preferred_element_type=jnp.float32),
+            jnp.dot(kt_ref[ki], ds, preferred_element_type=jnp.float32),
+        ))
+    return terms
+
+
+def pack_pair(first, second):
+    return jnp.concatenate([first[:64], second[:64], first[64:], second[64:]], axis=1)
+
+
+def pack_query(dqt, q_out, half):
+    dq = (dqt * SCALE).T.astype(jnp.bfloat16)
+    for i in range(2):
+        r = i * 128
+        q_out[2 * half + i] = jnp.concatenate([dq[r + 32 * j : r + 32 * j + 32] for j in range(4)], axis=1)
+
+
+def pack_keys(dk, dv, k_out, half):
+    dk = (dk * SCALE).astype(jnp.bfloat16)
+    dv = dv.astype(jnp.bfloat16)
+    for i in range(2):
+        r = i * 128
+        k_out[2 * half + i] = pack_pair(dk[r : r + 128], dv[r : r + 128])
+
+
+def pack_grads(dqt, dk, dv, q_out, k_out, half):
+    pack_query(dqt, q_out, half)
+    pack_keys(dk, dv, k_out, half)
+
+
 def grads_kernel(len_ref, q_ref, do_ref, k_ref, v_ref, mine, up1, up2, down1, down2,
-                 qp_ref, kp_ref, stat, todo, kt_ref, dqt, dk_acc, dv_acc):
+                 qp_ref, kp_ref, stat, dqt, dk_acc, dv_acc, todo, kt_ref):
     z = lax.axis_index("seq") // XN
     docs = Docs(len_ref)
     for qs, values in enumerate(combine_stats(docs, z, mine, up1, up2, down1, down2)):
@@ -193,35 +288,14 @@
     dv_acc[...] = jnp.zeros_like(dv_acc)
 
     def body(tiles):
-        raw = []
-        for qi, ki, q0, k0 in tiles:
-            s = raw_scores(tile_rows(k_ref, ki), tile_rows(q_ref, qi))
-            raw.append((s, raw_scores(tile_rows(v_ref, ki), tile_rows(do_ref, qi))))
-        weights = []
-        for (qi, ki, q0, k0), (s, dp) in zip(tiles, raw):
-            p = jnp.exp(masked(docs, s, q0, k0) - stat[qi, 0:1, :]) * stat[qi, 1:2, :]
-            weights.append((p.astype(jnp.bfloat16), (p * (dp - stat[qi, 2:3, :])).astype(jnp.bfloat16)))
-        terms = []
-        for (qi, ki, q0, k0), (p, ds) in zip(tiles, weights):
-            terms.append((
-                jnp.dot(p, tile_rows(do_ref, qi), preferred_element_type=jnp.float32),
-                jnp.dot(ds, tile_rows(q_ref, qi), preferred_element_type=jnp.float32),
-                jnp.dot(kt_ref[ki], ds, preferred_element_type=jnp.float32),
-            ))
-        for (qi, ki, q0, k0), (dv, dk, dq) in zip(tiles, terms):
+        for (qi, ki, q0, k0), (dv, dk, dq) in zip(tiles, tile_grads(docs, tiles, q_ref, do_ref, k_ref, v_ref, stat, kt_ref)):
             dv_acc[ki] += dv
             dk_acc[ki] += dk
             dqt[qi] += dq
 
-    for_groups(list_tiles(docs, z, todo), todo, body)
-    for i in range(8):
-        dq = (dqt[i] * SCALE).T.astype(jnp.bfloat16)
-        dk = (dk_acc[i] * SCALE).astype(jnp.bfloat16)
-        dv = dv_acc[i].astype(jnp.bfloat16)
-        for half in range(2):
-            r, c = half * 128, 2 * (i % 2) + half
-            qp_ref[i // 2, c] = jnp.concatenate([dq[r + 32 * j : r + 32 * j + 32] for j in range(4)], axis=1)
-            kp_ref[i // 2, c] = pack_pair(dk[r : r + 128], dv[r : r + 128])
+    for_groups(list_tiles(docs, z, todo, OFF), todo, body)
+    for i in range(2, 6):
+        pack_grads(dqt[i], dk_acc[i], dv_acc[i], qp_ref.at[i // 2 - 1], kp_ref.at[i // 2 - 1], i % 2)
 
 
 def copy_to(src, dst, send, recv, device):
@@ -253,10 +327,6 @@
     return ref[:, low:high][:, off - low : off - low + HEAD]
 
 
-def pack_pair(first, second):
-    return jnp.concatenate([first[:64], second[:64], first[64:], second[64:]], axis=1)
-
-
 def place():
     me = lax.axis_index("seq")
     z, x = me // XN, me % XN
@@ -269,7 +339,7 @@
 TYPES = (("q", 0), ("k", 1), ("q", 1), ("k", 0))
 
 
-def gather_kernel(len_ref, raw, q_out, do_out, k_out, v_out,
+def gather_kernel(len_ref, raw, q_out, do_out, k_out, v_out, near,
                   packed, own, q1, k1, qsel, ksel, q2, k2,
                   x_send, x_recv, z_send, z_recv):
     z, x, up, down, peer = place()
@@ -385,6 +455,17 @@
         unpack(k1[c], 1, c, k_out, v_out)
         unpack_own(2, c)
         unpack_own(3, c)
+    @pl.when(jnp.logical_not(top))
+    def _():
+        q_out[512:1024, :] = jnp.zeros((512, HEAD), jnp.bfloat16)
+        do_out[512:1024, :] = jnp.zeros((512, HEAD), jnp.bfloat16)
+
+    @pl.when(jnp.logical_not(low))
+    def _():
+        k_out[512:1024, :] = jnp.zeros((512, HEAD), jnp.bfloat16)
+        v_out[512:1024, :] = jnp.zeros((512, HEAD), jnp.bfloat16)
+
+    near_stats(docs, z, q_out, do_out, k_out, v_out, near)
     for d in (0, 1, 3, 2):
         c = source(d)
         z_got(2, c)
@@ -414,8 +495,8 @@
         copy.wait()
 
 
-def scatter_kernel(len_ref, qp, kp, qhome, khome,
-                   rq2, rk2, rq1, rk1, qs, ks, qfin, kfin,
+def scatter_kernel(len_ref, q_ref, do_ref, k_ref, v_ref, stat, dqt, dk_acc, dv_acc, qp, kp, qhome, khome,
+                   kt_ref, ownq, ownk, rq2, rk2, rq1, rk1, qs, ks, qfin, kfin,
                    z_send, z_recv, x_send, x_recv):
     z, x, up, down, peer = place()
     docs = Docs(len_ref)
@@ -433,7 +514,7 @@
         pl.when((low, top)[i % 2])(lambda: z_copy(i, c).wait_recv())
 
     def z_copy(i, c):
-        src, dst, to = ((qp.at[2, c], rq2.at[c], up), (kp.at[2, c], rk2.at[c], down),
+        src, dst, to = ((qp.at[1, c], rq2.at[c], up), (kp.at[1, c], rk2.at[c], down),
                         (qs.at[c], rq1.at[c], up), (ks.at[c], rk1.at[c], down))[i]
         return copy_to(src, dst, z_send.at[i, c], z_recv.at[i, c], to)
 
@@ -467,26 +548,39 @@
 
     second(order[0])
     second(order[1])
+    own = (0, 1, 6, 7)
+    for i in own:
+        kt_ref[i] = tile_rows(k_ref, i).T
+    for head, tiles in enumerate((diagonal_tiles(z)[:2], diagonal_tiles(z)[2:])):
+        pairs = [(qi, ki, q0, k0) for qi, q0, keys in tiles for ki, k0 in keys]
+        terms = tile_grads(docs, pairs, q_ref, do_ref, k_ref, v_ref, stat, kt_ref)
+        for half in range(2):
+            qi, ki = pairs[2 * half][0], pairs[2 * half][1]
+            dq = dqt[qi] + sum(t[2] for p, t in zip(pairs, terms) if p[0] == qi)
+            pack_query(dq, ownq.at[head], half)
+            dk = dk_acc[ki] + sum(t[1] for p, t in zip(pairs, terms) if p[1] == ki)
+            dv = dv_acc[ki] + sum(t[0] for p, t in zip(pairs, terms) if p[1] == ki)
+            pack_keys(dk, dv, ownk.at[head], half)
     for n, d in enumerate(order):
         c = dest(d)
         z_got(1, c)
         if n + 2 < XN:
             second(order[n + 2])
         back = rk2[c]
-        ks[c] = plus(kp[1, c], back, rm)
+        ks[c] = plus(kp[0, c], back, rm)
         z_start(3, c)
         z_got(0, c)
         fore = rq2[c]
-        qs[c] = plus(qp[1, c], fore, lm)
+        qs[c] = plus(qp[0, c], fore, lm)
         z_start(2, c)
-        send_home(1, 0, d, plus(kp[3, c], back, rk))
-        send_home(0, 1, d, plus(qp[3, c], fore, lq))
+        send_home(1, 0, d, plus(ownk[0, c], back, rk))
+        send_home(0, 1, d, plus(ownq[1, c], fore, lq))
     for d in order:
         c = dest(d)
         z_got(3, c)
-        send_home(1, 1, d, plus(kp[0, c], rk1[c], top))
+        send_home(1, 1, d, plus(ownk[1, c], rk1[c], top))
         z_got(2, c)
-        send_home(0, 0, d, plus(qp[0, c], rq1[c], low))
+        send_home(0, 0, d, plus(ownq[0, c], rq1[c], low))
     for i in range(4):
         for d in (1, 2, 3):
             x_copy(i // 2, i % 2, d).wait_recv()
@@ -535,27 +629,27 @@
     chunk = (XN, 64, 4 * HEAD)
     small = (XN, 32, 4 * HEAD)
     block = out(2048, HEAD)
-    qs, dos, ks, vs = pl.pallas_call(
+    stat = out(8, 4, TILE, dtype=jnp.float32)
+    todo = pltpu.SMEM((4, 64), jnp.int32)
+    qs, dos, ks, vs, near = pl.pallas_call(
         gather_kernel,
-        out_shape=(block,) * 4,
+        out_shape=(block,) * 4 + (stat,),
         name="gather",
         in_specs=[SM, VM],
-        out_specs=(VM,) * 4,
+        out_specs=(VM,) * 5,
         scratch_shapes=[buf(4, *chunk), buf(4, *chunk)] + [buf(*chunk)] * 6
         + [DMA((4, 3)), DMA((4, 3)), DMA((4, 4)), DMA((4, 4))],
         compiler_params=remote(0),
     )(doc_lengths, jnp.concatenate([queries, out_grad, key_vectors, value_vectors]))
-    stat = out(8, 4, TILE, dtype=jnp.float32)
-    todo = pltpu.SMEM((4, 64), jnp.int32)
     mine = pl.pallas_call(
         stats_kernel,
         name="stats",
         out_shape=stat,
-        in_specs=[SM] + [VM] * 4,
+        in_specs=[SM] + [VM] * 5,
         out_specs=VM,
         scratch_shapes=[todo],
         compiler_params=BIG,
-    )(doc_lengths, qs, dos, ks, vs)
+    )(doc_lengths, qs, dos, ks, vs, near)
     others = pl.pallas_call(
         share_kernel,
         name="share",
@@ -565,34 +659,28 @@
         scratch_shapes=[DMA((4,)), DMA((4,))],
         compiler_params=remote(1),
     )(mine)
-    qp, kp = pl.pallas_call(
+    acc = out(8, TILE, HEAD, dtype=jnp.float32)
+    qp, kp, *partial = pl.pallas_call(
         grads_kernel,
         name="grads",
-        out_shape=(out(4, *small), out(4, *chunk)),
+        out_shape=(out(2, *small), out(2, *chunk), stat, out(8, HEAD, TILE, dtype=jnp.float32), acc, acc),
         in_specs=[SM] + [VM] * 9,
-        out_specs=(VM, VM),
-        scratch_shapes=[
-            buf(8, 4, TILE, dtype=jnp.float32),
-            todo,
-            buf(8, HEAD, TILE),
-            buf(8, HEAD, TILE, dtype=jnp.float32),
-            buf(8, TILE, HEAD, dtype=jnp.float32),
-            buf(8, TILE, HEAD, dtype=jnp.float32),
-        ],
+        out_specs=(VM,) * 6,
+        scratch_shapes=[todo, buf(8, HEAD, TILE)],
         compiler_params=BIG,
     )(doc_lengths, qs, dos, ks, vs, mine, *others)
-    full = out(rows, width)
     home = pl.pallas_call(
         scatter_kernel,
         name="scatter",
         out_shape=(out(2, *small), out(2, *chunk)),
-        in_specs=[SM, VM, VM],
+        in_specs=[SM] + [VM] * 10,
         out_specs=(VM,) * 2,
-        scratch_shapes=[buf(*small), buf(*chunk), buf(*small), buf(*chunk), buf(*small), buf(*chunk),
+        scratch_shapes=[buf(8, HEAD, TILE), buf(2, *small), buf(2, *chunk),
+                        buf(*small), buf(*chunk), buf(*small), buf(*chunk), buf(*small), buf(*chunk),
                         buf(2, *small), buf(2, *chunk),
                         DMA((4, 4)), DMA((4, 4)), DMA((4, 3)), DMA((4, 3))],
         compiler_params=remote(2),
-    )(doc_lengths, qp, kp)
+    )(doc_lengths, qs, dos, ks, vs, *partial, qp, kp)
     full = out(rows, width)
     grads = pl.pallas_call(
         unpack_kernel,

time: 88 us -> 82.1 us (0.933)
  the two profiles are of different devices: /device:TPU:136 before, /device:TPU:168 now
where the time goes in v4:
time: 82.1 us; the launch traced here: 81.9 us
  Pallas kernels  79.6 us (97%)
  other arithmetic  1.67 us (2%)
    pallas_call x1, Pallas kernels, shards(): pl.pallas_call(gather_kernel, out_shape=(block,) * 4 + (stat,), name='gat...  32.6 us
    pallas_call x1, Pallas kernels, shards(): pl.pallas_call(scatter_kernel, name='scatter', out_shape=(out(2, *small),...  32.2 us
    pallas_call x1, Pallas kernels, shards(): pl.pallas_call(share_kernel, name='share', out_shape=(stat,) * 4, in_spec...  9.45 us
    pallas_call x1, Pallas kernels, shards(): pl.pallas_call(grads_kernel, name='grads', out_shape=(out(2, *small), out...  3.2 us
    concatenate x1, other arithmetic, shards(): jnp.concatenate([queries, out_grad, key_vectors, value_vectors])  1.67 us

profile of v4, /device:TPU:168, one launch (start us, length us, event | category | flops | bytes accessed | tf_op | source)
XLA Modules:
  0.0 81.9 jit_solution(16642491904863889957)
XLA Ops:
  0.6 0.0 copy-start
  0.6 1.7 %pad_maximum_fusion.raw = bf16[4,128,1792]{2,1,0:T(8,128)(2,1)S(1)} fusion(bf16[1,128,1792]{2,1,0:T(8,128)(2,1)} %param.7, bf16[1,128,1792]{2,1,0:T(8,128)(2,1)} %param.6, bf16[1,128,1792]{2,1,0:T(8,128)(2,1)} %param.8, bf16[1,128,1792]{2,1,0:T(8,128)(2,1)} %param.5), kind=kLoop, calls=%fused_computation | loop fusion | flops 2752512 | bytes 3670016 | tf_op jit(solution)/shard_map/concatenate | solution.py:643
  2.3 0.0 copy-done
  2.3 32.6 %gather.1 = (bf16[2048,224]{1,0:T(8,128)(2,1)S(1)}, bf16[2048,224]{1,0:T(8,128)(2,1)S(1)}, bf16[2048,224]{1,0:T(8,128)(2,1)S(1)}, bf16[2048,224]{1,0:T(8,128)(2,1)S(1)}, f32[8,4,256]{2,1,0:T(4,128)S(1)}) custom-call(s32[8]{0:T(128)S(1)} %copy-done, bf16[4,128,1792]{2,1,0:T(8,128)(2,1)S(1)} %pad_maximum_fusion.raw), custom_call_target="tpu_custom_call" | custom-call | tf_op jit(solution)/shard_map/gather/pallas_call | solution.py:634
  35.0 0.8 %stats.1.mine = f32[8,4,256]{2,1,0:T(4,128)S(1)} custom-call(s32[8]{0:T(128)S(1)} %copy-done, bf16[2048,224]{1,0:T(8,128)(2,1)S(1)} %get-tuple-element.23.q_ref, bf16[2048,224]{1,0:T(8,128)(2,1)S(1)} %get-tuple-element.24.do_ref, bf16[2048,224]{1,0:T(8,128)(2,1)S(1)} %get-tuple-element.25.k_ref, bf16[2048,224]{1,0:T(8,128)(2,1)S(1)} %get-tuple-element.26.v_ref, ...), custom_call_target="tpu_custom_call" | custom-call | tf_op jit(solution)/shard_map/stats/pallas_call | solution.py:644
  35.8 9.5 %share.1 = (f32[8,4,256]{2,1,0:T(4,128)S(1)}, f32[8,4,256]{2,1,0:T(4,128)S(1)}, f32[8,4,256]{2,1,0:T(4,128)S(1)}, f32[8,4,256]{2,1,0:T(4,128)S(1)}) custom-call(f32[8,4,256]{2,1,0:T(4,128)S(1)} %stats.1.mine), custom_call_target="tpu_custom_call" | custom-call | tf_op jit(solution)/shard_map/share/pallas_call | solution.py:653
  45.3 3.2 %grads.1 = (bf16[2,4,32,896]{3,2,1,0:T(8,128)(2,1)S(1)}, bf16[2,4,64,896]{3,2,1,0:T(8,128)(2,1)S(1)}, f32[8,4,256]{2,1,0:T(4,128)S(1)}, f32[8,224,256]{2,1,0:T(8...) custom-call(s32[8]{0:T(128)S(1)} %copy-done, bf16[2048,224]{1,0:T(8,128)(2,1)S(1)} %get-tuple-element.23.q_ref, ...), custom_call_target="tpu_custom_call" | custom-call | tf_op jit(solution)/shard_map/grads/pallas_call | solution.py:663
  48.5 32.2 %scatter.1 = (bf16[2,4,32,896]{3,2,1,0:T(8,128)(2,1)S(1)}, bf16[2,4,64,896]{3,2,1,0:T(8,128)(2,1)S(1)}) custom-call(s32[8]{0:T(128)S(1)} %copy-done, bf16[2048,224]{1,0:T(8,128)(2,1)S(1)} %get-tuple-element.23.q_ref, bf16[2048,224]{1,0:T(8,128)(2,1)S(1)} %get-tuple-element.24.do_ref, bf16[2048,224]{1,0:T(8,128)(2,1)S(1)} %get-tuple-element.25.k_ref, ...), custom_call_target="tpu_custom_call" | custom-call | tf_op jit(solution)/shard_map/scatter/pallas_call | solution.py:672
  80.7 1.3 %unpack.1 = (bf16[128,1792]{1,0:T(8,128)(2,1)}, bf16[128,1792]{1,0:T(8,128)(2,1)}, bf16[128,1792]{1,0:T(8,128)(2,1)}) custom-call(bf16[2,4,32,896]{3,2,1,0:T(8,128)(2,1)S(1)} %get-tuple-element.38.qhome, bf16[2,4,64,896]{3,2,1,0:T(8,128)(2,1)S(1)} %get-tuple-element.39.khome), custom_call_target="tpu_custom_call" | custom-call | tf_op jit(solution)/shard_map/unpack/pallas_call | solution.py:685
Async XLA Ops:
  0.6 1.7 %copy-start = (s32[8]{0:T(128)S(1)}, s32[8]{0:T(128)}, u32[]{:S(2)}) copy-start(s32[8]{0:T(128)} %len_ref.7) | copy-start | bytes 100

commit v5 on v4

--- a/solution.py
+++ b/solution.py
@@ -17,7 +17,6 @@
 ITEMS = ((0, 3), (1, 3), (2, 3), (0, 2), (1, 2), (2, 2), (3, 0), (3, 1), (3, 2), (2, 0), (2, 1))
 
 LATE = tuple(item for item in ITEMS if 2 in item)
-OFF = tuple(item for item in ITEMS if item not in ((0, 3), (3, 0)))
 
 
 class Docs:
@@ -269,11 +268,6 @@
         k_out[2 * half + i] = pack_pair(dk[r : r + 128], dv[r : r + 128])
 
 
-def pack_grads(dqt, dk, dv, q_out, k_out, half):
-    pack_query(dqt, q_out, half)
-    pack_keys(dk, dv, k_out, half)
-
-
 def grads_kernel(len_ref, q_ref, do_ref, k_ref, v_ref, mine, up1, up2, down1, down2,
                  qp_ref, kp_ref, stat, dqt, dk_acc, dv_acc, todo, kt_ref):
     z = lax.axis_index("seq") // XN
@@ -293,9 +287,10 @@
             dk_acc[ki] += dk
             dqt[qi] += dq
 
-    for_groups(list_tiles(docs, z, todo, OFF), todo, body)
-    for i in range(2, 6):
-        pack_grads(dqt[i], dk_acc[i], dv_acc[i], qp_ref.at[i // 2 - 1], kp_ref.at[i // 2 - 1], i % 2)
+    for_groups(list_tiles(docs, z, todo, LATE), todo, body)
+    for half in range(2):
+        pack_query(dqt[4 + half], qp_ref, half)
+        pack_keys(dk_acc[4 + half], dv_acc[4 + half], kp_ref, half)
 
 
 def copy_to(src, dst, send, recv, device):
@@ -496,7 +491,7 @@
 
 
 def scatter_kernel(len_ref, q_ref, do_ref, k_ref, v_ref, stat, dqt, dk_acc, dv_acc, qp, kp, qhome, khome,
-                   kt_ref, ownq, ownk, rq2, rk2, rq1, rk1, qs, ks, qfin, kfin,
+                   kt_ref, ownq, ownk, q1p, k1p, rq2, rk2, rq1, rk1, qs, ks, qfin, kfin,
                    z_send, z_recv, x_send, x_recv):
     z, x, up, down, peer = place()
     docs = Docs(len_ref)
@@ -514,7 +509,7 @@
         pl.when((low, top)[i % 2])(lambda: z_copy(i, c).wait_recv())
 
     def z_copy(i, c):
-        src, dst, to = ((qp.at[1, c], rq2.at[c], up), (kp.at[1, c], rk2.at[c], down),
+        src, dst, to = ((qp.at[c], rq2.at[c], up), (kp.at[c], rk2.at[c], down),
                         (qs.at[c], rq1.at[c], up), (ks.at[c], rk1.at[c], down))[i]
         return copy_to(src, dst, z_send.at[i, c], z_recv.at[i, c], to)
 
@@ -546,41 +541,54 @@
         z_start(1, dest(d))
         z_start(0, dest(d))
 
-    second(order[0])
-    second(order[1])
-    own = (0, 1, 6, 7)
-    for i in own:
-        kt_ref[i] = tile_rows(k_ref, i).T
-    for head, tiles in enumerate((diagonal_tiles(z)[:2], diagonal_tiles(z)[2:])):
+    for d in order:
+        z_start(1, dest(d))
+    for d in order:
+        z_start(0, dest(d))
+
+    def near_grads(head):
+        tiles = [tile for tile in near_tiles(docs, z) if (tile[0] >= 6) == bool(head)]
+        for ki in (range(4), (6, 7))[1 - head]:
+            kt_ref[ki] = tile_rows(k_ref, ki).T
         pairs = [(qi, ki, q0, k0) for qi, q0, keys in tiles for ki, k0 in keys]
         terms = tile_grads(docs, pairs, q_ref, do_ref, k_ref, v_ref, stat, kt_ref)
-        for half in range(2):
-            qi, ki = pairs[2 * half][0], pairs[2 * half][1]
+        for qi in sorted({p[0] for p in pairs}):
             dq = dqt[qi] + sum(t[2] for p, t in zip(pairs, terms) if p[0] == qi)
-            pack_query(dq, ownq.at[head], half)
+            pack_query(dq, (ownq.at[0], q1p, None, ownq.at[1])[qi // 2], qi % 2)
+        for ki in sorted({p[1] for p in pairs}):
             dk = dk_acc[ki] + sum(t[1] for p, t in zip(pairs, terms) if p[1] == ki)
             dv = dv_acc[ki] + sum(t[0] for p, t in zip(pairs, terms) if p[1] == ki)
-            pack_keys(dk, dv, ownk.at[head], half)
+            pack_keys(dk, dv, (ownk.at[1], k1p, None, ownk.at[0])[ki // 2], ki % 2)
+
+    def key_home(d):
+        c = dest(d)
+        z_got(1, c)
+        send_home(1, 0, d, plus(ownk[0, c], rk2[c], rk))
+
+    near_grads(0)
+    for d in order:
+        c = dest(d)
+        z_got(0, c)
+        qs[c] = plus(q1p[c], rq2[c], lm)
+        z_start(2, c)
+    key_home(order[0])
+    key_home(order[1])
+    near_grads(1)
     for n, d in enumerate(order):
         c = dest(d)
-        z_got(1, c)
-        if n + 2 < XN:
-            second(order[n + 2])
-        back = rk2[c]
-        ks[c] = plus(kp[0, c], back, rm)
+        if n >= 2:
+            key_home(d)
+        ks[c] = plus(k1p[c], rk2[c], rm)
         z_start(3, c)
-        z_got(0, c)
-        fore = rq2[c]
-        qs[c] = plus(qp[0, c], fore, lm)
-        z_start(2, c)
-        send_home(1, 0, d, plus(ownk[0, c], back, rk))
-        send_home(0, 1, d, plus(ownq[1, c], fore, lq))
+        send_home(0, 1, d, plus(ownq[1, c], rq2[c], lq))
+    for d in order:
+        c = dest(d)
+        z_got(2, c)
+        send_home(0, 0, d, plus(ownq[0, c], rq1[c], low))
     for d in order:
         c = dest(d)
         z_got(3, c)
         send_home(1, 1, d, plus(ownk[1, c], rk1[c], top))
-        z_got(2, c)
-        send_home(0, 0, d, plus(ownq[0, c], rq1[c], low))
     for i in range(4):
         for d in (1, 2, 3):
             x_copy(i // 2, i % 2, d).wait_recv()
@@ -663,7 +671,7 @@
     qp, kp, *partial = pl.pallas_call(
         grads_kernel,
         name="grads",
-        out_shape=(out(2, *small), out(2, *chunk), stat, out(8, HEAD, TILE, dtype=jnp.float32), acc, acc),
+        out_shape=(out(*small), out(*chunk), stat, out(8, HEAD, TILE, dtype=jnp.float32), acc, acc),
         in_specs=[SM] + [VM] * 9,
         out_specs=(VM,) * 6,
         scratch_shapes=[todo, buf(8, HEAD, TILE)],
@@ -675,7 +683,7 @@
         out_shape=(out(2, *small), out(2, *chunk)),
         in_specs=[SM] + [VM] * 10,
         out_specs=(VM,) * 2,
-        scratch_shapes=[buf(8, HEAD, TILE), buf(2, *small), buf(2, *chunk),
+        scratch_shapes=[buf(8, HEAD, TILE), buf(2, *small), buf(2, *chunk), buf(*small), buf(*chunk),
                         buf(*small), buf(*chunk), buf(*small), buf(*chunk), buf(*small), buf(*chunk),
                         buf(2, *small), buf(2, *chunk),
                         DMA((4, 4)), DMA((4, 4)), DMA((4, 3)), DMA((4, 3))],

time: 82.1 us -> 78.6 us (0.957)
  the two profiles are of different devices: /device:TPU:168 before, /device:TPU:56 now
where the time goes in v5:
time: 78.6 us; the launch traced here: 78 us
  Pallas kernels  75.7 us (96%)
  other arithmetic  1.67 us (2%)
    pallas_call x1, Pallas kernels, shards(): pl.pallas_call(gather_kernel, out_shape=(block,) * 4 + (stat,), name='gat...  31.4 us
    pallas_call x1, Pallas kernels, shards(): pl.pallas_call(scatter_kernel, name='scatter', out_shape=(out(2, *small),...  26.1 us
    pallas_call x1, Pallas kernels, shards(): pl.pallas_call(share_kernel, name='share', out_shape=(stat,) * 4, in_spec...  14.3 us
    pallas_call x1, Pallas kernels, shards(): pl.pallas_call(grads_kernel, name='grads', out_shape=(out(*small), out(*c...  1.75 us
    concatenate x1, other arithmetic, shards(): jnp.concatenate([queries, out_grad, key_vectors, value_vectors])  1.67 us

profile of v5, /device:TPU:56, one launch (start us, length us, event | category | flops | bytes accessed | tf_op | source)
XLA Modules:
  0.0 78.0 jit_solution(1256768856735307578)
XLA Ops:
  0.6 0.0 copy-start
  0.6 1.7 %pad_maximum_fusion.raw = bf16[4,128,1792]{2,1,0:T(8,128)(2,1)S(1)} fusion(bf16[1,128,1792]{2,1,0:T(8,128)(2,1)} %param.7, bf16[1,128,1792]{2,1,0:T(8,128)(2,1)} %param.6, bf16[1,128,1792]{2,1,0:T(8,128)(2,1)} %param.8, bf16[1,128,1792]{2,1,0:T(8,128)(2,1)} %param.5), kind=kLoop, calls=%fused_computation | loop fusion | flops 2752512 | bytes 3670016 | tf_op jit(solution)/shard_map/concatenate | solution.py:651
  2.3 0.0 copy-done
  2.3 31.4 %gather.1 = (bf16[2048,224]{1,0:T(8,128)(2,1)S(1)}, bf16[2048,224]{1,0:T(8,128)(2,1)S(1)}, bf16[2048,224]{1,0:T(8,128)(2,1)S(1)}, bf16[2048,224]{1,0:T(8,128)(2,1)S(1)}, f32[8,4,256]{2,1,0:T(4,128)S(1)}) custom-call(s32[8]{0:T(128)S(1)} %copy-done, bf16[4,128,1792]{2,1,0:T(8,128)(2,1)S(1)} %pad_maximum_fusion.raw), custom_call_target="tpu_custom_call" | custom-call | tf_op jit(solution)/shard_map/gather/pallas_call | solution.py:642
  33.7 0.8 %stats.1.mine = f32[8,4,256]{2,1,0:T(4,128)S(1)} custom-call(s32[8]{0:T(128)S(1)} %copy-done, bf16[2048,224]{1,0:T(8,128)(2,1)S(1)} %get-tuple-element.23.q_ref, bf16[2048,224]{1,0:T(8,128)(2,1)S(1)} %get-tuple-element.24.do_ref, bf16[2048,224]{1,0:T(8,128)(2,1)S(1)} %get-tuple-element.25.k_ref, bf16[2048,224]{1,0:T(8,128)(2,1)S(1)} %get-tuple-element.26.v_ref, ...), custom_call_target="tpu_custom_call" | custom-call | tf_op jit(solution)/shard_map/stats/pallas_call | solution.py:652
  34.6 14.3 %share.1 = (f32[8,4,256]{2,1,0:T(4,128)S(1)}, f32[8,4,256]{2,1,0:T(4,128)S(1)}, f32[8,4,256]{2,1,0:T(4,128)S(1)}, f32[8,4,256]{2,1,0:T(4,128)S(1)}) custom-call(f32[8,4,256]{2,1,0:T(4,128)S(1)} %stats.1.mine), custom_call_target="tpu_custom_call" | custom-call | tf_op jit(solution)/shard_map/share/pallas_call | solution.py:661
  48.9 1.8 %grads.1 = (bf16[4,32,896]{2,1,0:T(8,128)(2,1)S(1)}, bf16[4,64,896]{2,1,0:T(8,128)(2,1)S(1)}, f32[8,4,256]{2,1,0:T(4,128)S(1)}, f32[8,224,256]{2,1,0:T(8,128)S(1...) custom-call(s32[8]{0:T(128)S(1)} %copy-done, bf16[2048,224]{1,0:T(8,128)(2,1)S(1)} %get-tuple-element.23.q_ref, ...), custom_call_target="tpu_custom_call" | custom-call | tf_op jit(solution)/shard_map/grads/pallas_call | solution.py:671
  50.7 26.1 %scatter.1 = (bf16[2,4,32,896]{3,2,1,0:T(8,128)(2,1)S(1)}, bf16[2,4,64,896]{3,2,1,0:T(8,128)(2,1)S(1)}) custom-call(s32[8]{0:T(128)S(1)} %copy-done, bf16[2048,224]{1,0:T(8,128)(2,1)S(1)} %get-tuple-element.23.q_ref, bf16[2048,224]{1,0:T(8,128)(2,1)S(1)} %get-tuple-element.24.do_ref, bf16[2048,224]{1,0:T(8,128)(2,1)S(1)} %get-tuple-element.25.k_ref, ...), custom_call_target="tpu_custom_call" | custom-call | tf_op jit(solution)/shard_map/scatter/pallas_call | solution.py:680
  76.7 1.3 %unpack.1 = (bf16[128,1792]{1,0:T(8,128)(2,1)}, bf16[128,1792]{1,0:T(8,128)(2,1)}, bf16[128,1792]{1,0:T(8,128)(2,1)}) custom-call(bf16[2,4,32,896]{3,2,1,0:T(8,128)(2,1)S(1)} %get-tuple-element.38.qhome, bf16[2,4,64,896]{3,2,1,0:T(8,128)(2,1)S(1)} %get-tuple-element.39.khome), custom_call_target="tpu_custom_call" | custom-call | tf_op jit(solution)/shard_map/unpack/pallas_call | solution.py:693
Async XLA Ops:
  0.6 1.7 %copy-start = (s32[8]{0:T(128)S(1)}, s32[8]{0:T(128)}, u32[]{:S(2)}) copy-start(s32[8]{0:T(128)} %len_ref.7) | copy-start | bytes 100

commit v6 on v5

--- a/solution.py
+++ b/solution.py
@@ -1,4 +1,5 @@
 import functools
+import math
 
 import jax
 import jax.numpy as jnp
@@ -11,6 +12,7 @@
 ZN, XN = 8, 4
 SCALE = HEAD ** (-0.5)
 NEG = -1e30
+LOG2E = math.log2(math.e)
 LOW = -1e20
 TILE = 256
 GROUP = 4
@@ -100,7 +102,7 @@
         todo[0, count + i] = 0
         todo[1, count + i] = 0
         todo[2, count + i] = 0
-        todo[3, count + i] = 1 << 20
+        todo[3, count + i] = -(1 << 20)
     return count
 
 
@@ -119,13 +121,15 @@
 
 
 def masked(docs, s, q0, k0):
-    kpos = k0 + lax.broadcasted_iota(jnp.int32, (TILE, 1), 0)
+    row = lax.broadcasted_iota(jnp.int32, (TILE, TILE), 0)
     qpos = q0 + lax.broadcasted_iota(jnp.int32, (1, TILE), 1)
-    qstart = docs.row_start(qpos)
-    return jnp.where((kpos <= qpos) & (kpos >= qstart), s * SCALE, NEG)
-
-
-FAR = 1 << 20
+    allowed = row >= docs.row_start(qpos) - k0
+    if q0 is k0:
+        allowed = allowed & (row <= lax.broadcasted_iota(jnp.int32, (1, TILE), 1))
+    return jnp.where(allowed, s * (SCALE * LOG2E), NEG)
+
+
+FAR = -(1 << 20)
 
 
 def diagonal_tiles(z):
@@ -152,50 +156,71 @@
     return tiles
 
 
+def part_stats(docs, q, do, q0, keys):
+    raw = [(masked(docs, raw_scores(k, q), q0, k0), raw_scores(v, do)) for k, v, k0 in keys]
+    m = jnp.full((1, TILE), LOW, jnp.float32)
+    for s, dp in raw:
+        m = jnp.maximum(m, jnp.max(s, axis=0, keepdims=True))
+    l = jnp.zeros((1, TILE), jnp.float32)
+    d = jnp.zeros((1, TILE), jnp.float32)
+    for s, dp in raw:
+        p = jnp.exp2(s - m)
+        l = l + jnp.sum(p, axis=0, keepdims=True)
+        d = d + jnp.sum(p * dp, axis=0, keepdims=True)
+    return m, l, d
+
+
+def put_stats(st_ref, qi, values):
+    for r, value in enumerate(values):
+        st_ref[qi, r : r + 1, :] = value
+
+
+def add_stats(st_ref, qi, part, use):
+    old = [st_ref[qi, r : r + 1, :] for r in range(3)]
+    m = jnp.maximum(old[0], jnp.where(use, part[0], LOW))
+    a, b = jnp.exp2(old[0] - m), jnp.where(use, jnp.exp2(part[0] - m), 0.0)
+    put_stats(st_ref, qi, (m, old[1] * a + part[1] * b, old[2] * a + part[2] * b))
+
+
 def near_stats(docs, z, q_ref, do_ref, k_ref, v_ref, st_ref):
     for qi, q0, keys in near_tiles(docs, z):
-        raw = []
-        for ki, k0 in keys:
-            s = raw_scores(tile_rows(k_ref, ki), tile_rows(q_ref, qi))
-            raw.append((masked(docs, s, q0, k0), raw_scores(tile_rows(v_ref, ki), tile_rows(do_ref, qi))))
-        m = jnp.full((1, TILE), LOW, jnp.float32)
-        for s, dp in raw:
-            m = jnp.maximum(m, jnp.max(s, axis=0, keepdims=True))
-        l = jnp.zeros((1, TILE), jnp.float32)
-        d = jnp.zeros((1, TILE), jnp.float32)
-        for s, dp in raw:
-            p = jnp.exp(s - m)
-            l = l + jnp.sum(p, axis=0, keepdims=True)
-            d = d + jnp.sum(p * dp, axis=0, keepdims=True)
-        st_ref[qi, 0:1, :] = m
-        st_ref[qi, 1:2, :] = l
-        st_ref[qi, 2:3, :] = d
-    for qi in (4, 5):
-        st_ref[qi, 0:1, :] = jnp.full((1, TILE), LOW, jnp.float32)
-        st_ref[qi, 1:3, :] = jnp.zeros((2, TILE), jnp.float32)
-
-
-def stats_kernel(len_ref, q_ref, do_ref, k_ref, v_ref, near, st_ref, todo):
-    z = lax.axis_index("seq") // XN
-    docs = Docs(len_ref)
-    st_ref[...] = near[...]
-
-    def body(tiles):
-        raw = []
-        for qi, ki, q0, k0 in tiles:
-            s = raw_scores(tile_rows(k_ref, ki), tile_rows(q_ref, qi))
-            raw.append((s, raw_scores(tile_rows(v_ref, ki), tile_rows(do_ref, qi))))
-        for (qi, ki, q0, k0), (s, dp) in zip(tiles, raw):
-            s = masked(docs, s, q0, k0)
-            old = st_ref[qi, 0:1, :]
-            new = jnp.maximum(old, jnp.max(s, axis=0, keepdims=True))
-            p = jnp.exp(s - new)
-            alpha = jnp.exp(old - new)
-            st_ref[qi, 0:1, :] = new
-            st_ref[qi, 1:2, :] = st_ref[qi, 1:2, :] * alpha + jnp.sum(p, axis=0, keepdims=True)
-            st_ref[qi, 2:3, :] = st_ref[qi, 2:3, :] * alpha + jnp.sum(p * dp, axis=0, keepdims=True)
-
-    for_groups(list_tiles(docs, z, todo, LATE), todo, body)
+        tiles = [(tile_rows(k_ref, ki), tile_rows(v_ref, ki), k0) for ki, k0 in keys]
+        put_stats(st_ref, qi, part_stats(docs, tile_rows(q_ref, qi), tile_rows(do_ref, qi), q0, tiles))
+
+
+def late_stats(docs, z, q_ref, do_ref, k_ref, v_ref, st_ref):
+    lk, lq = docs.case(z * 512)
+    rk, rq = docs.case(z * 512 + 512)
+    lm, rm = jnp.logical_not(lk | lq), jnp.logical_not(rk | rq)
+    q_ids, k_ids, _ = slots(docs, z)
+    here, q2, k2 = z * 512, q_ids[2] * 512, k_ids[2] * 512
+    q_ok, k_ok = q_ids[2] < ZN, k_ids[2] >= 0
+
+    def start(use, pos, j):
+        return jnp.where(use, pos, FAR) + j * TILE
+
+    def pick(ref, use, one, other):
+        return jnp.where(use, tile_rows(ref, one), tile_rows(ref, other))
+
+    own = jnp.logical_not(rk) & q_ok
+    both = ((lk & rm) | (rq & lm)) & q_ok & k_ok
+    cross = (lk & jnp.logical_not(rk) & (z < ZN - 1) & k_ok) | (rq & jnp.logical_not(lq) & (z > 0) & q_ok)
+    for i in range(2):
+        keys = [(pick(k_ref, rq, j, 6 + j), pick(v_ref, rq, j, 6 + j), start(own, here, j)) for j in range(2)]
+        keys += [(tile_rows(k_ref, 4 + j), tile_rows(v_ref, 4 + j), start(both, k2, j)) for j in range(2)]
+        put_stats(st_ref, 4 + i, part_stats(docs, tile_rows(q_ref, 4 + i), tile_rows(do_ref, 4 + i), q2 + i * TILE, keys))
+    for i in range(2):
+        keys = [(tile_rows(k_ref, 4 + j), tile_rows(v_ref, 4 + j), start(jnp.logical_not(lq) & k_ok, k2, j)) for j in range(2)]
+        part = part_stats(docs, pick(q_ref, lk, i, 6 + i), pick(do_ref, lk, i, 6 + i), here + i * TILE, keys)
+        add_stats(st_ref, i, part, lk)
+        add_stats(st_ref, 6 + i, part, lm)
+    for i in range(2):
+        keys = [(pick(k_ref, lk, 4 + j, 2 + j), pick(v_ref, lk, 4 + j, 2 + j), start(cross, jnp.where(lk, k2, here - 512), j))
+                for j in range(2)]
+        part = part_stats(docs, pick(q_ref, lk, 2 + i, 4 + i), pick(do_ref, lk, 2 + i, 4 + i),
+                          jnp.where(lk, here + 512, q2) + i * TILE, keys)
+        add_stats(st_ref, 2 + i, part, lk)
+        add_stats(st_ref, 4 + i, part, jnp.logical_not(lk))
 
 
 def combine_stats(docs, z, mine, up1, up2, down1, down2):
@@ -223,10 +248,11 @@
     out = []
     for parts in groups:
         m = functools.reduce(jnp.maximum, [p[0] for p in parts])
-        l = sum(p[1] * jnp.exp(p[0] - m) for p in parts)
-        d = sum(p[2] * jnp.exp(p[0] - m) for p in parts)
-        inv = jnp.where(l > 0.0, 1.0 / jnp.where(l > 0.0, l, 1.0), 0.0)
-        out.append((m, inv, d * inv))
+        l = sum(p[1] * jnp.exp2(p[0] - m) for p in parts)
+        d = sum(p[2] * jnp.exp2(p[0] - m) for p in parts)
+        some = l > 0.0
+        l = jnp.where(some, l, 1.0)
+        out.append((jnp.where(some, m + jnp.log2(l), -NEG), d / l))
     return out
 
 
@@ -237,8 +263,8 @@
         raw.append((s, raw_scores(tile_rows(v_ref, ki), tile_rows(do_ref, qi))))
     weights = []
     for (qi, ki, q0, k0), (s, dp) in zip(tiles, raw):
-        p = jnp.exp(masked(docs, s, q0, k0) - stat[qi, 0:1, :]) * stat[qi, 1:2, :]
-        weights.append((p.astype(jnp.bfloat16), (p * (dp - stat[qi, 2:3, :])).astype(jnp.bfloat16)))
+        p = jnp.exp2(masked(docs, s, q0, k0) - stat[qi, 0:1, :])
+        weights.append((p.astype(jnp.bfloat16), (p * (dp - stat[qi, 1:2, :])).astype(jnp.bfloat16)))
     terms = []
     for (qi, ki, q0, k0), (p, ds) in zip(tiles, weights):
         terms.append((
@@ -268,13 +294,9 @@
         k_out[2 * half + i] = pack_pair(dk[r : r + 128], dv[r : r + 128])
 
 
-def grads_kernel(len_ref, q_ref, do_ref, k_ref, v_ref, mine, up1, up2, down1, down2,
-                 qp_ref, kp_ref, stat, dqt, dk_acc, dv_acc, todo, kt_ref):
+def grads_kernel(len_ref, q_ref, do_ref, k_ref, v_ref, stat, qp_ref, kp_ref, dqt, dk_acc, dv_acc, todo, kt_ref):
     z = lax.axis_index("seq") // XN
     docs = Docs(len_ref)
-    for qs, values in enumerate(combine_stats(docs, z, mine, up1, up2, down1, down2)):
-        for r, value in enumerate(values):
-            stat[2 * qs : 2 * qs + 2, r : r + 1, :] = value
     for i in range(8):
         kt_ref[i] = k_ref[i * TILE : (i + 1) * TILE, :].T
     dqt[...] = jnp.zeros_like(dqt)
@@ -334,14 +356,30 @@
 TYPES = (("q", 0), ("k", 1), ("q", 1), ("k", 0))
 
 
-def gather_kernel(len_ref, raw, q_out, do_out, k_out, v_out, near,
-                  packed, own, q1, k1, qsel, ksel, q2, k2,
-                  x_send, x_recv, z_send, z_recv):
+def gather_kernel(len_ref, raw, q_out, do_out, k_out, v_out, stat,
+                  packed, own, q1, k1, qsel, ksel, q2, k2, mine, up1, up2, down1, down2,
+                  x_send, x_recv, z_send, z_recv, s_send, s_recv):
     z, x, up, down, peer = place()
     low, top = z > 0, z < ZN - 1
+    below, above = z > 1, z < ZN - 2
+    upper = lax.rem(z + 2, ZN) * XN + x
+    lower = lax.rem(z + ZN - 2, ZN) * XN + x
     meet(peer[1:])
-    pl.when(low)(lambda: meet([down]))
-    pl.when(top)(lambda: meet([up]))
+    expected = jnp.int32(3)
+    for use, to in ((low, down), (top, up), (below, lower), (above, upper)):
+        pl.when(use)(functools.partial(meet, [to]))
+        expected = expected + jnp.where(use, 1, 0)
+
+    @pl.when(jnp.logical_not(top))
+    def _():
+        q1[...] = jnp.zeros_like(q1)
+        q2[...] = jnp.zeros_like(q2)
+
+    @pl.when(jnp.logical_not(low))
+    def _():
+        k1[...] = jnp.zeros_like(k1)
+        k2[...] = jnp.zeros_like(k2)
+
     docs = Docs(len_ref)
     lk, lq = docs.case(z * 512)
     rk, rq = docs.case(z * 512 + 512)
@@ -401,7 +439,7 @@
     for xp in range(XN):
         pack(0, xp)
     own[0, x] = packed[0, x]
-    pl.semaphore_wait(pltpu.get_barrier_semaphore(), 3 + jnp.where(low, 1, 0) + jnp.where(top, 1, 0))
+    pl.semaphore_wait(pltpu.get_barrier_semaphore(), expected)
     for d in (1, 3):
         x_copy(0, d).start()
     z_start(0, x)
@@ -450,44 +488,38 @@
         unpack(k1[c], 1, c, k_out, v_out)
         unpack_own(2, c)
         unpack_own(3, c)
-    @pl.when(jnp.logical_not(top))
-    def _():
-        q_out[512:1024, :] = jnp.zeros((512, HEAD), jnp.bfloat16)
-        do_out[512:1024, :] = jnp.zeros((512, HEAD), jnp.bfloat16)
-
-    @pl.when(jnp.logical_not(low))
-    def _():
-        k_out[512:1024, :] = jnp.zeros((512, HEAD), jnp.bfloat16)
-        v_out[512:1024, :] = jnp.zeros((512, HEAD), jnp.bfloat16)
-
-    near_stats(docs, z, q_out, do_out, k_out, v_out, near)
+    near_stats(docs, z, q_out, do_out, k_out, v_out, mine)
     for d in (0, 1, 3, 2):
         c = source(d)
         z_got(2, c)
         unpack(q2[c], 2, c, q_out, do_out)
         z_got(3, c)
         unpack(k2[c], 2, c, k_out, v_out)
+    late_stats(docs, z, q_out, do_out, k_out, v_out, mine)
+    shares = []
+    for i, (ref, tiles, to, sent, got) in enumerate((
+        (up1, (0, 8), down, low, top),
+        (down1, (2, 4), up, top, low),
+        (up2, (0, 2), lower, below, above),
+        (down2, (4, 2), upper, above, below),
+    )):
+        part = pl.ds(*tiles)
+        shares.append((copy_to(mine.at[part], ref.at[part], s_send.at[i], s_recv.at[i], to), sent, got))
+    for copy, sent, got in shares:
+        pl.when(sent)(copy.start)
+    for copy, sent, got in shares:
+        pl.when(got)(copy.wait_recv)
+    for qs, values in enumerate(combine_stats(docs, z, mine, up1, up2, down1, down2)):
+        for r, value in enumerate(values):
+            stat[2 * qs : 2 * qs + 2, r : r + 1, :] = value
+    for copy, sent, got in shares:
+        pl.when(sent)(copy.wait_send)
     for t in range(4):
         for d in (1, 2, 3):
             x_copy(t, d).wait_send()
     for t in range(4):
         for c in range(XN):
             pl.when((low, top)[t % 2])(z_copy(t, c).wait_send)
-
-
-def share_kernel(mine, up1, up2, down1, down2, send, recv):
-    z, x, up, down, _ = place()
-    upper = lax.rem(z + 2, ZN) * XN + x
-    lower = lax.rem(z + ZN - 2, ZN) * XN + x
-    greet([up, upper, down, lower])
-    copies = []
-    for i, (ref, tiles, to) in enumerate(((up1, (0, 8), down), (down1, (2, 4), up), (up2, (0, 2), lower), (down2, (4, 2), upper))):
-        part = pl.ds(*tiles)
-        copies.append(copy_to(mine.at[part], ref.at[part], send.at[i], recv.at[i], to))
-    for copy in copies:
-        copy.start()
-    for copy in copies:
-        copy.wait()
 
 
 def scatter_kernel(len_ref, q_ref, do_ref, k_ref, v_ref, stat, dqt, dk_acc, dv_acc, qp, kp, qhome, khome,
@@ -639,44 +671,27 @@
     block = out(2048, HEAD)
     stat = out(8, 4, TILE, dtype=jnp.float32)
     todo = pltpu.SMEM((4, 64), jnp.int32)
-    qs, dos, ks, vs, near = pl.pallas_call(
+    qs, dos, ks, vs, stats = pl.pallas_call(
         gather_kernel,
         out_shape=(block,) * 4 + (stat,),
         name="gather",
         in_specs=[SM, VM],
         out_specs=(VM,) * 5,
         scratch_shapes=[buf(4, *chunk), buf(4, *chunk)] + [buf(*chunk)] * 6
-        + [DMA((4, 3)), DMA((4, 3)), DMA((4, 4)), DMA((4, 4))],
+        + [buf(8, 4, TILE, dtype=jnp.float32)] * 5
+        + [DMA((4, 3)), DMA((4, 3)), DMA((4, 4)), DMA((4, 4)), DMA((4,)), DMA((4,))],
         compiler_params=remote(0),
     )(doc_lengths, jnp.concatenate([queries, out_grad, key_vectors, value_vectors]))
-    mine = pl.pallas_call(
-        stats_kernel,
-        name="stats",
-        out_shape=stat,
-        in_specs=[SM] + [VM] * 5,
-        out_specs=VM,
-        scratch_shapes=[todo],
-        compiler_params=BIG,
-    )(doc_lengths, qs, dos, ks, vs, near)
-    others = pl.pallas_call(
-        share_kernel,
-        name="share",
-        out_shape=(stat,) * 4,
-        in_specs=[VM],
-        out_specs=(VM,) * 4,
-        scratch_shapes=[DMA((4,)), DMA((4,))],
-        compiler_params=remote(1),
-    )(mine)
     acc = out(8, TILE, HEAD, dtype=jnp.float32)
     qp, kp, *partial = pl.pallas_call(
         grads_kernel,
         name="grads",
-        out_shape=(out(*small), out(*chunk), stat, out(8, HEAD, TILE, dtype=jnp.float32), acc, acc),
-        in_specs=[SM] + [VM] * 9,
-        out_specs=(VM,) * 6,
+        out_shape=(out(*small), out(*chunk), out(8, HEAD, TILE, dtype=jnp.float32), acc, acc),
+        in_specs=[SM] + [VM] * 5,
+        out_specs=(VM,) * 5,
         scratch_shapes=[todo, buf(8, HEAD, TILE)],
         compiler_params=BIG,
-    )(doc_lengths, qs, dos, ks, vs, mine, *others)
+    )(doc_lengths, qs, dos, ks, vs, stats)
     home = pl.pallas_call(
         scatter_kernel,
         name="scatter",
@@ -688,7 +703,7 @@
                         buf(2, *small), buf(2, *chunk),
                         DMA((4, 4)), DMA((4, 4)), DMA((4, 3)), DMA((4, 3))],
         compiler_params=remote(2),
-    )(doc_lengths, qs, dos, ks, vs, *partial, qp, kp)
+    )(doc_lengths, qs, dos, ks, vs, stats, *partial, qp, kp)
     full = out(rows, width)
     grads = pl.pallas_call(
         unpack_kernel,

time: 78.6 us -> 75.2 us (0.957)
  Pallas kernels: 75.7 us -> 72.7 us
    pallas_call x2 -> x0, Pallas kernels: 15.1 us -> none  [the longest x1 14.3 us: shards(): pl.pallas_call(share_kernel, name='share', out_shape=(stat,) * 4, in_spec...]
    pallas_call x1, Pallas kernels: 31.4 us -> 42.3 us  [shards(): pl.pallas_call(gather_kernel, out_shape=(block,) * 4 + (stat,), name='gat...]
    pallas_call x1, Pallas kernels: 26.1 us -> 27.4 us  [shards(): pl.pallas_call(scatter_kernel, name='scatter', out_shape=(out(2, *small),...]
where the time goes in v6:
time: 75.2 us; the launch traced here: 75 us
  Pallas kernels  72.7 us (97%)
  other arithmetic  1.67 us (2%)
    pallas_call x1, Pallas kernels, shards(): pl.pallas_call(gather_kernel, out_shape=(block,) * 4 + (stat,), name='gat...  42.3 us
    pallas_call x1, Pallas kernels, shards(): pl.pallas_call(scatter_kernel, name='scatter', out_shape=(out(2, *small),...  27.4 us
    pallas_call x1, Pallas kernels, shards(): pl.pallas_call(grads_kernel, name='grads', out_shape=(out(*small), out(*c...  1.7 us
    concatenate x1, other arithmetic, shards(): jnp.concatenate([queries, out_grad, key_vectors, value_vectors])  1.67 us

profile of v6, /device:TPU:56, one launch (start us, length us, event | category | flops | bytes accessed | tf_op | source)
XLA Modules:
  0.0 75.0 jit_solution(1846116924422387660)
XLA Ops:
  0.6 0.0 copy-start
  0.6 1.7 %pad_maximum_fusion.raw = bf16[4,128,1792]{2,1,0:T(8,128)(2,1)S(1)} fusion(bf16[1,128,1792]{2,1,0:T(8,128)(2,1)} %param.7, bf16[1,128,1792]{2,1,0:T(8,128)(2,1)} %param.6, bf16[1,128,1792]{2,1,0:T(8,128)(2,1)} %param.8, bf16[1,128,1792]{2,1,0:T(8,128)(2,1)} %param.5), kind=kLoop, calls=%fused_computation | loop fusion | flops 2752512 | bytes 3670016 | tf_op jit(solution)/shard_map/concatenate | solution.py:684
  2.3 0.0 copy-done
  2.3 42.3 %gather.1 = (bf16[2048,224]{1,0:T(8,128)(2,1)S(1)}, bf16[2048,224]{1,0:T(8,128)(2,1)S(1)}, bf16[2048,224]{1,0:T(8,128)(2,1)S(1)}, bf16[2048,224]{1,0:T(8,128)(2,1)S(1)}, f32[8,4,256]{2,1,0:T(4,128)S(1)}) custom-call(s32[8]{0:T(128)S(1)} %copy-done, bf16[4,128,1792]{2,1,0:T(8,128)(2,1)S(1)} %pad_maximum_fusion.raw), custom_call_target="tpu_custom_call" | custom-call | tf_op jit(solution)/shard_map/gather/pallas_call | solution.py:674
  44.6 1.7 %grads.1 = (bf16[4,32,896]{2,1,0:T(8,128)(2,1)S(1)}, bf16[4,64,896]{2,1,0:T(8,128)(2,1)S(1)}, f32[8,224,256]{2,1,0:T(8,128)S(1)}, f32[8,256,224]{2,1,0:T(8,128)S(1)}, f32[8,256,224]{2,1,0:T(8,128)S(1)}) custom-call(s32[8]{0:T(128)S(1)} %copy-done, bf16[2048,224]{1,0:T(8,128)(2,1)S(1)} %get-tuple-element.18.q_ref, ...), custom_call_target="tpu_custom_call" | custom-call | tf_op jit(solution)/shard_map/grads/pallas_call | solution.py:686
  46.3 27.4 %scatter.1 = (bf16[2,4,32,896]{3,2,1,0:T(8,128)(2,1)S(1)}, bf16[2,4,64,896]{3,2,1,0:T(8,128)(2,1)S(1)}) custom-call(s32[8]{0:T(128)S(1)} %copy-done, bf16[2048,224]{1,0:T(8,128)(2,1)S(1)} %get-tuple-element.18.q_ref, bf16[2048,224]{1,0:T(8,128)(2,1)S(1)} %get-tuple-element.19.do_ref, bf16[2048,224]{1,0:T(8,128)(2,1)S(1)} %get-tuple-element.20.k_ref, ...), custom_call_target="tpu_custom_call" | custom-call | tf_op jit(solution)/shard_map/scatter/pallas_call | solution.py:695
  73.8 1.3 %unpack.1 = (bf16[128,1792]{1,0:T(8,128)(2,1)}, bf16[128,1792]{1,0:T(8,128)(2,1)}, bf16[128,1792]{1,0:T(8,128)(2,1)}) custom-call(bf16[2,4,32,896]{3,2,1,0:T(8,128)(2,1)S(1)} %get-tuple-element.28.qhome, bf16[2,4,64,896]{3,2,1,0:T(8,128)(2,1)S(1)} %get-tuple-element.29.khome), custom_call_target="tpu_custom_call" | custom-call | tf_op jit(solution)/shard_map/unpack/pallas_call | solution.py:708
Async XLA Ops:
  0.6 1.7 %copy-start = (s32[8]{0:T(128)S(1)}, s32[8]{0:T(128)}, u32[]{:S(2)}) copy-start(s32[8]{0:T(128)} %len_ref.5) | copy-start | bytes 100

commit v7 on v6

--- a/solution.py
+++ b/solution.py
@@ -120,12 +120,14 @@
     return lax.dot_general(k, q, NT, preferred_element_type=jnp.float32)
 
 
-def masked(docs, s, q0, k0):
+def masked(docs, s, q0, k0, near=False):
     row = lax.broadcasted_iota(jnp.int32, (TILE, TILE), 0)
     qpos = q0 + lax.broadcasted_iota(jnp.int32, (1, TILE), 1)
     allowed = row >= docs.row_start(qpos) - k0
     if q0 is k0:
         allowed = allowed & (row <= lax.broadcasted_iota(jnp.int32, (1, TILE), 1))
+    elif near:
+        allowed = allowed & (row <= qpos - k0)
     return jnp.where(allowed, s * (SCALE * LOG2E), NEG)
 
 
@@ -156,8 +158,8 @@
     return tiles
 
 
-def part_stats(docs, q, do, q0, keys):
-    raw = [(masked(docs, raw_scores(k, q), q0, k0), raw_scores(v, do)) for k, v, k0 in keys]
+def part_stats(docs, q, do, q0, keys, near=False):
+    raw = [(masked(docs, raw_scores(k, q), q0, k0, near), raw_scores(v, do)) for k, v, k0 in keys]
     m = jnp.full((1, TILE), LOW, jnp.float32)
     for s, dp in raw:
         m = jnp.maximum(m, jnp.max(s, axis=0, keepdims=True))
@@ -182,13 +184,22 @@
     put_stats(st_ref, qi, (m, old[1] * a + part[1] * b, old[2] * a + part[2] * b))
 
 
-def near_stats(docs, z, q_ref, do_ref, k_ref, v_ref, st_ref):
-    for qi, q0, keys in near_tiles(docs, z):
-        tiles = [(tile_rows(k_ref, ki), tile_rows(v_ref, ki), k0) for ki, k0 in keys]
-        put_stats(st_ref, qi, part_stats(docs, tile_rows(q_ref, qi), tile_rows(do_ref, qi), q0, tiles))
-
-
-def late_stats(docs, z, q_ref, do_ref, k_ref, v_ref, st_ref):
+def near_half(docs, z, h, q_ref, do_ref, k_ref, v_ref, st_ref):
+    _, lq = docs.case(z * 512)
+    rk, _ = docs.case(z * 512 + 512)
+    here = z * 512
+    fore = jnp.where(jnp.logical_not(rk) & (z < ZN - 1), here, FAR)
+    back = jnp.where(jnp.logical_not(lq) & (z > 0), here - 512, FAR)
+    k, v = tile_rows(k_ref, 6 + h), tile_rows(v_ref, 6 + h)
+    for i in range(4):
+        first = (here, fore)[i // 2] + h * TILE
+        part = part_stats(docs, tile_rows(q_ref, i), tile_rows(do_ref, i), here + i * TILE, [(k, v, first)], i < 2)
+        add_stats(st_ref, i, part, True)
+    keys = [(tile_rows(k_ref, j), tile_rows(v_ref, j), (here, back)[j // 2] + j % 2 * TILE) for j in range(4)]
+    put_stats(st_ref, 6 + h, part_stats(docs, tile_rows(q_ref, 6 + h), tile_rows(do_ref, 6 + h), here + h * TILE, keys, True))
+
+
+def late_half(docs, z, h, other, q_ref, do_ref, k_ref, v_ref, st_ref):
     lk, lq = docs.case(z * 512)
     rk, rq = docs.case(z * 512 + 512)
     lm, rm = jnp.logical_not(lk | lq), jnp.logical_not(rk | rq)
@@ -205,22 +216,26 @@
     own = jnp.logical_not(rk) & q_ok
     both = ((lk & rm) | (rq & lm)) & q_ok & k_ok
     cross = (lk & jnp.logical_not(rk) & (z < ZN - 1) & k_ok) | (rq & jnp.logical_not(lq) & (z > 0) & q_ok)
+    halves = [h] if other is None else [h, other]
+    keys = [(pick(k_ref, rq, j, 6 + j), pick(v_ref, rq, j, 6 + j), start(own, here, j)) for j in range(2)]
+    keys += [(tile_rows(k_ref, 4 + j), tile_rows(v_ref, 4 + j), start(both, k2, j)) for j in halves]
+    put_stats(st_ref, 4 + h, part_stats(docs, tile_rows(q_ref, 4 + h), tile_rows(do_ref, 4 + h), q2 + h * TILE, keys))
+    if other is not None:
+        keys = [(tile_rows(k_ref, 4 + h), tile_rows(v_ref, 4 + h), start(both, k2, h))]
+        part = part_stats(docs, tile_rows(q_ref, 4 + other), tile_rows(do_ref, 4 + other), q2 + other * TILE, keys)
+        add_stats(st_ref, 4 + other, part, True)
+    second = (tile_rows(k_ref, 4 + h), tile_rows(v_ref, 4 + h), start(jnp.logical_not(lq) & k_ok, k2, h))
     for i in range(2):
-        keys = [(pick(k_ref, rq, j, 6 + j), pick(v_ref, rq, j, 6 + j), start(own, here, j)) for j in range(2)]
-        keys += [(tile_rows(k_ref, 4 + j), tile_rows(v_ref, 4 + j), start(both, k2, j)) for j in range(2)]
-        put_stats(st_ref, 4 + i, part_stats(docs, tile_rows(q_ref, 4 + i), tile_rows(do_ref, 4 + i), q2 + i * TILE, keys))
-    for i in range(2):
-        keys = [(tile_rows(k_ref, 4 + j), tile_rows(v_ref, 4 + j), start(jnp.logical_not(lq) & k_ok, k2, j)) for j in range(2)]
-        part = part_stats(docs, pick(q_ref, lk, i, 6 + i), pick(do_ref, lk, i, 6 + i), here + i * TILE, keys)
+        part = part_stats(docs, pick(q_ref, lk, i, 6 + i), pick(do_ref, lk, i, 6 + i), here + i * TILE, [second])
         add_stats(st_ref, i, part, lk)
         add_stats(st_ref, 6 + i, part, lm)
     for i in range(2):
-        keys = [(pick(k_ref, lk, 4 + j, 2 + j), pick(v_ref, lk, 4 + j, 2 + j), start(cross, jnp.where(lk, k2, here - 512), j))
-                for j in range(2)]
-        part = part_stats(docs, pick(q_ref, lk, 2 + i, 4 + i), pick(do_ref, lk, 2 + i, 4 + i),
-                          jnp.where(lk, here + 512, q2) + i * TILE, keys)
+        key = (pick(k_ref, lk, 4 + h, 2 + i), pick(v_ref, lk, 4 + h, 2 + i),
+               jnp.where(lk, start(cross, k2, h), start(cross, here - 512, i)))
+        part = part_stats(docs, pick(q_ref, lk, 2 + i, 4 + h), pick(do_ref, lk, 2 + i, 4 + h),
+                          jnp.where(lk, here + 512 + i * TILE, q2 + h * TILE), [key])
         add_stats(st_ref, 2 + i, part, lk)
-        add_stats(st_ref, 4 + i, part, jnp.logical_not(lk))
+        add_stats(st_ref, 4 + h, part, jnp.logical_not(lk))
 
 
 def combine_stats(docs, z, mine, up1, up2, down1, down2):
@@ -419,7 +434,7 @@
 
     def got_x(t, d):
         back = XN - d
-        copy_to(packed.at[t, x], own.at[t, source(d)], x_send.at[t, back - 1], x_recv.at[t, back - 1], peer[d]).wait_recv()
+        copy_to(packed.at[t, x], own.at[t, source(d)], x_send.at[t, back - 1], x_recv.at[t, back - 1], peer[1]).wait_recv()
 
     def second(i, c):
         z_got(i - 2, c)
@@ -473,29 +488,58 @@
         unpack_own(t, source(3))
     first(0, 2)
     first(1, 2)
-    x_copy(2, 2).start()
-    x_copy(3, 2).start()
     unpack(q1[x], 1, x, q_out, do_out)
     unpack(k1[x], 1, x, k_out, v_out)
     for t in (0, 1):
         unpack_own(t, source(2))
-    for d in (1, 3, 2):
-        c = source(d)
-        for t in (2, 3):
-            got_x(t, d)
-            second(t, c)
+    def pass_on(i, c):
+        if i == 2:
+            qsel[c] = jnp.where(lq, own[2, c], q1[c])
+        else:
+            ksel[c] = jnp.where(rk, own[3, c], k1[c])
+        z_start(i, c)
+
+    def unpack_first(c):
         unpack(q1[c], 1, c, q_out, do_out)
         unpack(k1[c], 1, c, k_out, v_out)
-        unpack_own(2, c)
-        unpack_own(3, c)
-    near_stats(docs, z, q_out, do_out, k_out, v_out, mine)
-    for d in (0, 1, 3, 2):
-        c = source(d)
+
+    def unpack_second(c):
         z_got(2, c)
         unpack(q2[c], 2, c, q_out, do_out)
         z_got(3, c)
         unpack(k2[c], 2, c, k_out, v_out)
-    late_stats(docs, z, q_out, do_out, k_out, v_out, mine)
+
+    for i in (0, 1, 2, 3):
+        put_stats(mine, i, (jnp.full((1, TILE), LOW, jnp.float32),) + (jnp.zeros((1, TILE), jnp.float32),) * 2)
+    arrays = (q_out, do_out, k_out, v_out, mine)
+    half = x // 2
+    step = 1 + 2 * lax.rem(x, 2)
+    steps = (step, XN - step, 2)
+    mate = source(step)
+    for t in (2, 3):
+        got_x(t, step)
+        z_got(t - 2, mate)
+        pass_on(t, mate)
+        x_copy(t, 2).start()
+        unpack_own(t, mate)
+    unpack_first(mate)
+    for d in steps[1:]:
+        z_got(0, source(d))
+        z_got(1, source(d))
+        unpack_first(source(d))
+    near_half(docs, z, half, *arrays)
+    for d in steps[1:]:
+        for t in (2, 3):
+            got_x(t, d)
+            pass_on(t, source(d))
+            unpack_own(t, source(d))
+    near_half(docs, z, 1 - half, *arrays)
+    unpack_second(x)
+    unpack_second(mate)
+    late_half(docs, z, half, None, *arrays)
+    for d in steps[1:]:
+        unpack_second(source(d))
+    late_half(docs, z, 1 - half, half, *arrays)
     shares = []
     for i, (ref, tiles, to, sent, got) in enumerate((
         (up1, (0, 8), down, low, top),

time: 75.2 us -> 74.3 us (0.988)
  Pallas kernels: 72.7 us -> 71.1 us
    pallas_call x1, Pallas kernels: 27.4 us -> 26.4 us  [shards(): pl.pallas_call(scatter_kernel, name='scatter', out_shape=(out(2, *small),...]
where the time goes in v7:
time: 74.3 us; the launch traced here: 73.5 us
  Pallas kernels  71.1 us (96%)
  other arithmetic  1.67 us (2%)
    pallas_call x1, Pallas kernels, shards(): pl.pallas_call(gather_kernel, out_shape=(block,) * 4 + (stat,), name='gat...  41.7 us
    pallas_call x1, Pallas kernels, shards(): pl.pallas_call(scatter_kernel, name='scatter', out_shape=(out(2, *small),...  26.4 us
    pallas_call x1, Pallas kernels, shards(): pl.pallas_call(grads_kernel, name='grads', out_shape=(out(*small), out(*c...  1.7 us
    concatenate x1, other arithmetic, shards(): jnp.concatenate([queries, out_grad, key_vectors, value_vectors])  1.67 us

profile of v7, /device:TPU:56, one launch (start us, length us, event | category | flops | bytes accessed | tf_op | source)
XLA Modules:
  0.0 73.5 jit_solution(18316018912614781554)
XLA Ops:
  0.6 0.0 copy-start
  0.6 1.7 %pad_maximum_fusion.raw = bf16[4,128,1792]{2,1,0:T(8,128)(2,1)S(1)} fusion(bf16[1,128,1792]{2,1,0:T(8,128)(2,1)} %param.7, bf16[1,128,1792]{2,1,0:T(8,128)(2,1)} %param.6, bf16[1,128,1792]{2,1,0:T(8,128)(2,1)} %param.8, bf16[1,128,1792]{2,1,0:T(8,128)(2,1)} %param.5), kind=kLoop, calls=%fused_computation | loop fusion | flops 2752512 | bytes 3670016 | tf_op jit(solution)/shard_map/concatenate | solution.py:728
  2.3 0.0 copy-done
  2.3 41.7 %gather.1 = (bf16[2048,224]{1,0:T(8,128)(2,1)S(1)}, bf16[2048,224]{1,0:T(8,128)(2,1)S(1)}, bf16[2048,224]{1,0:T(8,128)(2,1)S(1)}, bf16[2048,224]{1,0:T(8,128)(2,1)S(1)}, f32[8,4,256]{2,1,0:T(4,128)S(1)}) custom-call(s32[8]{0:T(128)S(1)} %copy-done, bf16[4,128,1792]{2,1,0:T(8,128)(2,1)S(1)} %pad_maximum_fusion.raw), custom_call_target="tpu_custom_call" | custom-call | tf_op jit(solution)/shard_map/gather/pallas_call | solution.py:718
  44.1 1.7 %grads.1 = (bf16[4,32,896]{2,1,0:T(8,128)(2,1)S(1)}, bf16[4,64,896]{2,1,0:T(8,128)(2,1)S(1)}, f32[8,224,256]{2,1,0:T(8,128)S(1)}, f32[8,256,224]{2,1,0:T(8,128)S(1)}, f32[8,256,224]{2,1,0:T(8,128)S(1)}) custom-call(s32[8]{0:T(128)S(1)} %copy-done, bf16[2048,224]{1,0:T(8,128)(2,1)S(1)} %get-tuple-element.18.q_ref, ...), custom_call_target="tpu_custom_call" | custom-call | tf_op jit(solution)/shard_map/grads/pallas_call | solution.py:730
  45.8 26.4 %scatter.1 = (bf16[2,4,32,896]{3,2,1,0:T(8,128)(2,1)S(1)}, bf16[2,4,64,896]{3,2,1,0:T(8,128)(2,1)S(1)}) custom-call(s32[8]{0:T(128)S(1)} %copy-done, bf16[2048,224]{1,0:T(8,128)(2,1)S(1)} %get-tuple-element.18.q_ref, bf16[2048,224]{1,0:T(8,128)(2,1)S(1)} %get-tuple-element.19.do_ref, bf16[2048,224]{1,0:T(8,128)(2,1)S(1)} %get-tuple-element.20.k_ref, ...), custom_call_target="tpu_custom_call" | custom-call | tf_op jit(solution)/shard_map/scatter/pallas_call | solution.py:739
  72.2 1.3 %unpack.1 = (bf16[128,1792]{1,0:T(8,128)(2,1)}, bf16[128,1792]{1,0:T(8,128)(2,1)}, bf16[128,1792]{1,0:T(8,128)(2,1)}) custom-call(bf16[2,4,32,896]{3,2,1,0:T(8,128)(2,1)S(1)} %get-tuple-element.28.qhome, bf16[2,4,64,896]{3,2,1,0:T(8,128)(2,1)S(1)} %get-tuple-element.29.khome), custom_call_target="tpu_custom_call" | custom-call | tf_op jit(solution)/shard_map/unpack/pallas_call | solution.py:752
Async XLA Ops:
  0.6 1.7 %copy-start = (s32[8]{0:T(128)S(1)}, s32[8]{0:T(128)}, u32[]{:S(2)}) copy-start(s32[8]{0:T(128)} %len_ref.5) | copy-start | bytes 100

commit v8 on v7

--- a/solution.py
+++ b/solution.py
@@ -675,8 +675,9 @@
             x_copy(i // 2, i % 2, d).wait_send()
 
 
-def unpack_kernel(qhome, khome, dq_out, dk_out, dv_out):
-    for a, out, n in ((0, dq_out, 4), (0, dk_out, 2), (1, dv_out, 2)):
+def unpack_kernel(qhome, khome, dq_out, dk_out, dv_out, stage, sem):
+    copies = []
+    for i, (a, out, n) in enumerate(((0, dq_out, 4), (0, dk_out, 2), (1, dv_out, 2))):
         home = qhome if n == 4 else khome
         step = 128 // n
         for part in range(n):
@@ -685,7 +686,11 @@
             for xs in range(XN):
                 for head in range(2):
                     pieces.append(home[head, xs][:, lanes : lanes + HEAD])
-            out[part * step : (part + 1) * step, :] = jnp.concatenate(pieces, axis=1)
+            stage[i, part * step : (part + 1) * step, :] = jnp.concatenate(pieces, axis=1)
+        copies.append(pltpu.make_async_copy(stage.at[i], out, sem.at[i]))
+        copies[-1].start()
+    for copy in copies:
+        copy.wait()
 
 
 VM = pl.BlockSpec(memory_space=pltpu.VMEM)
@@ -754,7 +759,8 @@
         name="unpack",
         out_shape=(full,) * 3,
         in_specs=[VM, VM],
-        out_specs=(VM,) * 3,
+        out_specs=(HB,) * 3,
+        scratch_shapes=[buf(3, rows, width), DMA((3,))],
         compiler_params=BIG,
     )(*home)
     return tuple(g[None] for g in grads)

time: 74.3 us -> 73.7 us (level); the launches traced: 73.5 us -> 73.6 us
    pallas_call x1, Pallas kernels: 1.7 us -> 2.64 us  [shards(): pl.pallas_call(grads_kernel, name='grads', out_shape=(out(*small), out(*c...]
    pallas_call x1, Pallas kernels: 26.4 us -> 25.5 us  [shards(): pl.pallas_call(scatter_kernel, name='scatter', out_shape=(out(2, *small),...]
where the time goes in v8:
time: 73.7 us; the launch traced here: 73.6 us
  Pallas kernels  71.1 us (96%)
  other arithmetic  1.67 us (2%)
  between operations  0.83 us (1%)
    pallas_call x1, Pallas kernels, shards(): pl.pallas_call(gather_kernel, out_shape=(block,) * 4 + (stat,), name='gat...  41.7 us
    pallas_call x1, Pallas kernels, shards(): pl.pallas_call(scatter_kernel, name='scatter', out_shape=(out(2, *small),...  25.5 us
    pallas_call x1, Pallas kernels, shards(): pl.pallas_call(grads_kernel, name='grads', out_shape=(out(*small), out(*c...  2.64 us
    concatenate x1, other arithmetic, shards(): jnp.concatenate([queries, out_grad, key_vectors, value_vectors])  1.67 us

profile of v8, /device:TPU:56, one launch (start us, length us, event | category | flops | bytes accessed | tf_op | source)
XLA Modules:
  0.0 73.6 jit_solution(11788186117633800862)
XLA Ops:
  0.6 0.0 copy-start
  0.6 1.7 %pad_maximum_fusion.raw = bf16[4,128,1792]{2,1,0:T(8,128)(2,1)S(1)} fusion(bf16[1,128,1792]{2,1,0:T(8,128)(2,1)} %param.7, bf16[1,128,1792]{2,1,0:T(8,128)(2,1)} %param.6, bf16[1,128,1792]{2,1,0:T(8,128)(2,1)} %param.8, bf16[1,128,1792]{2,1,0:T(8,128)(2,1)} %param.5), kind=kLoop, calls=%fused_computation | loop fusion | flops 2752512 | bytes 3670016 | tf_op jit(solution)/shard_map/concatenate | solution.py:733
  2.3 0.0 copy-done
  2.3 41.7 %gather.1 = (bf16[2048,224]{1,0:T(8,128)(2,1)S(1)}, bf16[2048,224]{1,0:T(8,128)(2,1)S(1)}, bf16[2048,224]{1,0:T(8,128)(2,1)S(1)}, bf16[2048,224]{1,0:T(8,128)(2,1)S(1)}, f32[8,4,256]{2,1,0:T(4,128)S(1)}) custom-call(s32[8]{0:T(128)S(1)} %copy-done, bf16[4,128,1792]{2,1,0:T(8,128)(2,1)S(1)} %pad_maximum_fusion.raw), custom_call_target="tpu_custom_call" | custom-call | tf_op jit(solution)/shard_map/gather/pallas_call | solution.py:723
  44.1 2.6 %grads.1 = (bf16[4,32,896]{2,1,0:T(8,128)(2,1)S(1)}, bf16[4,64,896]{2,1,0:T(8,128)(2,1)S(1)}, f32[8,224,256]{2,1,0:T(8,128)S(1)}, f32[8,256,224]{2,1,0:T(8,128)S(1)}, f32[8,256,224]{2,1,0:T(8,128)S(1)}) custom-call(s32[8]{0:T(128)S(1)} %copy-done, bf16[2048,224]{1,0:T(8,128)(2,1)S(1)} %get-tuple-element.18.q_ref, ...), custom_call_target="tpu_custom_call" | custom-call | tf_op jit(solution)/shard_map/grads/pallas_call | solution.py:735
  46.7 25.5 %scatter.1 = (bf16[2,4,32,896]{3,2,1,0:T(8,128)(2,1)S(1)}, bf16[2,4,64,896]{3,2,1,0:T(8,128)(2,1)S(1)}) custom-call(s32[8]{0:T(128)S(1)} %copy-done, bf16[2048,224]{1,0:T(8,128)(2,1)S(1)} %get-tuple-element.18.q_ref, bf16[2048,224]{1,0:T(8,128)(2,1)S(1)} %get-tuple-element.19.do_ref, bf16[2048,224]{1,0:T(8,128)(2,1)S(1)} %get-tuple-element.20.k_ref, ...), custom_call_target="tpu_custom_call" | custom-call | tf_op jit(solution)/shard_map/scatter/pallas_call | solution.py:744
  72.2 1.3 %unpack.1 = (bf16[128,1792]{1,0:T(8,128)(2,1)}, bf16[128,1792]{1,0:T(8,128)(2,1)}, bf16[128,1792]{1,0:T(8,128)(2,1)}) custom-call(bf16[2,4,32,896]{3,2,1,0:T(8,128)(2,1)S(1)} %get-tuple-element.28.qhome, bf16[2,4,64,896]{3,2,1,0:T(8,128)(2,1)S(1)} %get-tuple-element.29.khome), custom_call_target="tpu_custom_call" | custom-call | tf_op jit(solution)/shard_map/unpack/pallas_call | solution.py:757
Async XLA Ops:
  0.6 1.7 %copy-start = (s32[8]{0:T(128)S(1)}, s32[8]{0:T(128)}, u32[]{:S(2)}) copy-start(s32[8]{0:T(128)} %len_ref.5) | copy-start | bytes 100
